TPU v7x, 32 devices: a whole 2x2x4 slice. The times are simulated.
32 devices in a mesh: dp: 4 (over y, core), space: 8 (over z, x).
Axes of the slice: x: 2, y: 2, z: 4, core: 2. Of those that a mesh axis runs over, the one named last changes fastest.
Arguments:
- inputs: bfloat16 [12, 8, 4, 8192], P('dp', 'space'), may hold values from -6 to 6
- mask_one: int32 [12, 8, 16, 8192], P('dp', 'space'), may hold values 0 or 1
- place_one: int32 [12, 8, 16, 1024], P('dp', 'space'), may hold values from 0 to 7
- pooled_one: bfloat16 [12, 8, 16, 1024], P('dp', 'space'), may hold values from 0 to 2
- w_two: bfloat16 [27, 16, 32], replicated, may hold values from -0.21875 to 0.21875
- mask_two: int32 [12, 8, 32, 1024], P('dp', 'space'), may hold values 0 or 1
- place_two: int32 [12, 8, 32, 128], P('dp', 'space'), may hold values from 0 to 7
- grad_two: bfloat16 [12, 8, 32, 128], P('dp', 'space'), may hold values from -24 to 24
Outputs:
- grad_pooled: bfloat16 [12, 8, 16, 1024], P('dp', 'space')
- grad_w_one: float32 [27, 4, 16], replicated
- grad_w_two: float32 [27, 16, 32], replicated
All inputs are finite; a program needn't handle non-finite values. No bound on the sum of `mask_one` or of `mask_two` on one device may be relied on, other than what follows from the above.
Results may differ from a plain program's by a relative error of at most 0.0029.
Values may be sent and summed in bfloat16 or wider, within the bound.
No kernel may reach another device: no remote copies, remote signals or barrier semaphores. Data moves between devices by JAX's collectives and lax.ppermute only.
A program may use at most 128 MiB of HBM per device.

v0:
```python
import functools

import jax
import jax.numpy as jnp
from jax import lax
from jax.experimental import pallas as pl
from jax.experimental.pallas import tpu as pltpu
from jax.sharding import PartitionSpec as P

C_IN = 4
C_ONE = 16
C_TWO = 32
BX = 4
BY = 8
BZ = 256
HX, HY, HZ = BX // 2, BY // 2, BZ // 2
QY, QZ = HY // 2, HZ // 2
LANES = 128
PACK = 16
OFFS = (-1, 0, 1)
GRAD_W_TWO = 27 * C_TWO
WIDTH = 1024
ONE_AT = WIDTH - LANES
NT = (((1,), (1,)), ((), ()))
f32, bf16, i32 = jnp.float32, jnp.bfloat16, jnp.int32


def iota(shape, dim):
    return lax.broadcasted_iota(i32, shape, dim)


def doubling():
    return (iota((LANES, 2 * LANES), 0) == iota((LANES, 2 * LANES), 1) // 2).astype(bf16)


def prepare(samples, grad, place, mask, source, vp, edge, own, faces_x, ends_y, mids_y):
    rows = samples * C_TWO
    table = doubling()
    values = jnp.dot(grad[...].reshape(rows, LANES), table, preferred_element_type=f32)
    spots = place[...].reshape(rows, LANES).astype(f32).astype(bf16)
    wide = jnp.dot(spots, table, preferred_element_type=f32)
    parity = (iota((rows, LANES), 1) % 2).astype(f32)
    halves = []
    for qy in range(QY):
        v = values[:, qy * LANES : (qy + 1) * LANES]
        p = wide[:, qy * LANES : (qy + 1) * LANES] - parity
        total = jnp.zeros((rows, LANES), f32)
        for x in range(HX):
            for dy in range(2):
                at = (x * HY + 2 * qy + dy) * LANES
                on = mask[:, 0, :, at : at + LANES].reshape(rows, LANES) == 1
                total = total + jnp.where(on & (p == 4.0 * x + 2.0 * dy), v, 0.0)
        halves.append(total)
    kept = jnp.concatenate(halves, axis=1).astype(bf16)
    v = lax.dot_general(kept, table, NT, preferred_element_type=f32).astype(bf16)
    vp[0:rows] = v
    vp[rows : 2 * rows] = spots
    lane = iota((LANES, LANES), 0)
    spot = (lane // QZ) * 2 + (lane % QZ == QZ - 1).astype(i32)
    spot = jnp.where((lane % QZ == 0) | (lane % QZ == QZ - 1), spot, -LANES)
    column = iota((LANES, LANES), 1)
    packed = jnp.zeros((C_TWO, LANES), f32)
    for s in range(samples):
        for t, field in enumerate((v, spots)):
            pick = (spot + (8 * s + 4 * t) == column).astype(bf16)
            packed = packed + jnp.dot(
                field[s * C_TWO : (s + 1) * C_TWO], pick, preferred_element_type=f32
            )
    edge[0:C_TWO] = packed.astype(bf16)
    pieces = [source[s, 0].astype(f32) for s in range(samples)]
    pieces.append(jnp.zeros((PACK - samples * C_IN, BX * BY * BZ), f32))
    cells = jnp.concatenate(pieces, axis=0)
    packed_cells = cells.astype(bf16)
    own[...] = packed_cells
    plane = BY * BZ
    faces_x[:, 0:plane] = packed_cells[:, 0:plane]
    faces_x[:, plane : 2 * plane] = packed_cells[:, (BX - 1) * plane :]
    for ref, pair in ((ends_y, (0, BX - 1)), (mids_y, (1, BX - 2))):
        for i, x in enumerate(pair):
            for j, y in enumerate((0, BY - 1)):
                at = (x * BY + y) * BZ
                ref[:, (2 * i + j) * BZ : (2 * i + j + 1) * BZ] = packed_cells[:, at : at + BZ]
    lane = iota((PACK, LANES), 1)
    ends = jnp.zeros((PACK, LANES), f32)
    for row in range(BX * BY):
        for last in range(2):
            at = row * BZ + last * (BZ - 1)
            ends = jnp.where(lane == 2 * row + last, cells[:, at : at + 1], ends)
    edge[C_TWO : C_TWO + PACK] = ends.astype(bf16)


def select_one(samples, place, mask, weights, chosen, flat_weights):
    rows = samples * C_ONE
    table = doubling()
    parity = (iota((rows, BZ), 1) % 2).astype(f32)
    for x in range(HX):
        for y in range(HY):
            at = (x * HY + y) * LANES
            spots = place[:, 0, :, at : at + LANES].reshape(rows, LANES).astype(f32).astype(bf16)
            wide = jnp.dot(spots, table, preferred_element_type=f32) - parity
            for dx in range(2):
                for dy in range(2):
                    to = ((2 * x + dx) * BY + 2 * y + dy) * BZ
                    on = mask[:, 0, :, to : to + BZ].reshape(rows, BZ) == 1
                    hit = on & (wide == 4.0 * dx + 2.0 * dy)
                    chosen[:, to : to + BZ] = jnp.where(hit, 1.0, 0.0).astype(bf16)
    flat_weights[...] = jnp.concatenate([weights[o] for o in range(27)], axis=1)


def main(samples, scale_one, scale_two, where, n_vp, n_edge, n_x, n_y, *refs):
    vps, refs = refs[:n_vp], refs[n_vp:]
    edges, refs = refs[:n_edge], refs[n_edge:]
    xs, refs = refs[:n_x], refs[n_x:]
    ys, refs = refs[:n_y], refs[n_y:]
    own, pooled, chosen, weights, out, sums, fields, conv_one, ahead = refs
    rows = samples * C_TWO
    lane_z = iota((C_TWO, LANES), 1)
    width = 3 * QY * LANES
    k = iota((2 * LANES, width), 0)
    j = iota((2 * LANES, width), 1)
    shift = j // (QY * LANES) - 1
    qy = (j // LANES) % QY
    z = j % LANES - shift
    inside = (z >= 0) & (z < LANES)
    window = qy * QZ + z // 2
    beyond = LANES + qy * 2 + (z < 0).astype(i32)
    tables = []
    for s in range(samples):
        tables.append(
            [
                (k == jnp.where(inside, window, beyond + (8 * s + 4 * t))).astype(bf16)
                for t in range(2)
            ]
        )
    parity = [((lane_z - oz) & 1).astype(f32) for oz in OFFS]
    first = iota((C_TWO, LANES), 1) < 0
    for a, nx in enumerate(OFFS):
        for b, ny in enumerate(OFFS):
            vp = vps[where["vp"][nx, ny]]
            low, high = (edges[where["edge"][nx, ny, nz]] for nz in (-1, 1))
            if low is high:
                edge = low[0:C_TWO]
            else:
                edge = jnp.where(lane_z % 2 == 1, low[0:C_TWO].astype(f32), high[0:C_TWO].astype(f32)).astype(bf16)
            for s in range(samples):
                at = s * C_TWO
                v = jnp.concatenate([vp[at : at + C_TWO], edge], axis=1)
                p = jnp.concatenate([vp[rows + at : rows + at + C_TWO], edge], axis=1)
                v = jnp.dot(v, tables[s][0], preferred_element_type=f32)
                p = jnp.dot(p, tables[s][1], preferred_element_type=f32)
                for x in {-1: (HX - 1,), 0: range(HX), 1: (0,)}[nx]:
                    for y in {-1: (HY - 1,), 0: range(HY), 1: (0,)}[ny]:
                        px, py = x + 1 + nx * HX, y + 1 + ny * HY
                        to = (px * (HY + 2) + py) * LANES
                        for i in range(3):
                            at_z = (i * QY + y // 2) * LANES
                            hit = p[:, at_z : at_z + LANES] - parity[i] == 4.0 * (x % 2) + 2.0 * (y % 2)
                            fields[s, i * C_TWO : (i + 1) * C_TWO, to : to + LANES] = jnp.where(
                                hit, v[:, at_z : at_z + LANES], 0.0
                            ).astype(bf16)
    line = HY * HZ
    grad_two = jnp.zeros((C_ONE, GRAD_W_TWO), f32)
    results = []
    for s in range(samples):
        parts = []
        for x in range(HX):
            behind = []
            for ox in OFFS:
                for oy in OFFS:
                    at = ((x + 1 - ox) * (HY + 2) + 1 - oy) * LANES
                    behind.append(fields[s, :, at : at + line])
            behind = jnp.concatenate(behind, axis=0)
            got = jnp.dot(weights[...], behind, preferred_element_type=f32).astype(bf16)
            out[s, 0, :, x * line : (x + 1) * line] = got
            parts.append(got)
            grad_two = grad_two + lax.dot_general(
                pooled[s, 0, :, x * line : (x + 1) * line], behind, NT, preferred_element_type=f32
            )
        results.append(jnp.concatenate(parts, axis=1))
    sums[:, 0:GRAD_W_TWO] = grad_two * scale_two
    sums[:, GRAD_W_TWO:ONE_AT] = jnp.zeros((C_ONE, ONE_AT - GRAD_W_TWO), f32)
    grad_pooled = jnp.concatenate(results, axis=0)
    table = doubling()
    for x in range(HX):
        for y in range(HY):
            at = (x * HY + y) * LANES
            wide = jnp.dot(grad_pooled[:, at : at + LANES], table, preferred_element_type=f32).astype(bf16)
            for dx in range(2):
                for dy in range(2):
                    to = ((2 * x + dx) * BY + 2 * y + dy) * BZ
                    conv_one[:, to : to + BZ] = wide * chosen[:, to : to + BZ]
    lane = iota((PACK, BZ), 1)
    plane = BY * BZ
    for px in range(BX + 2):
        nx = -1 if px == 0 else 1 if px == BX + 1 else 0
        x = (px - 1) % BX
        for py in range(BY + 2):
            ny = -1 if py == 0 else 1 if py == BY + 1 else 0
            y = (py - 1) % BY
            far_y = 0 if y == 0 else 1
            if ny == 0 and nx == 0:
                row = own[:, (x * BY + y) * BZ : (x * BY + y + 1) * BZ]
            elif ny == 0:
                at = (0 if x == 0 else 1) * plane + y * BZ
                row = xs[where["x"][nx]][:, at : at + BZ]
            else:
                at = ((2 if x >= 2 else 0) + far_y) * BZ
                row = ys[where["y"][nx, ny, x in (0, BX - 1)]][:, at : at + BZ]
            row = row.astype(f32)
            below = edges[where["edge"][nx, ny, -1]][C_TWO : C_TWO + PACK].astype(f32)
            above = edges[where["edge"][nx, ny, 1]][C_TWO : C_TWO + PACK].astype(f32)
            at = 2 * (x * BY + y)
            to = (px * (BY + 2) + py) * BZ
            before = jnp.where(lane == 0, below[:, at + 1 : at + 2], pltpu.roll(row, 1, 1))
            after = jnp.where(lane == BZ - 1, above[:, at : at + 1], pltpu.roll(row, BZ - 1, 1))
            for i, piece in enumerate((before, row, after)):
                ahead[i * PACK : (i + 1) * PACK, to : to + BZ] = piece.astype(bf16)
    rows_one = samples * C_ONE
    count = 27 * PACK
    product = jnp.zeros((rows_one, count), f32)
    for x in range(BX):
        pieces = []
        for ox in OFFS:
            for oy in OFFS:
                at = ((x + 1 + ox) * (BY + 2) + 1 + oy) * BZ
                pieces.append(ahead[:, at : at + plane])
        product = product + lax.dot_general(
            conv_one[:, x * plane : (x + 1) * plane],
            jnp.concatenate(pieces, axis=0),
            NT,
            preferred_element_type=f32,
        )
    sample_of = (iota((C_ONE, count), 1) % PACK) // C_IN
    folded = jnp.zeros((C_ONE, count), f32)
    for s in range(samples):
        folded = folded + jnp.where(sample_of == s, product[s * C_ONE : (s + 1) * C_ONE], 0.0)
    k = iota((count, LANES), 0)
    fold = ((k // PACK) * C_IN + k % C_IN == iota((count, LANES), 1)).astype(f32)
    sums[:, ONE_AT:] = (
        jnp.dot(folded, fold, preferred_element_type=f32, precision=lax.Precision.HIGHEST) * scale_one
    )


def finish(mine, theirs, grad_one, grad_two):
    total = mine[...] + theirs[...]
    for o in range(27):
        grad_two[o] = total[:, o * C_TWO : (o + 1) * C_TWO]
    turned = total[:, ONE_AT:].T
    for o in range(27):
        grad_one[o] = turned[o * C_IN : (o + 1) * C_IN]


def call(body, shapes, operands, scratch=(), flops=0, moved=0):
    return pl.pallas_call(
        body,
        out_shape=shapes,
        in_specs=[pl.BlockSpec(memory_space=pltpu.VMEM)] * len(operands),
        out_specs=jax.tree.map(lambda _: pl.BlockSpec(memory_space=pltpu.VMEM), shapes),
        scratch_shapes=list(scratch),
        compiler_params=pltpu.CompilerParams(vmem_limit_bytes=32 * 2**20),
        cost_estimate=pl.CostEstimate(flops=flops, bytes_accessed=moved, transcendentals=0),
    )(*operands)


def block_side(blocks):
    return min(k for k in range(1, blocks + 1) if k * k * k >= blocks)


def neighbour(array, side, stride, of):
    blocks = lax.axis_size("space")
    pairs = []
    for i in range(blocks):
        c = i // stride % side
        pairs.append((i + ((c + of) % side - c) * stride, i))
    return lax.ppermute(array, "space", pairs)


def both_sides(array, side, stride):
    below = neighbour(array, side, stride, -1)
    return {-1: below, 1: below if side == 2 else neighbour(array, side, stride, 1)}


def swapped(array, axis, bit):
    size = lax.axis_size(axis)
    return lax.ppermute(array, axis, [(i, i ^ bit) for i in range(size)])


def local(inputs, mask_one, place_one, pooled_one, w_two, mask_two, place_two, grad_two):
    blocks = lax.axis_size("space")
    side = block_side(blocks)
    samples = inputs.shape[0]
    cells = inputs.shape[3]
    half_cells = HX * HY * HZ
    shape = jax.ShapeDtypeStruct
    vp, edge, own, faces_x, ends_y, mids_y = call(
        functools.partial(prepare, samples),
        (
            shape((2 * samples * C_TWO, LANES), bf16),
            shape((C_TWO + PACK, LANES), bf16),
            shape((PACK, cells), bf16),
            shape((PACK, 2 * BY * BZ), bf16),
            shape((PACK, 4 * BZ), bf16),
            shape((PACK, 4 * BZ), bf16),
        ),
        (grad_two, place_two, mask_two, inputs),
        flops=2 * 10**7,
        moved=2**20,
    )
    chosen, flat_weights = call(
        functools.partial(select_one, samples),
        (shape((samples * C_ONE, cells), bf16), shape((C_ONE, 27 * C_TWO), bf16)),
        (place_one, mask_one, w_two),
        flops=2 * 10**7,
        moved=3 * 2**20,
    )
    edge_z = both_sides(edge, side, 1)
    vp_at = {(0, 0): vp}
    edge_at = {(0, 0, n): edge_z[n] for n in (-1, 1)}
    for n, got in both_sides(vp, side, side * side).items():
        vp_at[n, 0] = got
    for nz in (-1, 1):
        if nz == 1 and side == 2:
            for n in (-1, 1):
                edge_at[n, 0, 1] = edge_at[n, 0, -1]
            continue
        for n, got in both_sides(edge_z[nz], side, side * side).items():
            edge_at[n, 0, nz] = got
    ends_at = {(0, n): got for n, got in both_sides(ends_y, side, side).items()}
    mids_at = {(0, n): got for n, got in both_sides(mids_y, side, side).items()}
    for nx in OFFS:
        if nx == 1 and side == 2:
            for n in (-1, 1):
                vp_at[1, n] = vp_at[-1, n]
            continue
        for n, got in both_sides(vp_at[nx, 0], side, side).items():
            vp_at[nx, n] = got
    for nx in OFFS:
        for nz in (-1, 1):
            for n in (-1, 1):
                if side == 2 and (nx == 1 or nz == 1):
                    edge_at[nx, n, nz] = edge_at[-abs(nx), n, -1]
            if side == 2 and (nx == 1 or nz == 1):
                continue
            for n, got in both_sides(edge_at[nx, 0, nz], side, side).items():
                edge_at[nx, n, nz] = got
    faces_at = both_sides(faces_x, side, side * side)
    for ny in (-1, 1):
        if ny == 1 and side == 2:
            for n in (-1, 1):
                ends_at[n, 1] = ends_at[n, -1]
            continue
        for n, got in both_sides(ends_at[0, ny], side, side * side).items():
            ends_at[n, ny] = got

    def distinct(table):
        arrays, places = [], {}
        for key, array in table.items():
            found = [i for i, a in enumerate(arrays) if a is array]
            if not found:
                arrays.append(array)
            places[key] = found[0] if found else len(arrays) - 1
        return arrays, places

    y_at = {(nx, ny, True): a for (nx, ny), a in ends_at.items()}
    y_at.update({(nx, ny, False): a for (nx, ny), a in mids_at.items()})
    vps, where_vp = distinct(vp_at)
    edges, where_edge = distinct(edge_at)
    xs, where_x = distinct(faces_at)
    ys, where_y = distinct(y_at)
    where = {"vp": where_vp, "edge": where_edge, "x": where_x, "y": where_y}
    total = lax.axis_size("dp") * samples * blocks * cells
    body = functools.partial(
        main,
        samples,
        float(total) ** -0.5,
        float(total // 8) ** -0.5,
        where,
        len(vps),
        len(edges),
        len(xs),
        len(ys),
    )
    grad_pooled, sums = call(
        body,
        (shape((samples, 1, C_ONE, half_cells), bf16), shape((C_ONE, WIDTH), f32)),
        (*vps, *edges, *xs, *ys, own, pooled_one, chosen, flat_weights),
        scratch=(
            pltpu.VMEM((samples, 3 * C_TWO, (HX + 2) * (HY + 2) * HZ), bf16),
            pltpu.VMEM((samples * C_ONE, cells), bf16),
            pltpu.VMEM((3 * PACK, (BX + 2) * (BY + 2) * BZ), bf16),
        ),
        flops=10**9,
        moved=3 * 2**20,
    )
    steps = []
    for axis in ("dp", "space"):
        bit = 1
        while bit < lax.axis_size(axis):
            steps.append((axis, bit))
            bit *= 2
    for axis, bit in steps[:-1]:
        sums = sums + swapped(sums, axis, bit)
    grad_w_one, grad_w_two = call(
        finish,
        (shape((27, C_IN, C_ONE), f32), shape((27, C_ONE, C_TWO), f32)),
        (sums, swapped(sums, *steps[-1])),
    )
    return grad_pooled, grad_w_one, grad_w_two


def solution(mesh):
    split = P("dp", "space", None, None)
    return jax.shard_map(
        local,
        mesh=mesh,
        in_specs=(split, split, split, split, P(), split, split, split),
        out_specs=(split, P(), P()),
        check_vma=False,
    )
```

profile of v0, /device:TPU:0, one launch (start us, length us, event | category | flops | bytes accessed | tf_op | source)
XLA Modules:
  0.0 58.9 jit_solution(13778684455369266239)
XLA Ops:
  0.6 0.0 copy-start.1
  0.6 1.0 %copy-done.1 = s32[3,1,32,1024]{3,2,1,0:T(8,128)S(1)} copy-done((s32[3,1,32,1024]{3,2,1,0:T(8,128)S(1)}, s32[3,1,32,1024]{3,2,1,0:T(8,128)}, u32[]{:S(2)}) %copy-start.1) | copy-done | bytes 393240
  1.6 0.0 copy-start.3
  1.6 0.9 %copy-done.3 = bf16[3,1,4,8192]{3,2,1,0:T(4,128)(2,1)S(1)} copy-done((bf16[3,1,4,8192]{3,2,1,0:T(4,128)(2,1)S(1)}, bf16[3,1,4,8192]{3,2,1,0:T(4,128)(2,1)}, u32[]{:S(2)}) %copy-start.3) | copy-done | bytes 196632
  2.6 0.0 copy-start.5
  2.6 0.8 %copy-done.5 = s32[3,1,32,128]{3,2,1,0:T(8,128)S(1)} copy-done((s32[3,1,32,128]{3,2,1,0:T(8,128)S(1)}, s32[3,1,32,128]{3,2,1,0:T(8,128)}, u32[]{:S(2)}) %copy-start.5) | copy-done | bytes 49176
  3.4 0.0 copy-start.6
  3.4 0.7 %copy-done.6 = bf16[3,1,32,128]{3,2,1,0:T(8,128)(2,1)S(1)} copy-done((bf16[3,1,32,128]{3,2,1,0:T(8,128)(2,1)S(1)}, bf16[3,1,32,128]{3,2,1,0:T(8,128)(2,1)}, u32[]{:S(2)}) %copy-start.6) | copy-done | bytes 24600
  4.1 0.0 copy-start.7
  4.1 0.5 shard_map.103
  4.6 4.0 %collective-permute-start.7 = (bf16[16,4096]{1,0:T(8,128)(2,1)S(1)}, bf16[16,4096]{1,0:T(8,128)(2,1)S(1)}, u32[]{:S(2)}, u32[]{:S(2)}) collective-permute-start(bf16[16,4096]{1,0:T(8,128)(2,1)S(1)} %get-tuple-element.17), channel_id=1, source_target_pairs={{4,0},{5,1},{6,2},{7,3},{0,4},{1,5},{2,6},{3,7},{12,8},{13,9},{14,... | collective-permute-start | bytes 393224 | tf_op jit(solution)/shard_map/ppermute | solution.py:275
  8.6 0.0 collective-permute-start
  8.7 1.8 %collective-permute-start.3 = (bf16[48,128]{1,0:T(8,128)(2,1)S(1)}, bf16[48,128]{1,0:T(8,128)(2,1)S(1)}, u32[]{:S(2)}, u32[]{:S(2)}) collective-permute-start(bf16[48,128]{1,0:T(8,128)(2,1)S(1)} %get-tuple-element.16), channel_id=1, source_target_pairs={{1,0},{0,1},{3,2},{2,3},{5,4},{4,5},{7,6},{6,7},{9,8},{8,9},{11,10... | collective-permute-start | bytes 36872 | tf_op jit(solution)/shard_map/ppermute | solution.py:275
  10.5 1.6 %collective-permute-start.8 = (bf16[16,1024]{1,0:T(8,128)(2,1)S(1)}, bf16[16,1024]{1,0:T(8,128)(2,1)S(1)}, u32[]{:S(2)}, u32[]{:S(2)}) collective-permute-start(bf16[16,1024]{1,0:T(8,128)(2,1)S(1)} %get-tuple-element.18), channel_id=1, source_target_pairs={{2,0},{3,1},{0,2},{1,3},{6,4},{7,5},{4,6},{5,7},{10,8},{11,9},{8,1... | collective-permute-start | bytes 98312 | tf_op jit(solution)/shard_map/ppermute | solution.py:275
  12.0 0.3 collective-permute-done.3.refs_4_
  12.4 1.9 %collective-permute-start.6 = (bf16[48,128]{1,0:T(8,128)(2,1)S(1)}, bf16[48,128]{1,0:T(8,128)(2,1)S(1)}, u32[]{:S(2)}, u32[]{:S(2)}) collective-permute-start(bf16[48,128]{1,0:T(8,128)(2,1)S(1)} %collective-permute-done.3.refs_4_), channel_id=1, source_target_pairs={{2,0},{3,1},{0,2},{1,3},{6,4},{7,5},{4,6},{5,7},{10,8},{11,9},{8,1... | collective-permute-start | bytes 36872 | tf_op jit(solution)/shard_map/ppermute | solution.py:275
  14.2 2.6 %collective-permute-start.4 = (bf16[48,128]{1,0:T(8,128)(2,1)S(1)}, bf16[48,128]{1,0:T(8,128)(2,1)S(1)}, u32[]{:S(2)}, u32[]{:S(2)}) collective-permute-start(bf16[48,128]{1,0:T(8,128)(2,1)S(1)} %collective-permute-done.3.refs_4_), channel_id=1, source_target_pairs={{4,0},{5,1},{6,2},{7,3},{0,4},{1,5},{2,6},{3,7},{12,8},{13,9},{14,... | collective-permute-start | bytes 36872 | tf_op jit(solution)/shard_map/ppermute | solution.py:275
  16.8 0.0 collective-permute-done.6.refs_7_
  16.8 1.1 %collective-permute-start.2 = (bf16[192,128]{1,0:T(8,128)(2,1)S(1)}, bf16[192,128]{1,0:T(8,128)(2,1)S(1)}, u32[]{:S(2)}, u32[]{:S(2)}) collective-permute-start(bf16[192,128]{1,0:T(8,128)(2,1)S(1)} %get-tuple-element.15.refs_0_), channel_id=1, source_target_pairs={{2,0},{3,1},{0,2},{1,3},{6,4},{7,5},{4,6},{5,7},{10,8},{11,9},{8,1... | collective-permute-start | bytes 147464 | tf_op jit(solution)/shard_map/ppermute | solution.py:275
  17.9 0.0 collective-permute-done.refs_1_
  17.9 0.9 %collective-permute-start.1 = (bf16[192,128]{1,0:T(8,128)(2,1)S(1)}, bf16[192,128]{1,0:T(8,128)(2,1)S(1)}, u32[]{:S(2)}, u32[]{:S(2)}) collective-permute-start(bf16[192,128]{1,0:T(8,128)(2,1)S(1)} %collective-permute-done.refs_1_), channel_id=1, source_target_pairs={{2,0},{3,1},{0,2},{1,3},{6,4},{7,5},{4,6},{5,7},{10,8},{11,9},{8,1... | collective-permute-start | bytes 147464 | tf_op jit(solution)/shard_map/ppermute | solution.py:275
  18.9 0.0 collective-permute-done.4.refs_5_
  18.9 1.1 %collective-permute-start.10 = (bf16[16,1024]{1,0:T(8,128)(2,1)S(1)}, bf16[16,1024]{1,0:T(8,128)(2,1)S(1)}, u32[]{:S(2)}, u32[]{:S(2)}) collective-permute-start(bf16[16,1024]{1,0:T(8,128)(2,1)S(1)} %get-tuple-element.19), channel_id=1, source_target_pairs={{2,0},{3,1},{0,2},{1,3},{6,4},{7,5},{4,6},{5,7},{10,8},{11,9},{8,1... | collective-permute-start | bytes 98312 | tf_op jit(solution)/shard_map/ppermute | solution.py:275
  20.0 0.0 collective-permute-done.8.refs_9_
  20.0 4.3 %collective-permute-start.9 = (bf16[16,1024]{1,0:T(8,128)(2,1)S(1)}, bf16[16,1024]{1,0:T(8,128)(2,1)S(1)}, u32[]{:S(2)}, u32[]{:S(2)}) collective-permute-start(bf16[16,1024]{1,0:T(8,128)(2,1)S(1)} %collective-permute-done.8.refs_9_), channel_id=1, source_target_pairs={{4,0},{5,1},{6,2},{7,3},{0,4},{1,5},{2,6},{3,7},{12,8},{13,9},{14,... | collective-permute-start | bytes 98312 | tf_op jit(solution)/shard_map/ppermute | solution.py:275
  24.3 0.0 collective-permute-done.10.refs_11_
  24.3 0.1 collective-permute-start.5
  24.3 0.0 copy-start
  24.3 1.4 %copy-done = s32[3,1,16,8192]{3,2,1,0:T(8,128)S(1)} copy-done((s32[3,1,16,8192]{3,2,1,0:T(8,128)S(1)}, s32[3,1,16,8192]{3,2,1,0:T(8,128)}, u32[]{:S(2)}) %copy-start) | copy-done | bytes 1572888
  25.7 0.0 copy-start.2
  25.7 0.9 %copy-done.2 = s32[3,1,16,1024]{3,2,1,0:T(8,128)S(1)} copy-done((s32[3,1,16,1024]{3,2,1,0:T(8,128)S(1)}, s32[3,1,16,1024]{3,2,1,0:T(8,128)}, u32[]{:S(2)}) %copy-start.2) | copy-done | bytes 196632
  26.6 0.0 copy-start.4
  26.7 0.9 %copy-done.4 = bf16[27,16,32]{2,1,0:T(8,128)(2,1)S(1)} copy-done((bf16[27,16,32]{2,1,0:T(8,128)(2,1)S(1)}, bf16[27,16,32]{2,1,0:T(8,128)(2,1)}, u32[]{:S(2)}) %copy-start.4) | copy-done | bytes 27672
  27.5 0.4 shard_map.104
  27.9 0.0 collective-permute-done.5.refs_6_
  28.0 0.0 collective-permute-done.2.refs_3_
  28.0 0.0 collective-permute-done.9.refs_10_
  28.0 0.0 collective-permute-done.1.refs_2_
  28.0 0.0 collective-permute-done.7.refs_8_
  28.0 0.0 copy-done.7
  28.0 8.2 %shard_map.105 = (bf16[3,1,16,1024]{3,2,1,0:T(8,128)(2,1)}, f32[16,1024]{1,0:T(8,128)S(1)}) custom-call(bf16[192,128]{1,0:T(8,128)(2,1)S(1)} %get-tuple-element.15.refs_0_, bf16[192,128]{1,0:T(8,128)(2,1)S(1)} %collective-permute-done.refs_1_, bf16[192,128]{1,0:T(8,128)(2,1)S(1)} %collective-permute-done.1.refs_2_, ...), custom_call_target="tpu_custom_call" | custom-call | flops 1000000000 | bytes 3145728 | tf_op jit(solution)/shard_map/pallas_call | solution.py:254
  36.2 0.0 collective-permute-start.11
  36.2 1.3 %collective-permute-done.11 = f32[16,1024]{1,0:T(8,128)S(1)} collective-permute-done((f32[16,1024]{1,0:T(8,128)S(1)}, f32[16,1024]{1,0:T(8,128)S(1)}, u32[]{:S(2)}, u32[]{:S(2)}) %collective-permute-start.11) | collective-permute-done | bytes 65568 | tf_op jit(solution)/shard_map/ppermute | solution.py:285
  37.5 1.6 %collective-permute-start.12 = (f32[16,1024]{1,0:T(8,128)S(1)}, f32[16,1024]{1,0:T(8,128)S(1)}, u32[]{:S(2)}, u32[]{:S(2)}) collective-permute-start(f32[16,1024]{1,0:T(8,128)S(1)} %add.12), channel_id=1, source_target_pairs={{0,16},{8,24},{16,0},{24,8},{1,17},{9,25},{17,1},{25,9},{2,18},{10... | collective-permute-start | bytes 196616 | tf_op jit(solution)/shard_map/ppermute | solution.py:285
  39.1 2.7 %collective-permute-done.12 = f32[16,1024]{1,0:T(8,128)S(1)} collective-permute-done((f32[16,1024]{1,0:T(8,128)S(1)}, f32[16,1024]{1,0:T(8,128)S(1)}, u32[]{:S(2)}, u32[]{:S(2)}) %collective-permute-start.12) | collective-permute-done | bytes 65568 | tf_op jit(solution)/shard_map/ppermute | solution.py:285
  41.9 1.5 %collective-permute-start.13 = (f32[16,1024]{1,0:T(8,128)S(1)}, f32[16,1024]{1,0:T(8,128)S(1)}, u32[]{:S(2)}, u32[]{:S(2)}) collective-permute-start(f32[16,1024]{1,0:T(8,128)S(1)} %add.13), channel_id=1, source_target_pairs={{0,1},{1,0},{2,3},{3,2},{4,5},{5,4},{6,7},{7,6},{8,9},{9,8},{10,11... | collective-permute-start | bytes 196616 | tf_op jit(solution)/shard_map/ppermute | solution.py:285
  43.4 2.8 %collective-permute-done.13 = f32[16,1024]{1,0:T(8,128)S(1)} collective-permute-done((f32[16,1024]{1,0:T(8,128)S(1)}, f32[16,1024]{1,0:T(8,128)S(1)}, u32[]{:S(2)}, u32[]{:S(2)}) %collective-permute-start.13) | collective-permute-done | bytes 65568 | tf_op jit(solution)/shard_map/ppermute | solution.py:285
  46.2 2.0 %collective-permute-start.14 = (f32[16,1024]{1,0:T(8,128)S(1)}, f32[16,1024]{1,0:T(8,128)S(1)}, u32[]{:S(2)}, u32[]{:S(2)}) collective-permute-start(f32[16,1024]{1,0:T(8,128)S(1)} %add.14), channel_id=1, source_target_pairs={{0,2},{1,3},{2,0},{3,1},{4,6},{5,7},{6,4},{7,5},{8,10},{9,11},{10,... | collective-permute-start | bytes 196616 | tf_op jit(solution)/shard_map/ppermute | solution.py:285
  48.2 2.3 %collective-permute-done.14 = f32[16,1024]{1,0:T(8,128)S(1)} collective-permute-done((f32[16,1024]{1,0:T(8,128)S(1)}, f32[16,1024]{1,0:T(8,128)S(1)}, u32[]{:S(2)}, u32[]{:S(2)}) %collective-permute-start.14) | collective-permute-done | bytes 65568 | tf_op jit(solution)/shard_map/ppermute | solution.py:285
  50.6 3.9 %collective-permute-start.15 = (f32[16,1024]{1,0:T(8,128)S(1)}, f32[16,1024]{1,0:T(8,128)S(1)}, u32[]{:S(2)}, u32[]{:S(2)}) collective-permute-start(f32[16,1024]{1,0:T(8,128)S(1)} %add.15.mine), channel_id=1, source_target_pairs={{0,4},{1,5},{2,6},{3,7},{4,0},{5,1},{6,2},{7,3},{8,12},{9,13},{10,... | collective-permute-start | bytes 196616 | tf_op jit(solution)/shard_map/ppermute | solution.py:285
  54.5 2.9 %collective-permute-done.15.theirs = f32[16,1024]{1,0:T(8,128)S(1)} collective-permute-done((f32[16,1024]{1,0:T(8,128)S(1)}, f32[16,1024]{1,0:T(8,128)S(1)}, u32[]{:S(2)}, u32[]{:S(2)}) %collective-permute-start.15) | collective-permute-done | bytes 65568 | tf_op jit(solution)/shard_map/ppermute | solution.py:285
  57.4 0.8 %shard_map.106 = (f32[27,4,16]{2,1,0:T(4,128)S(1)}, f32[27,16,32]{2,1,0:T(8,128)}) custom-call(f32[16,1024]{1,0:T(8,128)S(1)} %add.15.mine, f32[16,1024]{1,0:T(8,128)S(1)} %collective-permute-done.15.theirs), custom_call_target="tpu_custom_call" | custom-call | tf_op jit(solution)/shard_map/pallas_call | solution.py:254
  58.2 0.7 %copy.11 = f32[27,4,16]{0,2,1:T(8,128)} copy(f32[27,4,16]{2,1,0:T(4,128)S(1)} %get-tuple-element.28) | data formatting | bytes 13824
  (4 shorter events, 0.0 us)
Async XLA Ops:
  0.6 1.0 %copy-start.1 = (s32[3,1,32,1024]{3,2,1,0:T(8,128)S(1)}, s32[3,1,32,1024]{3,2,1,0:T(8,128)}, u32[]{:S(2)}) copy-start(s32[3,1,32,1024]{3,2,1,0:T(8,128)} %mask.2) | copy-start | bytes 1179652
  1.6 0.9 %copy-start.3 = (bf16[3,1,4,8192]{3,2,1,0:T(4,128)(2,1)S(1)}, bf16[3,1,4,8192]{3,2,1,0:T(4,128)(2,1)}, u32[]{:S(2)}) copy-start(bf16[3,1,4,8192]{3,2,1,0:T(4,128)(2,1)} %source.1) | copy-start | bytes 589828
  2.6 0.8 %copy-start.5 = (s32[3,1,32,128]{3,2,1,0:T(8,128)S(1)}, s32[3,1,32,128]{3,2,1,0:T(8,128)}, u32[]{:S(2)}) copy-start(s32[3,1,32,128]{3,2,1,0:T(8,128)} %place.2) | copy-start | bytes 147460
  3.4 0.7 %copy-start.6 = (bf16[3,1,32,128]{3,2,1,0:T(8,128)(2,1)S(1)}, bf16[3,1,32,128]{3,2,1,0:T(8,128)(2,1)}, u32[]{:S(2)}) copy-start(bf16[3,1,32,128]{3,2,1,0:T(8,128)(2,1)} %grad.1) | copy-start | bytes 73732
  4.1 23.9 %copy-start.7 = (bf16[3,1,16,1024]{3,2,1,0:T(8,128)(2,1)S(1)}, bf16[3,1,16,1024]{3,2,1,0:T(8,128)(2,1)}, u32[]{:S(2)}) copy-start(bf16[3,1,16,1024]{3,2,1,0:T(8,128)(2,1)} %refs_13_.1) | copy-start | bytes 294916
  4.6 23.4 %collective-permute-start.7 = (bf16[16,4096]{1,0:T(8,128)(2,1)S(1)}, bf16[16,4096]{1,0:T(8,128)(2,1)S(1)}, u32[]{:S(2)}, u32[]{:S(2)}) collective-permute-start(bf16[16,4096]{1,0:T(8,128)(2,1)S(1)} %get-tuple-element.17), channel_id=1, source_target_pairs={{4,0},{5,1},{6,2},{7,3},{0,4},{1,5},{2,6},{3,7},{12,8},{13,9},{14,... | collective-permute-start | bytes 393224 | tf_op jit(solution)/shard_map/ppermute | solution.py:275
  8.6 9.3 %collective-permute-start = (bf16[192,128]{1,0:T(8,128)(2,1)S(1)}, bf16[192,128]{1,0:T(8,128)(2,1)S(1)}, u32[]{:S(2)}, u32[]{:S(2)}) collective-permute-start(bf16[192,128]{1,0:T(8,128)(2,1)S(1)} %get-tuple-element.15.refs_0_), channel_id=1, source_target_pairs={{4,0},{5,1},{6,2},{7,3},{0,4},{1,5},{2,6},{3,7},{12,8},{13,9},{14,... | collective-permute-start | bytes 147464 | tf_op jit(solution)/shard_map/ppermute | solution.py:275
  8.7 3.7 %collective-permute-start.3 = (bf16[48,128]{1,0:T(8,128)(2,1)S(1)}, bf16[48,128]{1,0:T(8,128)(2,1)S(1)}, u32[]{:S(2)}, u32[]{:S(2)}) collective-permute-start(bf16[48,128]{1,0:T(8,128)(2,1)S(1)} %get-tuple-element.16), channel_id=1, source_target_pairs={{1,0},{0,1},{3,2},{2,3},{5,4},{4,5},{7,6},{6,7},{9,8},{8,9},{11,10... | collective-permute-start | bytes 36872 | tf_op jit(solution)/shard_map/ppermute | solution.py:275
  10.5 9.5 %collective-permute-start.8 = (bf16[16,1024]{1,0:T(8,128)(2,1)S(1)}, bf16[16,1024]{1,0:T(8,128)(2,1)S(1)}, u32[]{:S(2)}, u32[]{:S(2)}) collective-permute-start(bf16[16,1024]{1,0:T(8,128)(2,1)S(1)} %get-tuple-element.18), channel_id=1, source_target_pairs={{2,0},{3,1},{0,2},{1,3},{6,4},{7,5},{4,6},{5,7},{10,8},{11,9},{8,1... | collective-permute-start | bytes 98312 | tf_op jit(solution)/shard_map/ppermute | solution.py:275
  12.4 4.5 %collective-permute-start.6 = (bf16[48,128]{1,0:T(8,128)(2,1)S(1)}, bf16[48,128]{1,0:T(8,128)(2,1)S(1)}, u32[]{:S(2)}, u32[]{:S(2)}) collective-permute-start(bf16[48,128]{1,0:T(8,128)(2,1)S(1)} %collective-permute-done.3.refs_4_), channel_id=1, source_target_pairs={{2,0},{3,1},{0,2},{1,3},{6,4},{7,5},{4,6},{5,7},{10,8},{11,9},{8,1... | collective-permute-start | bytes 36872 | tf_op jit(solution)/shard_map/ppermute | solution.py:275
  14.2 4.6 %collective-permute-start.4 = (bf16[48,128]{1,0:T(8,128)(2,1)S(1)}, bf16[48,128]{1,0:T(8,128)(2,1)S(1)}, u32[]{:S(2)}, u32[]{:S(2)}) collective-permute-start(bf16[48,128]{1,0:T(8,128)(2,1)S(1)} %collective-permute-done.3.refs_4_), channel_id=1, source_target_pairs={{4,0},{5,1},{6,2},{7,3},{0,4},{1,5},{2,6},{3,7},{12,8},{13,9},{14,... | collective-permute-start | bytes 36872 | tf_op jit(solution)/shard_map/ppermute | solution.py:275
  16.8 11.1 %collective-permute-start.2 = (bf16[192,128]{1,0:T(8,128)(2,1)S(1)}, bf16[192,128]{1,0:T(8,128)(2,1)S(1)}, u32[]{:S(2)}, u32[]{:S(2)}) collective-permute-start(bf16[192,128]{1,0:T(8,128)(2,1)S(1)} %get-tuple-element.15.refs_0_), channel_id=1, source_target_pairs={{2,0},{3,1},{0,2},{1,3},{6,4},{7,5},{4,6},{5,7},{10,8},{11,9},{8,1... | collective-permute-start | bytes 147464 | tf_op jit(solution)/shard_map/ppermute | solution.py:275
  17.9 10.0 %collective-permute-start.1 = (bf16[192,128]{1,0:T(8,128)(2,1)S(1)}, bf16[192,128]{1,0:T(8,128)(2,1)S(1)}, u32[]{:S(2)}, u32[]{:S(2)}) collective-permute-start(bf16[192,128]{1,0:T(8,128)(2,1)S(1)} %collective-permute-done.refs_1_), channel_id=1, source_target_pairs={{2,0},{3,1},{0,2},{1,3},{6,4},{7,5},{4,6},{5,7},{10,8},{11,9},{8,1... | collective-permute-start | bytes 147464 | tf_op jit(solution)/shard_map/ppermute | solution.py:275
  18.9 5.4 %collective-permute-start.10 = (bf16[16,1024]{1,0:T(8,128)(2,1)S(1)}, bf16[16,1024]{1,0:T(8,128)(2,1)S(1)}, u32[]{:S(2)}, u32[]{:S(2)}) collective-permute-start(bf16[16,1024]{1,0:T(8,128)(2,1)S(1)} %get-tuple-element.19), channel_id=1, source_target_pairs={{2,0},{3,1},{0,2},{1,3},{6,4},{7,5},{4,6},{5,7},{10,8},{11,9},{8,1... | collective-permute-start | bytes 98312 | tf_op jit(solution)/shard_map/ppermute | solution.py:275
  20.0 8.0 %collective-permute-start.9 = (bf16[16,1024]{1,0:T(8,128)(2,1)S(1)}, bf16[16,1024]{1,0:T(8,128)(2,1)S(1)}, u32[]{:S(2)}, u32[]{:S(2)}) collective-permute-start(bf16[16,1024]{1,0:T(8,128)(2,1)S(1)} %collective-permute-done.8.refs_9_), channel_id=1, source_target_pairs={{4,0},{5,1},{6,2},{7,3},{0,4},{1,5},{2,6},{3,7},{12,8},{13,9},{14,... | collective-permute-start | bytes 98312 | tf_op jit(solution)/shard_map/ppermute | solution.py:275
  24.3 3.7 %collective-permute-start.5 = (bf16[48,128]{1,0:T(8,128)(2,1)S(1)}, bf16[48,128]{1,0:T(8,128)(2,1)S(1)}, u32[]{:S(2)}, u32[]{:S(2)}) collective-permute-start(bf16[48,128]{1,0:T(8,128)(2,1)S(1)} %collective-permute-done.4.refs_5_), channel_id=1, source_target_pairs={{2,0},{3,1},{0,2},{1,3},{6,4},{7,5},{4,6},{5,7},{10,8},{11,9},{8,1... | collective-permute-start | bytes 36872 | tf_op jit(solution)/shard_map/ppermute | solution.py:275
  24.3 1.4 %copy-start = (s32[3,1,16,8192]{3,2,1,0:T(8,128)S(1)}, s32[3,1,16,8192]{3,2,1,0:T(8,128)}, u32[]{:S(2)}) copy-start(s32[3,1,16,8192]{3,2,1,0:T(8,128)} %mask.3) | copy-start | bytes 4718596
  25.7 0.9 %copy-start.2 = (s32[3,1,16,1024]{3,2,1,0:T(8,128)S(1)}, s32[3,1,16,1024]{3,2,1,0:T(8,128)}, u32[]{:S(2)}) copy-start(s32[3,1,16,1024]{3,2,1,0:T(8,128)} %place.3) | copy-start | bytes 589828
  26.6 0.9 %copy-start.4 = (bf16[27,16,32]{2,1,0:T(8,128)(2,1)S(1)}, bf16[27,16,32]{2,1,0:T(8,128)(2,1)}, u32[]{:S(2)}) copy-start(bf16[27,16,32]{2,1,0:T(8,128)(2,1)} %weights.1) | copy-start | bytes 82948
  36.2 1.3 %collective-permute-start.11 = (f32[16,1024]{1,0:T(8,128)S(1)}, f32[16,1024]{1,0:T(8,128)S(1)}, u32[]{:S(2)}, u32[]{:S(2)}) collective-permute-start(f32[16,1024]{1,0:T(8,128)S(1)} %get-tuple-element.24), channel_id=1, source_target_pairs={{0,8},{8,0},{16,24},{24,16},{1,9},{9,1},{17,25},{25,17},{2,10},{10... | collective-permute-start | bytes 196616 | tf_op jit(solution)/shard_map/ppermute | solution.py:285
  37.5 4.3 %collective-permute-start.12 = (f32[16,1024]{1,0:T(8,128)S(1)}, f32[16,1024]{1,0:T(8,128)S(1)}, u32[]{:S(2)}, u32[]{:S(2)}) collective-permute-start(f32[16,1024]{1,0:T(8,128)S(1)} %add.12), channel_id=1, source_target_pairs={{0,16},{8,24},{16,0},{24,8},{1,17},{9,25},{17,1},{25,9},{2,18},{10... | collective-permute-start | bytes 196616 | tf_op jit(solution)/shard_map/ppermute | solution.py:285
  41.9 4.3 %collective-permute-start.13 = (f32[16,1024]{1,0:T(8,128)S(1)}, f32[16,1024]{1,0:T(8,128)S(1)}, u32[]{:S(2)}, u32[]{:S(2)}) collective-permute-start(f32[16,1024]{1,0:T(8,128)S(1)} %add.13), channel_id=1, source_target_pairs={{0,1},{1,0},{2,3},{3,2},{4,5},{5,4},{6,7},{7,6},{8,9},{9,8},{10,11... | collective-permute-start | bytes 196616 | tf_op jit(solution)/shard_map/ppermute | solution.py:285
  46.2 4.3 %collective-permute-start.14 = (f32[16,1024]{1,0:T(8,128)S(1)}, f32[16,1024]{1,0:T(8,128)S(1)}, u32[]{:S(2)}, u32[]{:S(2)}) collective-permute-start(f32[16,1024]{1,0:T(8,128)S(1)} %add.14), channel_id=1, source_target_pairs={{0,2},{1,3},{2,0},{3,1},{4,6},{5,7},{6,4},{7,5},{8,10},{9,11},{10,... | collective-permute-start | bytes 196616 | tf_op jit(solution)/shard_map/ppermute | solution.py:285
  50.6 6.9 %collective-permute-start.15 = (f32[16,1024]{1,0:T(8,128)S(1)}, f32[16,1024]{1,0:T(8,128)S(1)}, u32[]{:S(2)}, u32[]{:S(2)}) collective-permute-start(f32[16,1024]{1,0:T(8,128)S(1)} %add.15.mine), channel_id=1, source_target_pairs={{0,4},{1,5},{2,6},{3,7},{4,0},{5,1},{6,2},{7,3},{8,12},{9,13},{10,... | collective-permute-start | bytes 196616 | tf_op jit(solution)/shard_map/ppermute | solution.py:285
where the time goes:
time: 59.3 us; the launch traced here: 58.9 us
  starting transfers between devices  28.4 us (48%)
  waiting for transfers between devices  12.4 us (21%)
  Pallas kernels  9.91 us (17%)
  local copies, waits for them, and re-layouts  7.39 us (12%)
  between operations  0.72 us (1%)
    ppermute x11, starting transfers between devices, neighbour(): return lax.ppermute(array, 'space', pairs)  19.4 us
    ppermute x5, waiting for transfers between devices, swapped(): return lax.ppermute(array, axis, [(i, i ^ bit) for i in range(size)])  12 us
    pallas_call x4, Pallas kernels, call(): pl.pallas_call(body, out_shape=shapes, in_specs=[pl.BlockSpec(memory_spac...  9.91 us
    ppermute x5, starting transfers between devices, swapped(): return lax.ppermute(array, axis, [(i, i ^ bit) for i in range(size)])  9.08 us
    unnamed x17, local copies, waits for them, and re-layouts  7.39 us
  transfers between devices with their start and end apart: 16, of which 6 were waited for; matrix products, arithmetic and copies ran while one was open for 0% of the time, Pallas kernels for 1%

commit v1 on v0

v1 whole, which is shorter than its diff:
```python
import functools

import jax
import jax.numpy as jnp
from jax import lax
from jax.experimental import pallas as pl
from jax.experimental.pallas import tpu as pltpu
from jax.sharding import PartitionSpec as P

C_IN = 4
C_ONE = 16
C_TWO = 32
BX = 4
BY = 8
BZ = 256
HX, HY, HZ = BX // 2, BY // 2, BZ // 2
QY, QZ = HY // 2, HZ // 2
LANES = 128
PACK = 16
EDGE = C_TWO + PACK
OFFS = (-1, 0, 1)
GRAD_W_TWO = 27 * C_TWO
WIDTH = 1024
ONE_AT = WIDTH - LANES
STRIDE_ONE = LANES // C_IN
TABLE = 3 * QY * LANES
NT = (((1,), (1,)), ((), ()))
f32, bf16, i32 = jnp.float32, jnp.bfloat16, jnp.int32


def iota(shape, dim):
    return lax.broadcasted_iota(i32, shape, dim)


def doubling():
    return (iota((LANES, 2 * LANES), 0) == iota((LANES, 2 * LANES), 1) // 2).astype(bf16)


def fetch(pairs, sems):
    copies = [pltpu.make_async_copy(a, b, sems.at[i]) for i, (a, b) in enumerate(pairs)]
    for copy in copies:
        copy.start()
    return copies


def prepare(samples, *refs):
    far, (to_x, to_y, own), near, sems = refs[:4], refs[4:7], refs[7:11], refs[11]
    grad, place, mask, source = near
    copies = fetch(tuple(zip(far, near)), sems)
    rows = samples * C_TWO
    table = doubling()
    copies[0].wait()
    copies[1].wait()
    values = jnp.dot(grad[...].reshape(rows, LANES), table, preferred_element_type=f32)
    spots = place[...].reshape(rows, LANES).astype(f32).astype(bf16)
    wide = jnp.dot(spots, table, preferred_element_type=f32)
    parity = (iota((rows, LANES), 1) % 2).astype(f32)
    copies[2].wait()
    halves = []
    for qy in range(QY):
        v = values[:, qy * LANES : (qy + 1) * LANES]
        p = wide[:, qy * LANES : (qy + 1) * LANES] - parity
        total = jnp.zeros((rows, LANES), f32)
        for x in range(HX):
            for dy in range(2):
                at = (x * HY + 2 * qy + dy) * LANES
                on = mask[:, 0, :, at : at + LANES].reshape(rows, LANES) == 1
                total = total + jnp.where(on & (p == 4.0 * x + 2.0 * dy), v, 0.0)
        halves.append(total)
    kept = jnp.concatenate(halves, axis=1).astype(bf16)
    v = lax.dot_general(kept, table, NT, preferred_element_type=f32).astype(bf16)
    used = samples * C_IN
    for ref, at in ((to_x, BY * 4 * used), (to_y, 4 * 4 * used)):
        ref[at : at + rows] = v
        ref[at + rows : at + 2 * rows] = spots
    copies[3].wait()
    pieces = [source[s, 0].astype(f32) for s in range(samples)]
    if used < PACK:
        pieces.append(jnp.zeros((PACK - used, BX * BY * BZ), f32))
    cells = jnp.concatenate(pieces, axis=0)
    own[...] = cells.astype(bf16)
    for t in range(BY):
        group = []
        for x in (0, BX - 1):
            for y in (t // 2, BY - 1 - t // 2):
                at = (x * BY + y) * BZ + (t % 2) * LANES
                group.append(cells[0:used, at : at + LANES])
        to_x[4 * used * t : 4 * used * (t + 1)] = jnp.concatenate(group, axis=0).astype(bf16)
    for t in range(4):
        group = []
        for x in range(BX):
            at = (x * BY + (BY - 1) * (t // 2)) * BZ + (t % 2) * LANES
            group.append(cells[0:used, at : at + LANES])
        to_y[4 * used * t : 4 * used * (t + 1)] = jnp.concatenate(group, axis=0).astype(bf16)


def ends(samples, vp_row, to_x, own, edge):
    rows = samples * C_TWO
    lane = iota((LANES, LANES), 0)
    spot = (lane // QZ) * 2 + (lane % QZ == QZ - 1).astype(i32)
    spot = jnp.where((lane % QZ == 0) | (lane % QZ == QZ - 1), spot, -LANES)
    column = iota((LANES, LANES), 1)
    packed = jnp.zeros((C_TWO, LANES), f32)
    for s in range(samples):
        for t in range(2):
            pick = (spot + (8 * s + 4 * t) == column).astype(bf16)
            at = vp_row + t * rows + s * C_TWO
            packed = packed + jnp.dot(to_x[at : at + C_TWO], pick, preferred_element_type=f32)
    edge[0:C_TWO] = packed.astype(bf16)
    lane = iota((PACK, LANES), 1)
    packed = jnp.zeros((PACK, LANES), f32)
    for row in range(BX * BY):
        left = own[:, row * BZ : row * BZ + LANES].astype(f32)
        right = own[:, (row + 1) * BZ - LANES : (row + 1) * BZ].astype(f32)
        packed = jnp.where(lane == 2 * row, left[:, 0:1], packed)
        packed = jnp.where(lane == 2 * row + 1, right[:, LANES - 1 :], packed)
    edge[C_TWO:EDGE] = packed.astype(bf16)


def select_one(samples, *refs):
    far, (chosen, flat_weights, expand), near, sems = refs[:3], refs[3:6], refs[6:9], refs[9]
    place, mask, weights = near
    copies = fetch(tuple(zip(far, near)), sems)
    k = iota((2 * LANES, TABLE), 0)
    j = iota((1, TABLE), 1)
    shift = j // (QY * LANES) - 1
    qy = (j // LANES) % QY
    z = j % LANES - shift
    beyond = LANES + qy * 2 + (z < 0).astype(i32)
    expand[...] = (k == jnp.where((z >= 0) & (z < LANES), qy * QZ + z // 2, beyond)).astype(bf16)
    rows = samples * C_ONE
    table = doubling()
    parity = (iota((rows, BZ), 1) % 2).astype(f32)
    copies[2].wait()
    flat_weights[...] = jnp.concatenate([weights[o] for o in range(27)], axis=1)
    copies[0].wait()
    copies[1].wait()
    for x in range(HX):
        for y in range(HY):
            at = (x * HY + y) * LANES
            spots = place[:, 0, :, at : at + LANES].reshape(rows, LANES).astype(f32).astype(bf16)
            wide = jnp.dot(spots, table, preferred_element_type=f32) - parity
            for dx in range(2):
                for dy in range(2):
                    to = ((2 * x + dx) * BY + 2 * y + dy) * BZ
                    on = mask[:, 0, :, to : to + BZ].reshape(rows, BZ) == 1
                    hit = on & (wide == 4.0 * dx + 2.0 * dy)
                    chosen[:, to : to + BZ] = jnp.where(hit, 1.0, 0.0).astype(bf16)


def layer_two(samples, scale, vp_at, edge_at, *refs):
    blocks, (pooled, weights, expand, out, kept, sums, fields) = refs[:-7], refs[-7:]
    rows = samples * C_TWO
    parity_lane = iota((rows, LANES), 1)
    odd = iota((C_TWO, LANES), 1) % 2 == 1
    groups = {}
    for nx in OFFS:
        for ny in OFFS:
            key = (vp_at[nx, ny], edge_at[nx, ny, -1], edge_at[nx, ny, 1])
            groups.setdefault(key, []).append((nx, ny))
    for ((ref, at), low, high), places in groups.items():
        edge = blocks[low[0]][low[1] : low[1] + C_TWO].astype(f32)
        if low != high:
            other = blocks[high[0]][high[1] : high[1] + C_TWO].astype(f32)
            edge = jnp.where(odd, edge, other)
        parts = []
        for t in range(2):
            for s in range(samples):
                by = 8 * s + 4 * t
                parts.append(pltpu.roll(edge, LANES - by, 1) if by else edge)
        both = jnp.concatenate(
            [blocks[ref][at : at + 2 * rows], jnp.concatenate(parts, axis=0).astype(bf16)], axis=1
        )
        wide = jnp.dot(both, expand[...], preferred_element_type=f32)
        for i, oz in enumerate(OFFS):
            parity = ((parity_lane - oz) & 1).astype(f32)
            for qy in range(QY):
                lanes = slice((i * QY + qy) * LANES, (i * QY + qy + 1) * LANES)
                v = wide[0:rows, lanes].astype(bf16)
                p = (wide[rows : 2 * rows, lanes] - parity).astype(bf16)
                for x in range(HX):
                    for dy in range(2):
                        y = 2 * qy + dy
                        spots = []
                        for nx, ny in places:
                            near_x = nx == 0 or x == (HX - 1 if nx < 0 else 0)
                            near_y = ny == 0 or y == (HY - 1 if ny < 0 else 0)
                            if near_x and near_y:
                                spots.append((x + 1 + nx * HX) * (HY + 2) + y + 1 + ny * HY)
                        if not spots:
                            continue
                        cells = jnp.where(p == 4.0 * x + 2.0 * dy, v, jnp.zeros_like(v))
                        for spot in spots:
                            for s in range(samples):
                                fields[s, i * C_TWO : (i + 1) * C_TWO, spot * LANES : (spot + 1) * LANES] = (
                                    cells[s * C_TWO : (s + 1) * C_TWO]
                                )
    line = HY * HZ
    total = jnp.zeros((C_ONE, GRAD_W_TWO), f32)
    for s in range(samples):
        for x in range(HX):
            behind = []
            for ox in OFFS:
                for oy in OFFS:
                    at = ((x + 1 - ox) * (HY + 2) + 1 - oy) * LANES
                    behind.append(fields[s, :, at : at + line])
            behind = jnp.concatenate(behind, axis=0)
            got = jnp.dot(weights[...], behind, preferred_element_type=f32)
            got = got.astype(bf16)
            out[s, 0, :, x * line : (x + 1) * line] = got
            kept[s * C_ONE : (s + 1) * C_ONE, x * line : (x + 1) * line] = got
            total = total + lax.dot_general(
                pooled[s, 0, :, x * line : (x + 1) * line], behind, NT, preferred_element_type=f32
            )
    sums[:, 0:GRAD_W_TWO] = total * scale
    sums[:, GRAD_W_TWO:ONE_AT] = jnp.zeros((C_ONE, ONE_AT - GRAD_W_TWO), f32)


def layer_one(samples, scale, face_at, line_at, edge_at, *refs):
    blocks, (own, grad, chosen, before_sums, sums, conv_one, ahead) = refs[:-7], refs[-7:]
    used = samples * C_IN
    sums[:, 0:ONE_AT] = before_sums[...]
    lane = iota((PACK, BZ), 1)
    plane = BY * BZ
    for px in range(BX + 2):
        nx = -1 if px == 0 else 1 if px == BX + 1 else 0
        x = (px - 1) % BX
        for py in range(BY + 2):
            ny = -1 if py == 0 else 1 if py == BY + 1 else 0
            y = (py - 1) % BY
            if nx == 0 and ny == 0:
                row = own[:, (x * BY + y) * BZ : (x * BY + y + 1) * BZ].astype(f32)
            else:
                if ny == 0 or nx != 0:
                    ref, at = face_at[nx] if ny == 0 else line_at[nx, ny]
                    tile = 2 * min(y, BY - 1 - y)
                    chunk = 2 * (0 if x == 0 else 1) + (1 if y >= BY // 2 else 0)
                else:
                    ref, at = line_at[nx, ny]
                    tile = 2 * (0 if y == 0 else 1)
                    chunk = x
                halves = []
                for t in (tile, tile + 1):
                    four = blocks[ref][at + 4 * used * t : at + 4 * used * (t + 1)].astype(f32)
                    halves.append(four[chunk * used : (chunk + 1) * used])
                row = jnp.concatenate(halves, axis=1)
                if used < PACK:
                    row = jnp.concatenate([row, jnp.zeros((PACK - used, BZ), f32)], axis=0)
            ends = []
            for nz in (-1, 1):
                ref, at = edge_at[nx, ny, nz]
                ends.append(blocks[ref][at + C_TWO : at + EDGE].astype(f32))
            at = 2 * (x * BY + y)
            to = (px * (BY + 2) + py) * BZ
            before = jnp.where(lane == 0, ends[0][:, at + 1 : at + 2], pltpu.roll(row, 1, 1))
            after = jnp.where(lane == BZ - 1, ends[1][:, at : at + 1], pltpu.roll(row, BZ - 1, 1))
            for i, piece in enumerate((before, row, after)):
                ahead[i * PACK : (i + 1) * PACK, to : to + BZ] = piece.astype(bf16)
    table = doubling()
    line = HY * HZ
    for x in range(HX):
        for y in range(HY):
            at = x * line + y * LANES
            wide = jnp.dot(grad[:, at : at + LANES], table, preferred_element_type=f32).astype(bf16)
            for dx in range(2):
                for dy in range(2):
                    to = ((2 * x + dx) * BY + 2 * y + dy) * BZ
                    conv_one[:, to : to + BZ] = wide * chosen[:, to : to + BZ]
    rows = samples * C_ONE
    count = 27 * PACK
    product = jnp.zeros((rows, count), f32)
    for x in range(BX):
        pieces = []
        for ox in OFFS:
            for oy in OFFS:
                at = ((x + 1 + ox) * (BY + 2) + 1 + oy) * BZ
                pieces.append(ahead[:, at : at + plane])
        product = product + lax.dot_general(
            conv_one[:, x * plane : (x + 1) * plane],
            jnp.concatenate(pieces, axis=0),
            NT,
            preferred_element_type=f32,
        )
    sample_of = (iota((C_ONE, count), 1) % PACK) // C_IN
    folded = jnp.zeros((C_ONE, count), f32)
    for s in range(samples):
        folded = folded + jnp.where(sample_of == s, product[s * C_ONE : (s + 1) * C_ONE], 0.0)
    k = iota((count, LANES), 0)
    fold = ((k % C_IN) * STRIDE_ONE + k // PACK == iota((count, LANES), 1)).astype(f32)
    sums[:, ONE_AT:] = (
        jnp.dot(folded, fold, preferred_element_type=f32, precision=lax.Precision.HIGHEST) * scale
    )


def finish(mine, theirs, grad_one, grad_two):
    total = mine[...] + theirs[...]
    for o in range(27):
        grad_two[o] = total[:, o * C_TWO : (o + 1) * C_TWO]
    for c in range(C_IN):
        at = ONE_AT + c * STRIDE_ONE
        grad_one[c] = total[:, at : at + 27]


def call(body, shapes, operands, far=False, scratch=(), flops=0, moved=0):
    space = pltpu.HBM if far else pltpu.VMEM
    if far:
        scratch = [pltpu.VMEM(a.shape, a.dtype) for a in operands]
        scratch.append(pltpu.SemaphoreType.DMA((len(operands),)))
        operands = [pltpu.with_memory_space_constraint(a, pltpu.HBM) for a in operands]
    return pl.pallas_call(
        body,
        out_shape=shapes,
        in_specs=[pl.BlockSpec(memory_space=space)] * len(operands),
        out_specs=jax.tree.map(lambda _: pl.BlockSpec(memory_space=pltpu.VMEM), shapes),
        scratch_shapes=list(scratch),
        compiler_params=pltpu.CompilerParams(vmem_limit_bytes=32 * 2**20),
        cost_estimate=pl.CostEstimate(flops=flops, bytes_accessed=moved, transcendentals=0),
    )(*operands)


def block_side(blocks):
    return min(k for k in range(1, blocks + 1) if k * k * k >= blocks)


def neighbour(array, side, stride, of):
    blocks = lax.axis_size("space")
    pairs = []
    for i in range(blocks):
        c = i // stride % side
        pairs.append((i + ((c + of) % side - c) * stride, i))
    return lax.ppermute(array, "space", pairs)


def both_sides(array, side, stride):
    below = neighbour(array, side, stride, -1)
    return {-1: below, 1: below if side == 2 else neighbour(array, side, stride, 1)}


def swapped(array, axis, bit):
    size = lax.axis_size(axis)
    return lax.ppermute(array, axis, [(i, i ^ bit) for i in range(size)])


def stacked(parts):
    kept, starts, places = [], [], []
    rows = 0
    for part in parts:
        found = [i for i, a in enumerate(kept) if a is part]
        if not found:
            found = [len(kept)]
            kept.append(part)
            starts.append(rows)
            rows += part.shape[0]
        places.append(starts[found[0]])
    return jnp.concatenate(kept, axis=0), places


def operands_of(*tables):
    arrays, numbered = [], []
    for table in tables:
        new = {}
        for key, (array, row) in table.items():
            found = [i for i, a in enumerate(arrays) if a is array]
            if not found:
                found = [len(arrays)]
                arrays.append(array)
            new[key] = (found[0], row)
        numbered.append(new)
    return arrays, numbered


def local(inputs, mask_one, place_one, pooled_one, w_two, mask_two, place_two, grad_two):
    blocks = lax.axis_size("space")
    side = block_side(blocks)
    samples = inputs.shape[0]
    cells = inputs.shape[3]
    half_cells = HX * HY * HZ
    shape = jax.ShapeDtypeStruct
    vp_rows = 2 * samples * C_TWO
    four = 4 * samples * C_IN
    vp_row = BY * four
    to_x, to_y, own = call(
        functools.partial(prepare, samples),
        (
            shape((BY * four + vp_rows, LANES), bf16),
            shape((4 * four + vp_rows, LANES), bf16),
            shape((PACK, cells), bf16),
        ),
        (grad_two, place_two, mask_two, inputs),
        far=True,
        flops=2 * 10**7,
        moved=2**20,
    )
    edge = call(
        functools.partial(ends, samples, vp_row),
        shape((EDGE, LANES), bf16),
        (to_x, own),
        flops=10**7,
        moved=2**19,
    )
    chosen, flat_weights, expand = call(
        functools.partial(select_one, samples),
        (
            shape((samples * C_ONE, cells), bf16),
            shape((C_ONE, 27 * C_TWO), bf16),
            shape((2 * LANES, TABLE), bf16),
        ),
        (place_one, mask_one, w_two),
        far=True,
        flops=2 * 10**7,
        moved=3 * 2**20,
    )
    vp_at, edge_at, face_at, line_at = {(0, 0): (to_x, vp_row)}, {}, {}, {}
    from_x = both_sides(to_x, side, side * side)
    edge_z = both_sides(edge, side, 1)
    edge_x = {-1: both_sides(edge_z[-1], side, side * side)}
    edge_x[1] = edge_x[-1] if side == 2 else both_sides(edge_z[1], side, side * side)
    first = both_sides(to_y, side, side)
    parts = []
    for n in (-1, 1):
        again = n == 1 and side == 2
        parts += parts[:2] if again else [from_x[n][vp_row:], from_x[n][: 2 * four]]
    parts += [edge_z[-1], edge_z[1]] + [edge_x[nz][nx] for nz in (-1, 1) for nx in (-1, 1)]
    second, starts = stacked(parts)
    second = both_sides(second, side, side)
    for n in (-1, 1):
        vp_at[n, 0] = (from_x[n], vp_row)
        face_at[n] = (from_x[n], 0)
        vp_at[0, n] = (first[n], 4 * four)
        line_at[0, n] = (first[n], 0)
        edge_at[0, 0, n] = (edge_z[n], 0)
        for i, nx in enumerate((-1, 1)):
            edge_at[nx, 0, n] = (edge_x[n][nx], 0)
            vp_at[nx, n] = (second[n], starts[2 * i])
            line_at[nx, n] = (second[n], starts[2 * i + 1])
        for i, nz in enumerate((-1, 1)):
            edge_at[0, n, nz] = (second[n], starts[4 + i])
            for j, nx in enumerate((-1, 1)):
                edge_at[nx, n, nz] = (second[n], starts[6 + 2 * i + j])
    total = lax.axis_size("dp") * samples * blocks * cells
    arrays, tables = operands_of(vp_at, edge_at)
    grad_pooled, kept, sums = call(
        functools.partial(layer_two, samples, float(total // 8) ** -0.5, *tables),
        (
            shape((samples, 1, C_ONE, half_cells), bf16),
            shape((samples * C_ONE, half_cells), bf16),
            shape((C_ONE, ONE_AT), f32),
        ),
        (*arrays, pooled_one, flat_weights, expand),
        scratch=(pltpu.VMEM((samples, 3 * C_TWO, (HX + 2) * (HY + 2) * HZ), bf16),),
        flops=5 * 10**8,
        moved=2**20,
    )
    arrays, tables = operands_of(face_at, line_at, edge_at)
    sums = call(
        functools.partial(layer_one, samples, float(total) ** -0.5, *tables),
        shape((C_ONE, WIDTH), f32),
        (*arrays, own, kept, chosen, sums),
        scratch=(
            pltpu.VMEM((samples * C_ONE, cells), bf16),
            pltpu.VMEM((3 * PACK, (BX + 2) * (BY + 2) * BZ), bf16),
        ),
        flops=5 * 10**8,
        moved=2**20,
    )
    steps = []
    for axis in ("dp", "space"):
        bit = 1
        while bit < lax.axis_size(axis):
            steps.append((axis, bit))
            bit *= 2
    for axis, bit in steps[:-1]:
        sums = sums + swapped(sums, axis, bit)
    grad_w_one, grad_w_two = call(
        finish,
        (shape((C_IN, C_ONE, 27), f32), shape((27, C_ONE, C_TWO), f32)),
        (sums, swapped(sums, *steps[-1])),
    )
    return grad_pooled, jnp.transpose(grad_w_one, (2, 0, 1)), grad_w_two


def solution(mesh):
    split = P("dp", "space", None, None)
    return jax.shard_map(
        local,
        mesh=mesh,
        in_specs=(split, split, split, split, P(), split, split, split),
        out_specs=(split, P(), P()),
        check_vma=False,
    )
```

time: 59.3 us -> 45.8 us (0.77)
  starting transfers between devices: 28.4 us -> 15.2 us
  local copies, waits for them, and re-layouts: 7.39 us -> 0.01 us
  waiting for transfers between devices: 12.4 us -> 19.5 us
    ppermute x11 -> x5, starting transfers between devices: 19.4 us -> 9.08 us  [neighbour(): return lax.ppermute(array, 'space', pairs)]
    unnamed x17 -> x2, local copies, waits for them, and re-layouts: 7.39 us -> 0.01 us
    ppermute x11 -> x5, waiting for transfers between devices: 0.37 us -> 6.13 us  [neighbour(): return lax.ppermute(array, 'space', pairs)]
    ppermute x5, starting transfers between devices: 9.08 us -> 6.14 us  [swapped(): return lax.ppermute(array, axis, [(i, i ^ bit) for i in range(size)])]
    ppermute x5, waiting for transfers between devices: 12 us -> 13.4 us  [swapped(): return lax.ppermute(array, axis, [(i, i ^ bit) for i in range(size)])]
    pallas_call x4 -> x6, Pallas kernels: 9.91 us -> 10.2 us  [call(): pl.pallas_call(body, out_shape=shapes, in_specs=[pl.BlockSpec(memory_spac...]
  transfers between devices with their start and end apart: 16 -> 10, of which waited for: 6 -> 9; matrix products, arithmetic and copies ran while one was open for 0% -> 0% of each run, Pallas kernels for 1% -> 5%
where the time goes in v1:
time: 45.8 us; the launch traced here: 45.7 us
  waiting for transfers between devices  19.5 us (43%)
  starting transfers between devices  15.2 us (33%)
  Pallas kernels  10.2 us (22%)
  between operations  0.7 us (2%)
    ppermute x5, waiting for transfers between devices, swapped(): return lax.ppermute(array, axis, [(i, i ^ bit) for i in range(size)])  13.4 us
    pallas_call x6, Pallas kernels, call(): pl.pallas_call(body, out_shape=shapes, in_specs=[pl.BlockSpec(memory_spac...  10.2 us
    ppermute x5, starting transfers between devices, neighbour(): return lax.ppermute(array, 'space', pairs)  9.08 us
    ppermute x5, starting transfers between devices, swapped(): return lax.ppermute(array, axis, [(i, i ^ bit) for i in range(size)])  6.14 us
    ppermute x5, waiting for transfers between devices, neighbour(): return lax.ppermute(array, 'space', pairs)  6.13 us
  transfers between devices with their start and end apart: 10, of which 9 were waited for; matrix products, arithmetic and copies ran while one was open for 0% of the time, Pallas kernels for 5%

profile of v1, /device:TPU:0, one launch (start us, length us, event | category | flops | bytes accessed | tf_op | source)
XLA Modules:
  0.0 45.7 jit_solution(12710093713442030470)
XLA Ops:
  0.6 0.0 copy-start
  0.6 1.4 %shard_map.103 = (bf16[576,128]{1,0:T(8,128)(2,1)S(1)}, bf16[384,128]{1,0:T(8,128)(2,1)S(1)}, bf16[16,8192]{1,0:T(8,128)(2,1)S(1)}) custom-call(bf16[3,1,32,128]{3,2,1,0:T(8,128)(2,1)} %refs_0_.2, s32[3,1,32,128]{3,2,1,0:T(8,128)} %refs_1_.2, s32[3,1,32,1024]{3,2,1,0:T(8,128)} %refs_2_.2, bf16[3,1,4,8192]{3,2,1,0:T(4,128)(2,1)} %refs_3_.1), custom_call_target="tpu_custom_call" | custom-call | flops 20000000 | bytes 1048576 | tf_op jit(solution)/shard_map/pallas_call | solution.py:310
  2.0 4.1 %collective-permute-start = (bf16[576,128]{1,0:T(8,128)(2,1)S(1)}, bf16[576,128]{1,0:T(8,128)(2,1)S(1)}, u32[]{:S(2)}, u32[]{:S(2)}) collective-permute-start(bf16[576,128]{1,0:T(8,128)(2,1)S(1)} %get-tuple-element.14.to_x.refs_0_), channel_id=1, source_target_pairs={{4,0},{5,1},{6,2},{7,3},{0,4},{1,5},{2,6},{3,7},{12,8},{13,9},{14,... | collective-permute-start | bytes 442376 | tf_op jit(solution)/shard_map/ppermute | solution.py:331
  6.1 0.2 shard_map.104
  6.3 1.5 %collective-permute-start.2 = (bf16[48,128]{1,0:T(8,128)(2,1)S(1)}, bf16[48,128]{1,0:T(8,128)(2,1)S(1)}, u32[]{:S(2)}, u32[]{:S(2)}) collective-permute-start(bf16[48,128]{1,0:T(8,128)(2,1)S(1)} %shard_map.104), channel_id=1, source_target_pairs={{1,0},{0,1},{3,2},{2,3},{5,4},{4,5},{7,6},{6,7},{9,8},{8,9},{11,10... | collective-permute-start | bytes 36872 | tf_op jit(solution)/shard_map/ppermute | solution.py:331
  7.8 2.2 %collective-permute-done.2.refs_4_.refs_3_ = bf16[48,128]{1,0:T(8,128)(2,1)S(1)} collective-permute-done((bf16[48,128]{1,0:T(8,128)(2,1)S(1)}, bf16[48,128]{1,0:T(8,128)(2,1)S(1)}, u32[]{:S(2)}, u32[]{:S(2)}) %collective-permute-start.2) | collective-permute-done | bytes 12320 | tf_op jit(solution)/shard_map/ppermute | solution.py:331
  10.0 0.0 collective-permute-start.3
  10.1 1.9 %collective-permute-start.1 = (bf16[384,128]{1,0:T(8,128)(2,1)S(1)}, bf16[384,128]{1,0:T(8,128)(2,1)S(1)}, u32[]{:S(2)}, u32[]{:S(2)}) collective-permute-start(bf16[384,128]{1,0:T(8,128)(2,1)S(1)} %get-tuple-element.15), channel_id=1, source_target_pairs={{2,0},{3,1},{0,2},{1,3},{6,4},{7,5},{4,6},{5,7},{10,8},{11,9},{8,1... | collective-permute-start | bytes 294920 | tf_op jit(solution)/shard_map/ppermute | solution.py:331
  11.9 1.4 %collective-permute-done.refs_1_.refs_0_ = bf16[576,128]{1,0:T(8,128)(2,1)S(1)} collective-permute-done((bf16[576,128]{1,0:T(8,128)(2,1)S(1)}, bf16[576,128]{1,0:T(8,128)(2,1)S(1)}, u32[]{:S(2)}, u32[]{:S(2)}) %collective-permute-start) | collective-permute-done | bytes 147488 | tf_op jit(solution)/shard_map/ppermute | solution.py:331
  13.4 1.3 %collective-permute-done.3.refs_5_.refs_4_ = bf16[48,128]{1,0:T(8,128)(2,1)S(1)} collective-permute-done((bf16[48,128]{1,0:T(8,128)(2,1)S(1)}, bf16[48,128]{1,0:T(8,128)(2,1)S(1)}, u32[]{:S(2)}, u32[]{:S(2)}) %collective-permute-start.3) | collective-permute-done | bytes 12320 | tf_op jit(solution)/shard_map/ppermute | solution.py:331
  14.7 1.5 %collective-permute-start.4 = (bf16[384,128]{1,0:T(8,128)(2,1)S(1)}, bf16[384,128]{1,0:T(8,128)(2,1)S(1)}, u32[]{:S(2)}, u32[]{:S(2)}) collective-permute-start(bf16[384,128]{1,0:T(8,128)(2,1)S(1)} %pad_maximum_fusion), channel_id=1, source_target_pairs={{2,0},{3,1},{0,2},{1,3},{6,4},{7,5},{4,6},{5,7},{10,8},{11,9},{8,1... | collective-permute-start | bytes 294920 | tf_op jit(solution)/shard_map/ppermute | solution.py:331
  16.3 2.0 %shard_map.105 = (bf16[48,8192]{1,0:T(8,128)(2,1)S(1)}, bf16[16,864]{1,0:T(8,128)(2,1)S(1)}, bf16[256,768]{1,0:T(8,128)(2,1)S(1)}) custom-call(s32[3,1,16,1024]{3,2,1,0:T(8,128)} %refs_0_.3, s32[3,1,16,8192]{3,2,1,0:T(8,128)} %refs_1_.3, bf16[27,16,32]{2,1,0:T(8,128)(2,1)} %refs_2_.3), custom_call_target="tpu_custom_call" | custom-call | flops 20000000 | bytes 3145728 | tf_op jit(solution)/shard_map/pallas_call | solution.py:310
  18.3 0.0 collective-permute-done.1.refs_2_.refs_1_
  18.3 1.2 %collective-permute-done.4.refs_3_.refs_2_ = bf16[384,128]{1,0:T(8,128)(2,1)S(1)} collective-permute-done((bf16[384,128]{1,0:T(8,128)(2,1)S(1)}, bf16[384,128]{1,0:T(8,128)(2,1)S(1)}, u32[]{:S(2)}, u32[]{:S(2)}) %collective-permute-start.4) | collective-permute-done | bytes 98336 | tf_op jit(solution)/shard_map/ppermute | solution.py:331
  19.4 0.0 copy-done
  19.4 3.2 %shard_map.106 = (bf16[3,1,16,1024]{3,2,1,0:T(8,128)(2,1)}, bf16[48,1024]{1,0:T(8,128)(2,1)S(1)}, f32[16,896]{1,0:T(8,128)S(1)}) custom-call(bf16[576,128]{1,0:T(8,128)(2,1)S(1)} %get-tuple-element.14.to_x.refs_0_, bf16[576,128]{1,0:T(8,128)(2,1)S(1)} %collective-permute-done.refs_1_.refs_0_, bf16[384,128]{1,0:T(8,128)(2,1)S(1)} %collective-permute-done.1.refs_2_.refs_1_, ...), custom_call_target="tpu_custom_call" | custom-call | flops 500000000 | bytes 1048576 | tf_op jit(solution)/shard_map/pallas_call | solution.py:310
  22.7 2.6 %shard_map.107 = f32[16,1024]{1,0:T(8,128)S(1)} custom-call(bf16[576,128]{1,0:T(8,128)(2,1)S(1)} %collective-permute-done.refs_1_.refs_0_, bf16[384,128]{1,0:T(8,128)(2,1)S(1)} %collective-permute-done.1.refs_2_.refs_1_, bf16[384,128]{1,0:T(8,128)(2,1)S(1)} %collective-permute-done.4.refs_3_.refs_2_, ...), custom_call_target="tpu_custom_call" | custom-call | flops 500000000 | bytes 1048576 | tf_op jit(solution)/shard_map/pallas_call | solution.py:310
  25.3 0.0 collective-permute-start.5
  25.3 1.3 %collective-permute-done.5 = f32[16,1024]{1,0:T(8,128)S(1)} collective-permute-done((f32[16,1024]{1,0:T(8,128)S(1)}, f32[16,1024]{1,0:T(8,128)S(1)}, u32[]{:S(2)}, u32[]{:S(2)}) %collective-permute-start.5) | collective-permute-done | bytes 65568 | tf_op jit(solution)/shard_map/ppermute | solution.py:341
  26.6 1.6 %collective-permute-start.6 = (f32[16,1024]{1,0:T(8,128)S(1)}, f32[16,1024]{1,0:T(8,128)S(1)}, u32[]{:S(2)}, u32[]{:S(2)}) collective-permute-start(f32[16,1024]{1,0:T(8,128)S(1)} %add.12), channel_id=1, source_target_pairs={{0,16},{8,24},{16,0},{24,8},{1,17},{9,25},{17,1},{25,9},{2,18},{10... | collective-permute-start | bytes 196616 | tf_op jit(solution)/shard_map/ppermute | solution.py:341
  28.2 2.7 %collective-permute-done.6 = f32[16,1024]{1,0:T(8,128)S(1)} collective-permute-done((f32[16,1024]{1,0:T(8,128)S(1)}, f32[16,1024]{1,0:T(8,128)S(1)}, u32[]{:S(2)}, u32[]{:S(2)}) %collective-permute-start.6) | collective-permute-done | bytes 65568 | tf_op jit(solution)/shard_map/ppermute | solution.py:341
  31.0 1.6 %collective-permute-start.7 = (f32[16,1024]{1,0:T(8,128)S(1)}, f32[16,1024]{1,0:T(8,128)S(1)}, u32[]{:S(2)}, u32[]{:S(2)}) collective-permute-start(f32[16,1024]{1,0:T(8,128)S(1)} %add.13), channel_id=1, source_target_pairs={{0,1},{1,0},{2,3},{3,2},{4,5},{5,4},{6,7},{7,6},{8,9},{9,8},{10,11... | collective-permute-start | bytes 196616 | tf_op jit(solution)/shard_map/ppermute | solution.py:341
  32.5 2.8 %collective-permute-done.7 = f32[16,1024]{1,0:T(8,128)S(1)} collective-permute-done((f32[16,1024]{1,0:T(8,128)S(1)}, f32[16,1024]{1,0:T(8,128)S(1)}, u32[]{:S(2)}, u32[]{:S(2)}) %collective-permute-start.7) | collective-permute-done | bytes 65568 | tf_op jit(solution)/shard_map/ppermute | solution.py:341
  35.3 1.5 %collective-permute-start.8 = (f32[16,1024]{1,0:T(8,128)S(1)}, f32[16,1024]{1,0:T(8,128)S(1)}, u32[]{:S(2)}, u32[]{:S(2)}) collective-permute-start(f32[16,1024]{1,0:T(8,128)S(1)} %add.14), channel_id=1, source_target_pairs={{0,2},{1,3},{2,0},{3,1},{4,6},{5,7},{6,4},{7,5},{8,10},{9,11},{10,... | collective-permute-start | bytes 196616 | tf_op jit(solution)/shard_map/ppermute | solution.py:341
  36.8 2.8 %collective-permute-done.8 = f32[16,1024]{1,0:T(8,128)S(1)} collective-permute-done((f32[16,1024]{1,0:T(8,128)S(1)}, f32[16,1024]{1,0:T(8,128)S(1)}, u32[]{:S(2)}, u32[]{:S(2)}) %collective-permute-start.8) | collective-permute-done | bytes 65568 | tf_op jit(solution)/shard_map/ppermute | solution.py:341
  39.6 1.5 %collective-permute-start.9 = (f32[16,1024]{1,0:T(8,128)S(1)}, f32[16,1024]{1,0:T(8,128)S(1)}, u32[]{:S(2)}, u32[]{:S(2)}) collective-permute-start(f32[16,1024]{1,0:T(8,128)S(1)} %add.15.mine), channel_id=1, source_target_pairs={{0,4},{1,5},{2,6},{3,7},{4,0},{5,1},{6,2},{7,3},{8,12},{9,13},{10,... | collective-permute-start | bytes 196616 | tf_op jit(solution)/shard_map/ppermute | solution.py:341
  41.1 3.8 %collective-permute-done.9.theirs = f32[16,1024]{1,0:T(8,128)S(1)} collective-permute-done((f32[16,1024]{1,0:T(8,128)S(1)}, f32[16,1024]{1,0:T(8,128)S(1)}, u32[]{:S(2)}, u32[]{:S(2)}) %collective-permute-start.9) | collective-permute-done | bytes 65568 | tf_op jit(solution)/shard_map/ppermute | solution.py:341
  44.9 0.8 %shard_map.108 = (f32[4,16,27]{2,1,0:T(8,128)}, f32[27,16,32]{2,1,0:T(8,128)}) custom-call(f32[16,1024]{1,0:T(8,128)S(1)} %add.15.mine, f32[16,1024]{1,0:T(8,128)S(1)} %collective-permute-done.9.theirs), custom_call_target="tpu_custom_call" | custom-call | tf_op jit(solution)/shard_map/pallas_call | solution.py:310
  (7 shorter events, 0.1 us)
Async XLA Ops:
  0.6 18.8 %copy-start = (bf16[3,1,16,1024]{3,2,1,0:T(8,128)(2,1)S(1)}, bf16[3,1,16,1024]{3,2,1,0:T(8,128)(2,1)}, u32[]{:S(2)}) copy-start(bf16[3,1,16,1024]{3,2,1,0:T(8,128)(2,1)} %refs_6_.1) | copy-start | bytes 294916
  2.0 11.4 %collective-permute-start = (bf16[576,128]{1,0:T(8,128)(2,1)S(1)}, bf16[576,128]{1,0:T(8,128)(2,1)S(1)}, u32[]{:S(2)}, u32[]{:S(2)}) collective-permute-start(bf16[576,128]{1,0:T(8,128)(2,1)S(1)} %get-tuple-element.14.to_x.refs_0_), channel_id=1, source_target_pairs={{4,0},{5,1},{6,2},{7,3},{0,4},{1,5},{2,6},{3,7},{12,8},{13,9},{14,... | collective-permute-start | bytes 442376 | tf_op jit(solution)/shard_map/ppermute | solution.py:331
  6.3 3.7 %collective-permute-start.2 = (bf16[48,128]{1,0:T(8,128)(2,1)S(1)}, bf16[48,128]{1,0:T(8,128)(2,1)S(1)}, u32[]{:S(2)}, u32[]{:S(2)}) collective-permute-start(bf16[48,128]{1,0:T(8,128)(2,1)S(1)} %shard_map.104), channel_id=1, source_target_pairs={{1,0},{0,1},{3,2},{2,3},{5,4},{4,5},{7,6},{6,7},{9,8},{8,9},{11,10... | collective-permute-start | bytes 36872 | tf_op jit(solution)/shard_map/ppermute | solution.py:331
  10.0 4.7 %collective-permute-start.3 = (bf16[48,128]{1,0:T(8,128)(2,1)S(1)}, bf16[48,128]{1,0:T(8,128)(2,1)S(1)}, u32[]{:S(2)}, u32[]{:S(2)}) collective-permute-start(bf16[48,128]{1,0:T(8,128)(2,1)S(1)} %collective-permute-done.2.refs_4_.refs_3_), channel_id=1, source_target_pairs={{4,0},{5,1},{6,2},{7,3},{0,4},{1,5},{2,6},{3,7},{12,8},{13,9},{14,... | collective-permute-start | bytes 36872 | tf_op jit(solution)/shard_map/ppermute | solution.py:331
  10.1 8.2 %collective-permute-start.1 = (bf16[384,128]{1,0:T(8,128)(2,1)S(1)}, bf16[384,128]{1,0:T(8,128)(2,1)S(1)}, u32[]{:S(2)}, u32[]{:S(2)}) collective-permute-start(bf16[384,128]{1,0:T(8,128)(2,1)S(1)} %get-tuple-element.15), channel_id=1, source_target_pairs={{2,0},{3,1},{0,2},{1,3},{6,4},{7,5},{4,6},{5,7},{10,8},{11,9},{8,1... | collective-permute-start | bytes 294920 | tf_op jit(solution)/shard_map/ppermute | solution.py:331
  14.7 4.7 %collective-permute-start.4 = (bf16[384,128]{1,0:T(8,128)(2,1)S(1)}, bf16[384,128]{1,0:T(8,128)(2,1)S(1)}, u32[]{:S(2)}, u32[]{:S(2)}) collective-permute-start(bf16[384,128]{1,0:T(8,128)(2,1)S(1)} %pad_maximum_fusion), channel_id=1, source_target_pairs={{2,0},{3,1},{0,2},{1,3},{6,4},{7,5},{4,6},{5,7},{10,8},{11,9},{8,1... | collective-permute-start | bytes 294920 | tf_op jit(solution)/shard_map/ppermute | solution.py:331
  25.3 1.3 %collective-permute-start.5 = (f32[16,1024]{1,0:T(8,128)S(1)}, f32[16,1024]{1,0:T(8,128)S(1)}, u32[]{:S(2)}, u32[]{:S(2)}) collective-permute-start(f32[16,1024]{1,0:T(8,128)S(1)} %shard_map.107), channel_id=1, source_target_pairs={{0,8},{8,0},{16,24},{24,16},{1,9},{9,1},{17,25},{25,17},{2,10},{10... | collective-permute-start | bytes 196616 | tf_op jit(solution)/shard_map/ppermute | solution.py:341
  26.6 4.3 %collective-permute-start.6 = (f32[16,1024]{1,0:T(8,128)S(1)}, f32[16,1024]{1,0:T(8,128)S(1)}, u32[]{:S(2)}, u32[]{:S(2)}) collective-permute-start(f32[16,1024]{1,0:T(8,128)S(1)} %add.12), channel_id=1, source_target_pairs={{0,16},{8,24},{16,0},{24,8},{1,17},{9,25},{17,1},{25,9},{2,18},{10... | collective-permute-start | bytes 196616 | tf_op jit(solution)/shard_map/ppermute | solution.py:341
  31.0 4.3 %collective-permute-start.7 = (f32[16,1024]{1,0:T(8,128)S(1)}, f32[16,1024]{1,0:T(8,128)S(1)}, u32[]{:S(2)}, u32[]{:S(2)}) collective-permute-start(f32[16,1024]{1,0:T(8,128)S(1)} %add.13), channel_id=1, source_target_pairs={{0,1},{1,0},{2,3},{3,2},{4,5},{5,4},{6,7},{7,6},{8,9},{9,8},{10,11... | collective-permute-start | bytes 196616 | tf_op jit(solution)/shard_map/ppermute | solution.py:341
  35.3 4.3 %collective-permute-start.8 = (f32[16,1024]{1,0:T(8,128)S(1)}, f32[16,1024]{1,0:T(8,128)S(1)}, u32[]{:S(2)}, u32[]{:S(2)}) collective-permute-start(f32[16,1024]{1,0:T(8,128)S(1)} %add.14), channel_id=1, source_target_pairs={{0,2},{1,3},{2,0},{3,1},{4,6},{5,7},{6,4},{7,5},{8,10},{9,11},{10,... | collective-permute-start | bytes 196616 | tf_op jit(solution)/shard_map/ppermute | solution.py:341
  39.6 5.2 %collective-permute-start.9 = (f32[16,1024]{1,0:T(8,128)S(1)}, f32[16,1024]{1,0:T(8,128)S(1)}, u32[]{:S(2)}, u32[]{:S(2)}) collective-permute-start(f32[16,1024]{1,0:T(8,128)S(1)} %add.15.mine), channel_id=1, source_target_pairs={{0,4},{1,5},{2,6},{3,7},{4,0},{5,1},{6,2},{7,3},{8,12},{9,13},{10,... | collective-permute-start | bytes 196616 | tf_op jit(solution)/shard_map/ppermute | solution.py:341

commit v2 on v1

v2 whole, which is shorter than its diff:
```python
import functools

import jax
import jax.numpy as jnp
from jax import lax
from jax.experimental import pallas as pl
from jax.experimental.pallas import tpu as pltpu
from jax.sharding import PartitionSpec as P

C_IN = 4
C_ONE = 16
C_TWO = 32
BX = 4
BY = 8
BZ = 256
HX, HY, HZ = BX // 2, BY // 2, BZ // 2
QY, QZ = HY // 2, HZ // 2
LANES = 128
PACK = 16
EDGE = C_TWO + PACK
OFFS = (-1, 0, 1)
GRAD_W_TWO = 27 * C_TWO
WIDTH = 1024
ONE_AT = WIDTH - LANES
STRIDE_ONE = LANES // C_IN
TABLE = 3 * QY * LANES
NT = (((1,), (1,)), ((), ()))
f32, bf16, i32 = jnp.float32, jnp.bfloat16, jnp.int32


def iota(shape, dim):
    return lax.broadcasted_iota(i32, shape, dim)


def doubling():
    return (iota((LANES, 2 * LANES), 0) == iota((LANES, 2 * LANES), 1) // 2).astype(bf16)


def fetch(pairs, sems):
    copies = [pltpu.make_async_copy(a, b, sems.at[i]) for i, (a, b) in enumerate(pairs)]
    for copy in copies:
        copy.start()
    return copies


def prepare(samples, *refs):
    far, (to_x, own), near, sems = refs[:4], refs[4:6], refs[6:10], refs[10]
    grad, place, mask, source = near
    copies = fetch(tuple(zip(far, near)), sems)
    rows = samples * C_TWO
    table = doubling()
    copies[0].wait()
    copies[1].wait()
    values = jnp.dot(grad[...].reshape(rows, LANES), table, preferred_element_type=f32)
    spots = place[...].reshape(rows, LANES).astype(f32).astype(bf16)
    wide = jnp.dot(spots, table, preferred_element_type=f32)
    parity = (iota((rows, LANES), 1) % 2).astype(f32)
    copies[2].wait()
    halves = []
    for qy in range(QY):
        v = values[:, qy * LANES : (qy + 1) * LANES]
        p = wide[:, qy * LANES : (qy + 1) * LANES] - parity
        total = jnp.zeros((rows, LANES), f32)
        for x in range(HX):
            for dy in range(2):
                at = (x * HY + 2 * qy + dy) * LANES
                on = mask[:, 0, :, at : at + LANES].reshape(rows, LANES) == 1
                total = total + jnp.where(on & (p == 4.0 * x + 2.0 * dy), v, 0.0)
        halves.append(total)
    kept = jnp.concatenate(halves, axis=1).astype(bf16)
    v = lax.dot_general(kept, table, NT, preferred_element_type=f32).astype(bf16)
    used = samples * C_IN
    at = BY * 4 * used
    to_x[at : at + rows] = v
    to_x[at + rows : at + 2 * rows] = spots
    copies[3].wait()
    pieces = [source[s, 0].astype(f32) for s in range(samples)]
    if used < PACK:
        pieces.append(jnp.zeros((PACK - used, BX * BY * BZ), f32))
    cells = jnp.concatenate(pieces, axis=0)
    own[...] = cells.astype(bf16)
    for t in range(BY):
        group = []
        for x in (0, BX - 1):
            for y in (t // 2, BY - 1 - t // 2):
                at = (x * BY + y) * BZ + (t % 2) * LANES
                group.append(cells[0:used, at : at + LANES])
        to_x[4 * used * t : 4 * used * (t + 1)] = jnp.concatenate(group, axis=0).astype(bf16)


def ends(samples, vp_row, to_x, own, edge):
    rows = samples * C_TWO
    lane = iota((LANES, LANES), 0)
    spot = (lane // QZ) * 2 + (lane % QZ == QZ - 1).astype(i32)
    spot = jnp.where((lane % QZ == 0) | (lane % QZ == QZ - 1), spot, -LANES)
    column = iota((LANES, LANES), 1)
    packed = jnp.zeros((C_TWO, LANES), f32)
    for s in range(samples):
        for t in range(2):
            pick = (spot + (8 * s + 4 * t) == column).astype(bf16)
            at = vp_row + t * rows + s * C_TWO
            packed = packed + jnp.dot(to_x[at : at + C_TWO], pick, preferred_element_type=f32)
    edge[0:C_TWO] = packed.astype(bf16)
    lane = iota((PACK, LANES), 1)
    packed = jnp.zeros((PACK, LANES), f32)
    for row in range(BX * BY):
        left = own[:, row * BZ : row * BZ + LANES].astype(f32)
        right = own[:, (row + 1) * BZ - LANES : (row + 1) * BZ].astype(f32)
        packed = jnp.where(lane == 2 * row, left[:, 0:1], packed)
        packed = jnp.where(lane == 2 * row + 1, right[:, LANES - 1 :], packed)
    edge[C_TWO:EDGE] = packed.astype(bf16)


def select_one(samples, vp_row, *refs):
    far, (to_x, own), (chosen, folded_weights, expand, to_y), near, sems = (
        refs[:3], refs[3:5], refs[5:9], refs[9:12], refs[12],
    )
    place, mask, weights = near
    copies = fetch(tuple(zip(far, near)), sems)
    used = samples * C_IN
    to_y[4 * 4 * used :] = to_x[vp_row:]
    for t in range(4):
        group = []
        for x in range(BX):
            at = (x * BY + (BY - 1) * (t // 2)) * BZ + (t % 2) * LANES
            group.append(own[:, at : at + LANES].astype(f32)[0:used])
        to_y[4 * used * t : 4 * used * (t + 1)] = jnp.concatenate(group, axis=0).astype(bf16)
    k = iota((2 * LANES, TABLE), 0)
    j = iota((1, TABLE), 1)
    shift = j // (QY * LANES) - 1
    qy = (j // LANES) % QY
    z = j % LANES - shift
    beyond = LANES + qy * 2 + (z < 0).astype(i32)
    expand[...] = (k == jnp.where((z >= 0) & (z < LANES), qy * QZ + z // 2, beyond)).astype(bf16)
    rows = samples * C_ONE
    table = doubling()
    parity = (iota((rows, BZ), 1) % 2).astype(f32)
    copies[2].wait()
    folded_weights[...] = jnp.concatenate(
        [jnp.concatenate([weights[3 * o + i] for i in range(3)], axis=1) for o in range(9)], axis=0
    )
    copies[0].wait()
    copies[1].wait()
    for x in range(HX):
        for y in range(HY):
            at = (x * HY + y) * LANES
            spots = place[:, 0, :, at : at + LANES].reshape(rows, LANES).astype(f32).astype(bf16)
            wide = jnp.dot(spots, table, preferred_element_type=f32) - parity
            for dx in range(2):
                for dy in range(2):
                    to = ((2 * x + dx) * BY + 2 * y + dy) * BZ
                    on = mask[:, 0, :, to : to + BZ].reshape(rows, BZ) == 1
                    hit = on & (wide == 4.0 * dx + 2.0 * dy)
                    chosen[:, to : to + BZ] = jnp.where(hit, 1.0, 0.0).astype(bf16)


def expand_windows(samples, vp_at, edge_at, ys, tile_of, blocks, expand, fields):
    rows = samples * C_TWO
    lane = iota((rows, LANES), 1)
    odd = iota((C_TWO, LANES), 1) % 2 == 1
    groups = {}
    for nx in OFFS:
        for ny in ys:
            key = (vp_at[nx, ny], edge_at[nx, ny, -1], edge_at[nx, ny, 1])
            groups.setdefault(key, []).append((nx, ny))
    for ((ref, at), low, high), places in groups.items():
        edge = blocks[low[0]][low[1] : low[1] + C_TWO].astype(f32)
        if low != high:
            other = blocks[high[0]][high[1] : high[1] + C_TWO].astype(f32)
            edge = jnp.where(odd, edge, other)
        parts = []
        for t in range(2):
            for s in range(samples):
                by = 8 * s + 4 * t
                parts.append(pltpu.roll(edge, LANES - by, 1) if by else edge)
        both = jnp.concatenate(
            [blocks[ref][at : at + 2 * rows], jnp.concatenate(parts, axis=0).astype(bf16)], axis=1
        )
        wide = jnp.dot(both, expand[...], preferred_element_type=f32)
        for i, oz in enumerate(OFFS):
            parity = ((lane - oz) & 1).astype(f32)
            for qy in range(QY):
                lanes = slice((i * QY + qy) * LANES, (i * QY + qy + 1) * LANES)
                v = wide[0:rows, lanes].astype(bf16)
                p = (wide[rows : 2 * rows, lanes] - parity).astype(bf16)
                for x in range(HX):
                    for dy in range(2):
                        y = 2 * qy + dy
                        spots = []
                        for nx, ny in places:
                            near_x = nx == 0 or x == (HX - 1 if nx < 0 else 0)
                            near_y = ny == 0 or y == (HY - 1 if ny < 0 else 0)
                            if near_x and near_y:
                                spots.append(tile_of[x + 1 + nx * HX, y + 1 + ny * HY])
                        if not spots:
                            continue
                        cells = jnp.where(p == 4.0 * x + 2.0 * dy, v, jnp.zeros_like(v))
                        for spot in spots:
                            for s in range(samples):
                                fields[s, i * C_TWO : (i + 1) * C_TWO, spot * LANES : (spot + 1) * LANES] = (
                                    cells[s * C_TWO : (s + 1) * C_TWO]
                                )


def tiles_inside():
    return {(px, py): px * HY + py - 1 for px in range(HX + 2) for py in range(1, HY + 1)}


def tiles_ends():
    return {(px, py): 2 * px + (py > 0) for px in range(HX + 2) for py in (0, HY + 1)}


def shift_pooled(samples, tile_of, pooled, moved):
    for (px, py), tile in tile_of.items():
        k = 0
        for ox in OFFS:
            for oy in OFFS:
                x, y = px - 1 + ox, py - 1 + oy
                inside = 0 <= x < HX and 0 <= y < HY
                for s in range(samples):
                    if inside:
                        at = (x * HY + y) * LANES
                        value = pooled[s, 0, :, at : at + LANES]
                    else:
                        value = jnp.zeros((C_ONE, LANES), bf16)
                    moved[s, k * C_ONE : (k + 1) * C_ONE, tile * LANES : (tile + 1) * LANES] = value
                k += 1


def products_two(samples, tile_of, fields, moved, weights, sums, totals):
    for s in range(samples):
        wide = jnp.dot(weights[...], fields[s], preferred_element_type=f32)
        for x in range(HX):
            for y in range(HY):
                k = 0
                for ox in OFFS:
                    for oy in OFFS:
                        tile = tile_of.get((x + 1 - ox, y + 1 - oy))
                        if tile is not None:
                            part = wide[k * C_ONE : (k + 1) * C_ONE, tile * LANES : (tile + 1) * LANES]
                            old = sums[s].get((x, y))
                            sums[s][x, y] = part if old is None else old + part
                        k += 1
        totals = totals + lax.dot_general(moved[s], fields[s], NT, preferred_element_type=f32)
    return totals


def layer_two_inside(samples, vp_at, edge_at, *refs):
    blocks, (pooled, weights, expand, part, total, moved_ends, fields, moved) = refs[:-8], refs[-8:]
    tile_of = tiles_inside()
    expand_windows(samples, vp_at, edge_at, (0,), tile_of, blocks, expand, fields)
    shift_pooled(samples, tile_of, pooled, moved)
    shift_pooled(samples, tiles_ends(), pooled, moved_ends)
    sums = [{} for _ in range(samples)]
    totals = jnp.zeros((9 * C_ONE, 3 * C_TWO), f32)
    total[...] = products_two(samples, tile_of, fields, moved, weights, sums, totals)
    for s in range(samples):
        for (x, y), value in sums[s].items():
            at = (x * HY + y) * LANES
            part[s * C_ONE : (s + 1) * C_ONE, at : at + LANES] = value


def layer_two_ends(samples, scale, vp_at, edge_at, *refs):
    blocks, (weights, expand, part, total, moved, out, kept, message, fields) = refs[:-9], refs[-9:]
    tile_of = tiles_ends()
    expand_windows(samples, vp_at, edge_at, (-1, 1), tile_of, blocks, expand, fields)
    sums = [
        {
            (x, y): part[s * C_ONE : (s + 1) * C_ONE, (x * HY + y) * LANES : (x * HY + y + 1) * LANES]
            for x in range(HX)
            for y in range(HY)
        }
        for s in range(samples)
    ]
    totals = products_two(samples, tile_of, fields, moved, weights, sums, total[...]) * scale
    for s in range(samples):
        for (x, y), value in sums[s].items():
            at = (x * HY + y) * LANES
            got = value.astype(bf16)
            out[s, 0, :, at : at + LANES] = got
            kept[s * C_ONE : (s + 1) * C_ONE, at : at + LANES] = got
    width = 3 * C_TWO
    for k in range(9):
        message[:, k * width : (k + 1) * width] = totals[k * C_ONE : (k + 1) * C_ONE]
    message[:, GRAD_W_TWO:ONE_AT] = jnp.zeros((C_ONE, ONE_AT - GRAD_W_TWO), f32)


def shift_input(samples, rows_of, face_at, line_at, edge_at, blocks, own, ahead):
    used = samples * C_IN
    lane = iota((PACK, BZ), 1)
    for (px, py), line in rows_of.items():
        nx = -1 if px == 0 else 1 if px == BX + 1 else 0
        ny = -1 if py == 0 else 1 if py == BY + 1 else 0
        x, y = (px - 1) % BX, (py - 1) % BY
        if nx == 0 and ny == 0:
            row = own[:, (x * BY + y) * BZ : (x * BY + y + 1) * BZ].astype(f32)
        else:
            if nx != 0:
                ref, at = face_at[nx] if ny == 0 else line_at[nx, ny]
                tile = 2 * min(y, BY - 1 - y)
                chunk = 2 * (0 if x == 0 else 1) + (1 if y >= BY // 2 else 0)
            else:
                ref, at = line_at[nx, ny]
                tile = 2 * (0 if y == 0 else 1)
                chunk = x
            halves = []
            for t in (tile, tile + 1):
                four = blocks[ref][at + 4 * used * t : at + 4 * used * (t + 1)].astype(f32)
                halves.append(four[chunk * used : (chunk + 1) * used])
            row = jnp.concatenate(halves, axis=1)
            if used < PACK:
                row = jnp.concatenate([row, jnp.zeros((PACK - used, BZ), f32)], axis=0)
        ends = []
        for nz in (-1, 1):
            ref, at = edge_at[nx, ny, nz]
            ends.append(blocks[ref][at + C_TWO : at + EDGE].astype(f32))
        at = 2 * (x * BY + y)
        to = line * BZ
        before = jnp.where(lane == 0, ends[0][:, at + 1 : at + 2], pltpu.roll(row, 1, 1))
        after = jnp.where(lane == BZ - 1, ends[1][:, at : at + 1], pltpu.roll(row, BZ - 1, 1))
        for i, piece in enumerate((before, row, after)):
            ahead[i * PACK : (i + 1) * PACK, to : to + BZ] = piece.astype(bf16)


def lines_inside():
    return {(px, py): px * BY + py - 1 for px in range(BX + 2) for py in range(1, BY + 1)}


def lines_ends():
    return {(px, py): 2 * px + (py > 0) for px in range(BX + 2) for py in (0, BY + 1)}


def layer_one_inside(samples, face_at, edge_at, *refs):
    blocks, (own, ahead) = refs[:-2], refs[-2:]
    shift_input(samples, lines_inside(), face_at, {}, edge_at, blocks, own, ahead)


def layer_one(samples, scale, line_at, edge_at, *refs):
    blocks, (own, ahead, grad, chosen, before_sums, sums, ahead_ends, inside, ends) = refs[:-9], refs[-9:]
    sums[:, 0:ONE_AT] = before_sums[...]
    shift_input(samples, lines_ends(), {}, line_at, edge_at, blocks, own, ahead_ends)
    rows = samples * C_ONE
    table = doubling()
    empty = jnp.zeros((rows, BZ), bf16)
    for x in range(BX):
        inside[x, 0:rows, (BY - 1) * BZ :] = empty
        inside[x, 2 * rows :, 0:BZ] = empty
        ends[x, 0:rows, BZ:] = empty
        ends[x, rows : 2 * rows, 0:BZ] = empty
        ends[x, rows : 2 * rows, BZ:] = empty
        ends[x, 2 * rows :, 0:BZ] = empty
    for x in range(HX):
        for y in range(HY):
            at = (x * HY + y) * LANES
            wide = jnp.dot(grad[:, at : at + LANES], table, preferred_element_type=f32).astype(bf16)
            for dx in range(2):
                for dy in range(2):
                    cx, cy = 2 * x + dx, 2 * y + dy
                    value = wide * chosen[:, (cx * BY + cy) * BZ : (cx * BY + cy + 1) * BZ]
                    for j, oy in enumerate(OFFS):
                        to = cy + oy
                        here = slice(j * rows, (j + 1) * rows)
                        if to < 0:
                            ends[cx, here, 0:BZ] = value
                        elif to >= BY:
                            ends[cx, here, BZ:] = value
                        else:
                            inside[cx, here, to * BZ : (to + 1) * BZ] = value
    width = 3 * 3 * PACK
    product = jnp.zeros((3 * rows, width), f32)
    for x in range(BX):
        for left, right, size in ((inside, ahead, BY * BZ), (ends, ahead_ends, 2 * BZ)):
            pieces = [right[:, (x + 1 + ox) * size : (x + 2 + ox) * size] for ox in OFFS]
            product = product + lax.dot_general(
                left[x], jnp.concatenate(pieces, axis=0), NT, preferred_element_type=f32
            )
    sample_of = (iota((C_ONE, width), 1) % PACK) // C_IN
    k = iota((width, LANES), 0)
    to = (k % C_IN) * STRIDE_ONE + (k // (3 * PACK)) * 9 + (k // PACK) % 3
    total = jnp.zeros((C_ONE, LANES), f32)
    for j in range(3):
        folded = jnp.zeros((C_ONE, width), f32)
        for s in range(samples):
            at = j * rows + s * C_ONE
            folded = folded + jnp.where(sample_of == s, product[at : at + C_ONE], 0.0)
        fold = (to + 3 * j == iota((width, LANES), 1)).astype(f32)
        total = total + jnp.dot(
            folded, fold, preferred_element_type=f32, precision=lax.Precision.HIGHEST
        )
    sums[:, ONE_AT:] = total * scale


def finish(mine, theirs, grad_one, grad_two):
    total = mine[...] + theirs[...]
    for o in range(27):
        grad_two[o] = total[:, o * C_TWO : (o + 1) * C_TWO]
    for c in range(C_IN):
        at = ONE_AT + c * STRIDE_ONE
        grad_one[c] = total[:, at : at + 27]


def call(body, shapes, operands, far=0, scratch=(), flops=0, moved=0):
    if far:
        scratch = [pltpu.VMEM(a.shape, a.dtype) for a in operands[:far]]
        scratch.append(pltpu.SemaphoreType.DMA((far,)))
        away = [pltpu.with_memory_space_constraint(a, pltpu.HBM) for a in operands[:far]]
        operands = (*away, *operands[far:])
    spaces = [pltpu.HBM] * far + [pltpu.VMEM] * (len(operands) - far)
    return pl.pallas_call(
        body,
        out_shape=shapes,
        in_specs=[pl.BlockSpec(memory_space=space) for space in spaces],
        out_specs=jax.tree.map(lambda _: pl.BlockSpec(memory_space=pltpu.VMEM), shapes),
        scratch_shapes=list(scratch),
        compiler_params=pltpu.CompilerParams(vmem_limit_bytes=32 * 2**20),
        cost_estimate=pl.CostEstimate(flops=flops, bytes_accessed=moved, transcendentals=0),
    )(*operands)


def block_side(blocks):
    return min(k for k in range(1, blocks + 1) if k * k * k >= blocks)


def from_block(array, side, *offset):
    pairs = []
    for i in range(lax.axis_size("space")):
        at = (i // (side * side), i // side % side, i % side)
        x, y, z = ((c + o) % side for c, o in zip(at, offset))
        pairs.append(((x * side + y) * side + z, i))
    return lax.ppermute(array, "space", pairs)


def both_sides(array, side, axis):
    below = from_block(array, side, *(-1 if a == axis else 0 for a in range(3)))
    if side == 2:
        return {-1: below, 1: below}
    return {-1: below, 1: from_block(array, side, *(1 if a == axis else 0 for a in range(3)))}


def swapped(array, axis, bit):
    size = lax.axis_size(axis)
    return lax.ppermute(array, axis, [(i, i ^ bit) for i in range(size)])


def stacked(parts):
    kept, starts, places = [], [], []
    rows = 0
    for part in parts:
        found = [i for i, a in enumerate(kept) if a is part]
        if not found:
            found = [len(kept)]
            kept.append(part)
            starts.append(rows)
            rows += part.shape[0]
        places.append(starts[found[0]])
    return jnp.concatenate(kept, axis=0), places


def operands_of(*tables):
    arrays, numbered = [], []
    for table in tables:
        new = {}
        for key, (array, row) in table.items():
            found = [i for i, a in enumerate(arrays) if a is array]
            if not found:
                found = [len(arrays)]
                arrays.append(array)
            new[key] = (found[0], row)
        numbered.append(new)
    return arrays, numbered


def local(inputs, mask_one, place_one, pooled_one, w_two, mask_two, place_two, grad_two):
    blocks = lax.axis_size("space")
    side = block_side(blocks)
    samples = inputs.shape[0]
    cells = inputs.shape[3]
    half_cells = HX * HY * HZ
    shape = jax.ShapeDtypeStruct
    vp_rows = 2 * samples * C_TWO
    four = 4 * samples * C_IN
    vp_row = BY * four
    to_x, own = call(
        functools.partial(prepare, samples),
        (shape((BY * four + vp_rows, LANES), bf16), shape((PACK, cells), bf16)),
        (grad_two, place_two, mask_two, inputs),
        far=4,
        flops=2 * 10**7,
        moved=2**20,
    )
    edge = call(
        functools.partial(ends, samples, vp_row),
        shape((EDGE, LANES), bf16),
        (to_x, own),
        flops=10**7,
        moved=2**19,
    )
    chosen, folded_weights, expand, to_y = call(
        functools.partial(select_one, samples, vp_row),
        (
            shape((samples * C_ONE, cells), bf16),
            shape((9 * C_ONE, 3 * C_TWO), bf16),
            shape((2 * LANES, TABLE), bf16),
            shape((4 * four + vp_rows, LANES), bf16),
        ),
        (place_one, mask_one, w_two, to_x, own),
        far=3,
        flops=2 * 10**7,
        moved=3 * 2**20,
    )
    vp_at, edge_at, face_at, line_at = {(0, 0): (to_x, vp_row)}, {}, {}, {}
    from_x = both_sides(to_x, side, 0)
    edge_z = both_sides(edge, side, 2)
    if side == 2:
        diagonal = from_block(edge, side, 1, 0, 1)
        edge_x = {nz: {nx: diagonal for nx in (-1, 1)} for nz in (-1, 1)}
    else:
        edge_x = {nz: {nx: from_block(edge, side, nx, 0, nz) for nx in (-1, 1)} for nz in (-1, 1)}
    first = both_sides(to_y, side, 1)
    parts = []
    for n in (-1, 1):
        again = n == 1 and side == 2
        parts += parts[:2] if again else [from_x[n][vp_row:], from_x[n][: 2 * four]]
    second, starts = stacked(parts)
    second = both_sides(second, side, 1)
    parts = [edge_z[-1], edge_z[1]] + [edge_x[nz][nx] for nz in (-1, 1) for nx in (-1, 1)]
    third, edge_starts = stacked(parts)
    third = both_sides(third, side, 1)
    for n in (-1, 1):
        vp_at[n, 0] = (from_x[n], vp_row)
        face_at[n] = (from_x[n], 0)
        vp_at[0, n] = (first[n], 4 * four)
        line_at[0, n] = (first[n], 0)
        edge_at[0, 0, n] = (edge_z[n], 0)
        for i, nx in enumerate((-1, 1)):
            edge_at[nx, 0, n] = (edge_x[n][nx], 0)
            vp_at[nx, n] = (second[n], starts[2 * i])
            line_at[nx, n] = (second[n], starts[2 * i + 1])
        for i, nz in enumerate((-1, 1)):
            edge_at[0, n, nz] = (third[n], edge_starts[i])
            for j, nx in enumerate((-1, 1)):
                edge_at[nx, n, nz] = (third[n], edge_starts[2 + 2 * i + j])
    total = lax.axis_size("dp") * samples * blocks * cells

    def near(table, y):
        return {key: value for key, value in table.items() if key[1] in y}

    arrays, tables = operands_of(near(vp_at, (0,)), near(edge_at, (0,)))
    tiles, end_tiles = (HX + 2) * HY, (HX + 2) * 2
    part, total_two, moved_ends = call(
        functools.partial(layer_two_inside, samples, *tables),
        (
            shape((samples * C_ONE, half_cells), f32),
            shape((9 * C_ONE, 3 * C_TWO), f32),
            shape((samples, 9 * C_ONE, end_tiles * LANES), bf16),
        ),
        (*arrays, pooled_one, folded_weights, expand),
        scratch=(
            pltpu.VMEM((samples, 3 * C_TWO, tiles * LANES), bf16),
            pltpu.VMEM((samples, 9 * C_ONE, tiles * LANES), bf16),
        ),
        flops=5 * 10**8,
        moved=2**20,
    )
    arrays, tables = operands_of(face_at, near(edge_at, (0,)))
    ahead = call(
        functools.partial(layer_one_inside, samples, *tables),
        shape((3 * PACK, (BX + 2) * BY * BZ), bf16),
        (*arrays, own),
        flops=10**8,
        moved=2**20,
    )
    arrays, tables = operands_of(near(vp_at, (-1, 1)), near(edge_at, (-1, 1)))
    grad_pooled, kept, sums = call(
        functools.partial(layer_two_ends, samples, float(total // 8) ** -0.5, *tables),
        (
            shape((samples, 1, C_ONE, half_cells), bf16),
            shape((samples * C_ONE, half_cells), bf16),
            shape((C_ONE, ONE_AT), f32),
        ),
        (*arrays, folded_weights, expand, part, total_two, moved_ends),
        scratch=(pltpu.VMEM((samples, 3 * C_TWO, end_tiles * LANES), bf16),),
        flops=5 * 10**8,
        moved=2**20,
    )
    arrays, tables = operands_of(line_at, near(edge_at, (-1, 1)))
    sums = call(
        functools.partial(layer_one, samples, float(total) ** -0.5, *tables),
        shape((C_ONE, WIDTH), f32),
        (*arrays, own, ahead, kept, chosen, sums),
        scratch=(
            pltpu.VMEM((3 * PACK, (BX + 2) * 2 * BZ), bf16),
            pltpu.VMEM((BX, 3 * samples * C_ONE, BY * BZ), bf16),
            pltpu.VMEM((BX, 3 * samples * C_ONE, 2 * BZ), bf16),
        ),
        flops=5 * 10**8,
        moved=2**20,
    )
    steps = []
    for axis in ("dp", "space"):
        bit = 1
        while bit < lax.axis_size(axis):
            steps.append((axis, bit))
            bit *= 2
    for axis, bit in steps[:-1]:
        sums = sums + swapped(sums, axis, bit)
    grad_w_one, grad_w_two = call(
        finish,
        (shape((C_IN, C_ONE, 27), f32), shape((27, C_ONE, C_TWO), f32)),
        (sums, swapped(sums, *steps[-1])),
    )
    return grad_pooled, jnp.transpose(grad_w_one, (2, 0, 1)), grad_w_two


def solution(mesh):
    split = P("dp", "space", None, None)
    return jax.shard_map(
        local,
        mesh=mesh,
        in_specs=(split, split, split, split, P(), split, split, split),
        out_specs=(split, P(), P()),
        check_vma=False,
    )
```

time: 45.8 us -> 43.2 us (0.943)
  waiting for transfers between devices: 19.5 us -> 15.4 us
  starting transfers between devices: 15.2 us -> 16.7 us
    ppermute x5 -> x6, waiting for transfers between devices: 6.13 us -> 2.39 us  [from_block(): return lax.ppermute(array, 'space', pairs)]
    ppermute x5, starting transfers between devices: 6.14 us -> 7.38 us  [swapped(): return lax.ppermute(array, axis, [(i, i ^ bit) for i in range(size)])]
    ppermute x5 -> x6, starting transfers between devices: 9.08 us -> 9.36 us  [from_block(): return lax.ppermute(array, 'space', pairs)]
    pallas_call x6 -> x8, Pallas kernels: 10.2 us -> 10.1 us  [call(): pl.pallas_call(body, out_shape=shapes, in_specs=[pl.BlockSpec(memory_spac...]
  transfers between devices with their start and end apart: 10 -> 11, of which waited for: 9 -> 8; matrix products, arithmetic and copies ran while one was open for 0% -> 0% of each run, Pallas kernels for 5% -> 11%
where the time goes in v2:
time: 43.2 us; the launch traced here: 43 us
  starting transfers between devices  16.7 us (39%)
  waiting for transfers between devices  15.4 us (36%)
  Pallas kernels  10.1 us (23%)
  between operations  0.71 us (2%)
    ppermute x5, waiting for transfers between devices, swapped(): return lax.ppermute(array, axis, [(i, i ^ bit) for i in range(size)])  13 us
    pallas_call x8, Pallas kernels, call(): pl.pallas_call(body, out_shape=shapes, in_specs=[pl.BlockSpec(memory_spac...  10.1 us
    ppermute x6, starting transfers between devices, from_block(): return lax.ppermute(array, 'space', pairs)  9.36 us
    ppermute x5, starting transfers between devices, swapped(): return lax.ppermute(array, axis, [(i, i ^ bit) for i in range(size)])  7.38 us
    ppermute x6, waiting for transfers between devices, from_block(): return lax.ppermute(array, 'space', pairs)  2.39 us
  transfers between devices with their start and end apart: 11, of which 8 were waited for; matrix products, arithmetic and copies ran while one was open for 0% of the time, Pallas kernels for 11%

profile of v2, /device:TPU:0, one launch (start us, length us, event | category | flops | bytes accessed | tf_op | source)
XLA Modules:
  0.0 43.0 jit_solution(11871693757626936313)
XLA Ops:
  0.6 1.3 %shard_map.103 = (bf16[576,128]{1,0:T(8,128)(2,1)S(1)}, bf16[16,8192]{1,0:T(8,128)(2,1)S(1)}) custom-call(bf16[3,1,32,128]{3,2,1,0:T(8,128)(2,1)} %refs_0_.2, s32[3,1,32,128]{3,2,1,0:T(8,128)} %refs_1_.2, s32[3,1,32,1024]{3,2,1,0:T(8,128)} %refs_2_.2, bf16[3,1,4,8192]{3,2,1,0:T(4,128)(2,1)} %refs_3_.1), custom_call_target="tpu_custom_call" | custom-call | flops 20000000 | bytes 1048576 | tf_op jit(solution)/shard_map/pallas_call | solution.py:409
  2.0 0.0 copy-start
  2.0 4.1 %collective-permute-start.1 = (bf16[576,128]{1,0:T(8,128)(2,1)S(1)}, bf16[576,128]{1,0:T(8,128)(2,1)S(1)}, u32[]{:S(2)}, u32[]{:S(2)}) collective-permute-start(bf16[576,128]{1,0:T(8,128)(2,1)S(1)} %get-tuple-element.17.refs_3_.to_x.refs_0_), channel_id=1, source_target_pairs={{4,0},{5,1},{6,2},{7,3},{0,4},{1,5},{2,6},{3,7},{12,8},{13,9},{14,... | collective-permute-start | bytes 442376 | tf_op jit(solution)/shard_map/ppermute | solution.py:430
  6.1 0.2 shard_map.105
  6.3 1.5 %collective-permute-start.3 = (bf16[48,128]{1,0:T(8,128)(2,1)S(1)}, bf16[48,128]{1,0:T(8,128)(2,1)S(1)}, u32[]{:S(2)}, u32[]{:S(2)}) collective-permute-start(bf16[48,128]{1,0:T(8,128)(2,1)S(1)} %shard_map.105), channel_id=1, source_target_pairs={{1,0},{0,1},{3,2},{2,3},{5,4},{4,5},{7,6},{6,7},{9,8},{8,9},{11,10... | collective-permute-start | bytes 36872 | tf_op jit(solution)/shard_map/ppermute | solution.py:430
  7.8 0.0 collective-permute-start.4
  7.8 2.0 %shard_map.104 = (bf16[48,8192]{1,0:T(8,128)(2,1)S(1)}, bf16[144,96]{1,0:T(8,128)(2,1)S(1)}, bf16[256,768]{1,0:T(8,128)(2,1)S(1)}, bf16[384,128]{1,0:T(8,128)(2,1)S(1)}) custom-call(s32[3,1,16,1024]{3,2,1,0:T(8,128)} %refs_0_.3, s32[3,1,16,8192]{3,2,1,0:T(8,128)} %refs_1_.3, bf16[27,16,32]{2,1,0:T(8,128)(2,1)} %refs_2_.3, ...), custom_call_target="tpu_custom_call" | custom-call | flops 20000000 | bytes 3145728 | tf_op jit(solution)/shard_map/pallas_call | solution.py:409
  9.8 1.9 %collective-permute-start = (bf16[384,128]{1,0:T(8,128)(2,1)S(1)}, bf16[384,128]{1,0:T(8,128)(2,1)S(1)}, u32[]{:S(2)}, u32[]{:S(2)}) collective-permute-start(bf16[384,128]{1,0:T(8,128)(2,1)S(1)} %get-tuple-element.19), channel_id=1, source_target_pairs={{2,0},{3,1},{0,2},{1,3},{6,4},{7,5},{4,6},{5,7},{10,8},{11,9},{8,1... | collective-permute-start | bytes 294920 | tf_op jit(solution)/shard_map/ppermute | solution.py:430
  11.7 1.8 %collective-permute-done.1.refs_1_.refs_0_ = bf16[576,128]{1,0:T(8,128)(2,1)S(1)} collective-permute-done((bf16[576,128]{1,0:T(8,128)(2,1)S(1)}, bf16[576,128]{1,0:T(8,128)(2,1)S(1)}, u32[]{:S(2)}, u32[]{:S(2)}) %collective-permute-start.1) | collective-permute-done | bytes 147488 | tf_op jit(solution)/shard_map/ppermute | solution.py:430
  13.6 0.7 %collective-permute-start.2 = (bf16[288,128]{1,0:T(8,128)(2,1)S(1)}, bf16[288,128]{1,0:T(8,128)(2,1)S(1)}, u32[]{:S(2)}, u32[]{:S(2)}) collective-permute-start(bf16[288,128]{1,0:T(8,128)(2,1)S(1)} %pad_maximum_fusion), channel_id=1, source_target_pairs={{2,0},{3,1},{0,2},{1,3},{6,4},{7,5},{4,6},{5,7},{10,8},{11,9},{8,1... | collective-permute-start | bytes 221192 | tf_op jit(solution)/shard_map/ppermute | solution.py:430
  14.3 0.0 collective-permute-done.3.refs_2_.refs_1_
  14.3 0.4 collective-permute-done.4.refs_3_.refs_2_
  14.7 1.1 %collective-permute-start.5 = (bf16[96,128]{1,0:T(8,128)(2,1)S(1)}, bf16[96,128]{1,0:T(8,128)(2,1)S(1)}, u32[]{:S(2)}, u32[]{:S(2)}) collective-permute-start(bf16[96,128]{1,0:T(8,128)(2,1)S(1)} %pad_maximum_fusion.1), channel_id=1, source_target_pairs={{2,0},{3,1},{0,2},{1,3},{6,4},{7,5},{4,6},{5,7},{10,8},{11,9},{8,1... | collective-permute-start | bytes 73736 | tf_op jit(solution)/shard_map/ppermute | solution.py:430
  15.7 0.0 copy-done
  15.7 2.1 %shard_map.106 = (f32[48,1024]{1,0:T(8,128)S(1)}, f32[144,96]{1,0:T(8,128)S(1)}, bf16[3,144,1024]{2,1,0:T(8,128)(2,1)S(1)}) custom-call(bf16[576,128]{1,0:T(8,128)(2,1)S(1)} %get-tuple-element.17.refs_3_.to_x.refs_0_, bf16[576,128]{1,0:T(8,128)(2,1)S(1)} %collective-permute-done.1.refs_1_.refs_0_, ...), custom_call_target="tpu_custom_call" | custom-call | flops 500000000 | bytes 1048576 | tf_op jit(solution)/shard_map/pallas_call | solution.py:409
  17.8 0.5 %shard_map.108.refs_4_ = bf16[48,12288]{1,0:T(8,128)(2,1)S(1)} custom-call(bf16[576,128]{1,0:T(8,128)(2,1)S(1)} %collective-permute-done.1.refs_1_.refs_0_, bf16[48,128]{1,0:T(8,128)(2,1)S(1)} %collective-permute-done.3.refs_2_.refs_1_, bf16[48,128]{1,0:T(8,128)(2,1)S(1)} %collective-permute-done.4.refs_3_.refs_2_, ...), custom_call_target="tpu_custom_call" | custom-call | flops 100000000 | bytes 1048576 | tf_op jit(solution)/shard_map/pallas_call | solution.py:409
  18.3 0.2 collective-permute-done.5.refs_2_
  18.5 0.0 collective-permute-done.refs_0_
  18.5 0.0 collective-permute-done.2.refs_1_
  18.5 1.6 %shard_map.107 = (bf16[3,1,16,1024]{3,2,1,0:T(8,128)(2,1)}, bf16[48,1024]{1,0:T(8,128)(2,1)S(1)}, f32[16,896]{1,0:T(8,128)S(1)}) custom-call(bf16[384,128]{1,0:T(8,128)(2,1)S(1)} %collective-permute-done.refs_0_, bf16[288,128]{1,0:T(8,128)(2,1)S(1)} %collective-permute-done.2.refs_1_, bf16[96,128]{1,0:T(8,128)(2,1)S(1)} %collective-permute-done.5.refs_2_, ...), custom_call_target="tpu_custom_call" | custom-call | flops 500000000 | bytes 1048576 | tf_op jit(solution)/shard_map/pallas_call | solution.py:409
  20.1 1.7 %shard_map.109 = f32[16,1024]{1,0:T(8,128)S(1)} custom-call(bf16[384,128]{1,0:T(8,128)(2,1)S(1)} %collective-permute-done.refs_0_, bf16[288,128]{1,0:T(8,128)(2,1)S(1)} %collective-permute-done.2.refs_1_, bf16[96,128]{1,0:T(8,128)(2,1)S(1)} %collective-permute-done.5.refs_2_, bf16[16,8192]{1,0:T(8,128)(2,1)S(1)} %get-tuple-element.18.refs_4_.own.refs_3_, ...), custom_call_target="tpu_custom_call" | custom-call | flops 500000000 | bytes 1048576 | tf_op jit(solution)/shard_map/pallas_call | solution.py:409
  21.8 0.0 collective-permute-start.6
  21.8 1.3 %collective-permute-done.6 = f32[16,1024]{1,0:T(8,128)S(1)} collective-permute-done((f32[16,1024]{1,0:T(8,128)S(1)}, f32[16,1024]{1,0:T(8,128)S(1)}, u32[]{:S(2)}, u32[]{:S(2)}) %collective-permute-start.6) | collective-permute-done | bytes 65568 | tf_op jit(solution)/shard_map/ppermute | solution.py:442
  23.0 1.6 %collective-permute-start.7 = (f32[16,1024]{1,0:T(8,128)S(1)}, f32[16,1024]{1,0:T(8,128)S(1)}, u32[]{:S(2)}, u32[]{:S(2)}) collective-permute-start(f32[16,1024]{1,0:T(8,128)S(1)} %add.12), channel_id=1, source_target_pairs={{0,16},{8,24},{16,0},{24,8},{1,17},{9,25},{17,1},{25,9},{2,18},{10... | collective-permute-start | bytes 196616 | tf_op jit(solution)/shard_map/ppermute | solution.py:442
  24.6 2.7 %collective-permute-done.7 = f32[16,1024]{1,0:T(8,128)S(1)} collective-permute-done((f32[16,1024]{1,0:T(8,128)S(1)}, f32[16,1024]{1,0:T(8,128)S(1)}, u32[]{:S(2)}, u32[]{:S(2)}) %collective-permute-start.7) | collective-permute-done | bytes 65568 | tf_op jit(solution)/shard_map/ppermute | solution.py:442
  27.4 1.4 %collective-permute-start.8 = (f32[16,1024]{1,0:T(8,128)S(1)}, f32[16,1024]{1,0:T(8,128)S(1)}, u32[]{:S(2)}, u32[]{:S(2)}) collective-permute-start(f32[16,1024]{1,0:T(8,128)S(1)} %add.13), channel_id=1, source_target_pairs={{0,1},{1,0},{2,3},{3,2},{4,5},{5,4},{6,7},{7,6},{8,9},{9,8},{10,11... | collective-permute-start | bytes 196616 | tf_op jit(solution)/shard_map/ppermute | solution.py:442
  28.8 2.9 %collective-permute-done.8 = f32[16,1024]{1,0:T(8,128)S(1)} collective-permute-done((f32[16,1024]{1,0:T(8,128)S(1)}, f32[16,1024]{1,0:T(8,128)S(1)}, u32[]{:S(2)}, u32[]{:S(2)}) %collective-permute-start.8) | collective-permute-done | bytes 65568 | tf_op jit(solution)/shard_map/ppermute | solution.py:442
  31.7 1.1 %collective-permute-start.9 = (f32[16,1024]{1,0:T(8,128)S(1)}, f32[16,1024]{1,0:T(8,128)S(1)}, u32[]{:S(2)}, u32[]{:S(2)}) collective-permute-start(f32[16,1024]{1,0:T(8,128)S(1)} %add.14), channel_id=1, source_target_pairs={{0,2},{1,3},{2,0},{3,1},{4,6},{5,7},{6,4},{7,5},{8,10},{9,11},{10,... | collective-permute-start | bytes 196616 | tf_op jit(solution)/shard_map/ppermute | solution.py:442
  32.9 3.2 %collective-permute-done.9 = f32[16,1024]{1,0:T(8,128)S(1)} collective-permute-done((f32[16,1024]{1,0:T(8,128)S(1)}, f32[16,1024]{1,0:T(8,128)S(1)}, u32[]{:S(2)}, u32[]{:S(2)}) %collective-permute-start.9) | collective-permute-done | bytes 65568 | tf_op jit(solution)/shard_map/ppermute | solution.py:442
  36.1 3.2 %collective-permute-start.10 = (f32[16,1024]{1,0:T(8,128)S(1)}, f32[16,1024]{1,0:T(8,128)S(1)}, u32[]{:S(2)}, u32[]{:S(2)}) collective-permute-start(f32[16,1024]{1,0:T(8,128)S(1)} %add.15.mine), channel_id=1, source_target_pairs={{0,4},{1,5},{2,6},{3,7},{4,0},{5,1},{6,2},{7,3},{8,12},{9,13},{10,... | collective-permute-start | bytes 196616 | tf_op jit(solution)/shard_map/ppermute | solution.py:442
  39.3 2.9 %collective-permute-done.10.theirs = f32[16,1024]{1,0:T(8,128)S(1)} collective-permute-done((f32[16,1024]{1,0:T(8,128)S(1)}, f32[16,1024]{1,0:T(8,128)S(1)}, u32[]{:S(2)}, u32[]{:S(2)}) %collective-permute-start.10) | collective-permute-done | bytes 65568 | tf_op jit(solution)/shard_map/ppermute | solution.py:442
  42.2 0.8 %shard_map.110 = (f32[4,16,27]{2,1,0:T(8,128)}, f32[27,16,32]{2,1,0:T(8,128)}) custom-call(f32[16,1024]{1,0:T(8,128)S(1)} %add.15.mine, f32[16,1024]{1,0:T(8,128)S(1)} %collective-permute-done.10.theirs), custom_call_target="tpu_custom_call" | custom-call | tf_op jit(solution)/shard_map/pallas_call | solution.py:409
  (8 shorter events, 0.1 us)
Async XLA Ops:
  2.0 13.8 %copy-start = (bf16[3,1,16,1024]{3,2,1,0:T(8,128)(2,1)S(1)}, bf16[3,1,16,1024]{3,2,1,0:T(8,128)(2,1)}, u32[]{:S(2)}) copy-start(bf16[3,1,16,1024]{3,2,1,0:T(8,128)(2,1)} %refs_4_.1) | copy-start | bytes 294916
  2.0 11.6 %collective-permute-start.1 = (bf16[576,128]{1,0:T(8,128)(2,1)S(1)}, bf16[576,128]{1,0:T(8,128)(2,1)S(1)}, u32[]{:S(2)}, u32[]{:S(2)}) collective-permute-start(bf16[576,128]{1,0:T(8,128)(2,1)S(1)} %get-tuple-element.17.refs_3_.to_x.refs_0_), channel_id=1, source_target_pairs={{4,0},{5,1},{6,2},{7,3},{0,4},{1,5},{2,6},{3,7},{12,8},{13,9},{14,... | collective-permute-start | bytes 442376 | tf_op jit(solution)/shard_map/ppermute | solution.py:430
  6.3 8.0 %collective-permute-start.3 = (bf16[48,128]{1,0:T(8,128)(2,1)S(1)}, bf16[48,128]{1,0:T(8,128)(2,1)S(1)}, u32[]{:S(2)}, u32[]{:S(2)}) collective-permute-start(bf16[48,128]{1,0:T(8,128)(2,1)S(1)} %shard_map.105), channel_id=1, source_target_pairs={{1,0},{0,1},{3,2},{2,3},{5,4},{4,5},{7,6},{6,7},{9,8},{8,9},{11,10... | collective-permute-start | bytes 36872 | tf_op jit(solution)/shard_map/ppermute | solution.py:430
  7.8 6.9 %collective-permute-start.4 = (bf16[48,128]{1,0:T(8,128)(2,1)S(1)}, bf16[48,128]{1,0:T(8,128)(2,1)S(1)}, u32[]{:S(2)}, u32[]{:S(2)}) collective-permute-start(bf16[48,128]{1,0:T(8,128)(2,1)S(1)} %shard_map.105), channel_id=1, source_target_pairs={{5,0},{4,1},{7,2},{6,3},{1,4},{0,5},{3,6},{2,7},{13,8},{12,9},{15,... | collective-permute-start | bytes 36872 | tf_op jit(solution)/shard_map/ppermute | solution.py:430
  9.8 8.7 %collective-permute-start = (bf16[384,128]{1,0:T(8,128)(2,1)S(1)}, bf16[384,128]{1,0:T(8,128)(2,1)S(1)}, u32[]{:S(2)}, u32[]{:S(2)}) collective-permute-start(bf16[384,128]{1,0:T(8,128)(2,1)S(1)} %get-tuple-element.19), channel_id=1, source_target_pairs={{2,0},{3,1},{0,2},{1,3},{6,4},{7,5},{4,6},{5,7},{10,8},{11,9},{8,1... | collective-permute-start | bytes 294920 | tf_op jit(solution)/shard_map/ppermute | solution.py:430
  13.6 4.9 %collective-permute-start.2 = (bf16[288,128]{1,0:T(8,128)(2,1)S(1)}, bf16[288,128]{1,0:T(8,128)(2,1)S(1)}, u32[]{:S(2)}, u32[]{:S(2)}) collective-permute-start(bf16[288,128]{1,0:T(8,128)(2,1)S(1)} %pad_maximum_fusion), channel_id=1, source_target_pairs={{2,0},{3,1},{0,2},{1,3},{6,4},{7,5},{4,6},{5,7},{10,8},{11,9},{8,1... | collective-permute-start | bytes 221192 | tf_op jit(solution)/shard_map/ppermute | solution.py:430
  14.7 3.8 %collective-permute-start.5 = (bf16[96,128]{1,0:T(8,128)(2,1)S(1)}, bf16[96,128]{1,0:T(8,128)(2,1)S(1)}, u32[]{:S(2)}, u32[]{:S(2)}) collective-permute-start(bf16[96,128]{1,0:T(8,128)(2,1)S(1)} %pad_maximum_fusion.1), channel_id=1, source_target_pairs={{2,0},{3,1},{0,2},{1,3},{6,4},{7,5},{4,6},{5,7},{10,8},{11,9},{8,1... | collective-permute-start | bytes 73736 | tf_op jit(solution)/shard_map/ppermute | solution.py:430
  21.8 1.3 %collective-permute-start.6 = (f32[16,1024]{1,0:T(8,128)S(1)}, f32[16,1024]{1,0:T(8,128)S(1)}, u32[]{:S(2)}, u32[]{:S(2)}) collective-permute-start(f32[16,1024]{1,0:T(8,128)S(1)} %shard_map.109), channel_id=1, source_target_pairs={{0,8},{8,0},{16,24},{24,16},{1,9},{9,1},{17,25},{25,17},{2,10},{10... | collective-permute-start | bytes 196616 | tf_op jit(solution)/shard_map/ppermute | solution.py:442
  23.0 4.3 %collective-permute-start.7 = (f32[16,1024]{1,0:T(8,128)S(1)}, f32[16,1024]{1,0:T(8,128)S(1)}, u32[]{:S(2)}, u32[]{:S(2)}) collective-permute-start(f32[16,1024]{1,0:T(8,128)S(1)} %add.12), channel_id=1, source_target_pairs={{0,16},{8,24},{16,0},{24,8},{1,17},{9,25},{17,1},{25,9},{2,18},{10... | collective-permute-start | bytes 196616 | tf_op jit(solution)/shard_map/ppermute | solution.py:442
  27.4 4.3 %collective-permute-start.8 = (f32[16,1024]{1,0:T(8,128)S(1)}, f32[16,1024]{1,0:T(8,128)S(1)}, u32[]{:S(2)}, u32[]{:S(2)}) collective-permute-start(f32[16,1024]{1,0:T(8,128)S(1)} %add.13), channel_id=1, source_target_pairs={{0,1},{1,0},{2,3},{3,2},{4,5},{5,4},{6,7},{7,6},{8,9},{9,8},{10,11... | collective-permute-start | bytes 196616 | tf_op jit(solution)/shard_map/ppermute | solution.py:442
  31.7 4.3 %collective-permute-start.9 = (f32[16,1024]{1,0:T(8,128)S(1)}, f32[16,1024]{1,0:T(8,128)S(1)}, u32[]{:S(2)}, u32[]{:S(2)}) collective-permute-start(f32[16,1024]{1,0:T(8,128)S(1)} %add.14), channel_id=1, source_target_pairs={{0,2},{1,3},{2,0},{3,1},{4,6},{5,7},{6,4},{7,5},{8,10},{9,11},{10,... | collective-permute-start | bytes 196616 | tf_op jit(solution)/shard_map/ppermute | solution.py:442
  36.1 6.2 %collective-permute-start.10 = (f32[16,1024]{1,0:T(8,128)S(1)}, f32[16,1024]{1,0:T(8,128)S(1)}, u32[]{:S(2)}, u32[]{:S(2)}) collective-permute-start(f32[16,1024]{1,0:T(8,128)S(1)} %add.15.mine), channel_id=1, source_target_pairs={{0,4},{1,5},{2,6},{3,7},{4,0},{5,1},{6,2},{7,3},{8,12},{9,13},{10,... | collective-permute-start | bytes 196616 | tf_op jit(solution)/shard_map/ppermute | solution.py:442

commit v3 on v2

--- a/solution.py
+++ b/solution.py
@@ -23,6 +23,7 @@
 WIDTH = 1024
 ONE_AT = WIDTH - LANES
 STRIDE_ONE = LANES // C_IN
+HALF = C_ONE // 2
 TABLE = 3 * QY * LANES
 NT = (((1,), (1,)), ((), ()))
 f32, bf16, i32 = jnp.float32, jnp.bfloat16, jnp.int32
@@ -261,7 +262,7 @@
 
 
 def layer_two_ends(samples, scale, vp_at, edge_at, *refs):
-    blocks, (weights, expand, part, total, moved, out, kept, message, fields) = refs[:-9], refs[-9:]
+    blocks, (weights, expand, part, total, moved, kept, message, fields) = refs[:-8], refs[-8:]
     tile_of = tiles_ends()
     expand_windows(samples, vp_at, edge_at, (-1, 1), tile_of, blocks, expand, fields)
     sums = [
@@ -276,9 +277,7 @@
     for s in range(samples):
         for (x, y), value in sums[s].items():
             at = (x * HY + y) * LANES
-            got = value.astype(bf16)
-            out[s, 0, :, at : at + LANES] = got
-            kept[s * C_ONE : (s + 1) * C_ONE, at : at + LANES] = got
+            kept[s * C_ONE : (s + 1) * C_ONE, at : at + LANES] = value.astype(bf16)
     width = 3 * C_TWO
     for k in range(9):
         message[:, k * width : (k + 1) * width] = totals[k * C_ONE : (k + 1) * C_ONE]
@@ -330,14 +329,18 @@
     return {(px, py): 2 * px + (py > 0) for px in range(BX + 2) for py in (0, BY + 1)}
 
 
+def emit(samples, kept, out):
+    for s in range(samples):
+        out[s, 0] = kept[s * C_ONE : (s + 1) * C_ONE]
+
+
 def layer_one_inside(samples, face_at, edge_at, *refs):
     blocks, (own, ahead) = refs[:-2], refs[-2:]
     shift_input(samples, lines_inside(), face_at, {}, edge_at, blocks, own, ahead)
 
 
 def layer_one(samples, scale, line_at, edge_at, *refs):
-    blocks, (own, ahead, grad, chosen, before_sums, sums, ahead_ends, inside, ends) = refs[:-9], refs[-9:]
-    sums[:, 0:ONE_AT] = before_sums[...]
+    blocks, (own, ahead, grad, chosen, before_sums, half, mine, other, ahead_ends, inside, ends) = refs[:-11], refs[-11:]
     shift_input(samples, lines_ends(), {}, line_at, edge_at, blocks, own, ahead_ends)
     rows = samples * C_ONE
     table = doubling()
@@ -387,25 +390,34 @@
         total = total + jnp.dot(
             folded, fold, preferred_element_type=f32, precision=lax.Precision.HIGHEST
         )
-    sums[:, ONE_AT:] = total * scale
-
-
-def finish(mine, theirs, grad_one, grad_two):
-    total = mine[...] + theirs[...]
-    for o in range(27):
-        grad_two[o] = total[:, o * C_TWO : (o + 1) * C_TWO]
-    for c in range(C_IN):
-        at = ONE_AT + c * STRIDE_ONE
-        grad_one[c] = total[:, at : at + 27]
-
-
-def call(body, shapes, operands, far=0, scratch=(), flops=0, moved=0):
+    sums = jnp.concatenate([before_sums[...], total * scale], axis=1)
+    top, bottom = sums[0:HALF], sums[HALF:]
+    first = half[0] == 0
+    mine[...] = jnp.where(first, top, bottom)
+    other[...] = jnp.where(first, bottom, top)
+
+
+def finish(half, mine, theirs, grad_one, grad_two):
+    first = half[0] == 0
+    top = jnp.where(first, mine[...], theirs[...])
+    bottom = jnp.where(first, theirs[...], mine[...])
+    for rows, part in ((slice(0, HALF), top), (slice(HALF, C_ONE), bottom)):
+        for o in range(27):
+            grad_two[o, rows] = part[:, o * C_TWO : (o + 1) * C_TWO]
+        for c in range(C_IN):
+            at = ONE_AT + c * STRIDE_ONE
+            grad_one[c, rows] = part[:, at : at + 27]
+
+
+def call(body, shapes, operands, far=0, scratch=(), flops=0, moved=0, scalars=()):
     if far:
         scratch = [pltpu.VMEM(a.shape, a.dtype) for a in operands[:far]]
         scratch.append(pltpu.SemaphoreType.DMA((far,)))
         away = [pltpu.with_memory_space_constraint(a, pltpu.HBM) for a in operands[:far]]
         operands = (*away, *operands[far:])
     spaces = [pltpu.HBM] * far + [pltpu.VMEM] * (len(operands) - far)
+    for i in scalars:
+        spaces[i] = pltpu.SMEM
     return pl.pallas_call(
         body,
         out_shape=shapes,
@@ -571,10 +583,9 @@
         moved=2**20,
     )
     arrays, tables = operands_of(near(vp_at, (-1, 1)), near(edge_at, (-1, 1)))
-    grad_pooled, kept, sums = call(
+    kept, sums = call(
         functools.partial(layer_two_ends, samples, float(total // 8) ** -0.5, *tables),
         (
-            shape((samples, 1, C_ONE, half_cells), bf16),
             shape((samples * C_ONE, half_cells), bf16),
             shape((C_ONE, ONE_AT), f32),
         ),
@@ -584,10 +595,13 @@
         moved=2**20,
     )
     arrays, tables = operands_of(line_at, near(edge_at, (-1, 1)))
-    sums = call(
+    half = (lax.axis_index("dp") % 2).astype(i32).reshape(1)
+    operands = (*arrays, own, ahead, kept, chosen, sums, half)
+    half_sums = shape((HALF, WIDTH), f32)
+    mine, other = call(
         functools.partial(layer_one, samples, float(total) ** -0.5, *tables),
-        shape((C_ONE, WIDTH), f32),
-        (*arrays, own, ahead, kept, chosen, sums),
+        (half_sums, half_sums),
+        operands,
         scratch=(
             pltpu.VMEM((3 * PACK, (BX + 2) * 2 * BZ), bf16),
             pltpu.VMEM((BX, 3 * samples * C_ONE, BY * BZ), bf16),
@@ -595,19 +609,26 @@
         ),
         flops=5 * 10**8,
         moved=2**20,
-    )
-    steps = []
+        scalars=(len(operands) - 1,),
+    )
+    grad_pooled = call(
+        functools.partial(emit, samples),
+        shape((samples, 1, C_ONE, half_cells), bf16),
+        (kept,),
+        flops=10**6,
+        moved=2**18,
+    )
+    mine = mine + swapped(other, "dp", 1)
     for axis in ("dp", "space"):
-        bit = 1
+        bit = 2 if axis == "dp" else 1
         while bit < lax.axis_size(axis):
-            steps.append((axis, bit))
+            mine = mine + swapped(mine, axis, bit)
             bit *= 2
-    for axis, bit in steps[:-1]:
-        sums = sums + swapped(sums, axis, bit)
     grad_w_one, grad_w_two = call(
         finish,
         (shape((C_IN, C_ONE, 27), f32), shape((27, C_ONE, C_TWO), f32)),
-        (sums, swapped(sums, *steps[-1])),
+        (half, mine, swapped(mine, "dp", 1)),
+        scalars=(0,),
     )
     return grad_pooled, jnp.transpose(grad_w_one, (2, 0, 1)), grad_w_two
 

time: 43.2 us -> 41.4 us (0.958)
  waiting for transfers between devices: 15.4 us -> 13.8 us
    ppermute x5 -> x6, waiting for transfers between devices: 13 us -> 11.4 us  [swapped(): return lax.ppermute(array, axis, [(i, i ^ bit) for i in range(size)])]
    ppermute x5 -> x6, starting transfers between devices: 7.38 us -> 7.13 us  [swapped(): return lax.ppermute(array, axis, [(i, i ^ bit) for i in range(size)])]
    pallas_call x8 -> x9, Pallas kernels: 10.1 us -> 10.2 us  [call(): pl.pallas_call(body, out_shape=shapes, in_specs=[pl.BlockSpec(memory_spac...]
  transfers between devices with their start and end apart: 11 -> 12, of which waited for: 8 -> 9; matrix products, arithmetic and copies ran while one was open for 0% -> 0% of each run, Pallas kernels for 11% -> 13%
where the time goes in v3:
time: 41.4 us; the launch traced here: 41.2 us
  starting transfers between devices  16.5 us (40%)
  waiting for transfers between devices  13.8 us (33%)
  Pallas kernels  10.2 us (25%)
  between operations  0.7 us (2%)
    ppermute x6, waiting for transfers between devices, swapped(): return lax.ppermute(array, axis, [(i, i ^ bit) for i in range(size)])  11.4 us
    pallas_call x9, Pallas kernels, call(): pl.pallas_call(body, out_shape=shapes, in_specs=[pl.BlockSpec(memory_spac...  10.2 us
    ppermute x6, starting transfers between devices, from_block(): return lax.ppermute(array, 'space', pairs)  9.36 us
    ppermute x6, starting transfers between devices, swapped(): return lax.ppermute(array, axis, [(i, i ^ bit) for i in range(size)])  7.13 us
    ppermute x6, waiting for transfers between devices, from_block(): return lax.ppermute(array, 'space', pairs)  2.39 us
  transfers between devices with their start and end apart: 12, of which 9 were waited for; matrix products, arithmetic and copies ran while one was open for 0% of the time, Pallas kernels for 13%

profile of v3, /device:TPU:0, one launch (start us, length us, event | category | flops | bytes accessed | tf_op | source)
XLA Modules:
  0.0 41.2 jit_solution(16433536123327640368)
XLA Ops:
  0.6 1.3 %shard_map.103 = (bf16[576,128]{1,0:T(8,128)(2,1)S(1)}, bf16[16,8192]{1,0:T(8,128)(2,1)S(1)}) custom-call(bf16[3,1,32,128]{3,2,1,0:T(8,128)(2,1)} %refs_0_.2, s32[3,1,32,128]{3,2,1,0:T(8,128)} %refs_1_.2, s32[3,1,32,1024]{3,2,1,0:T(8,128)} %refs_2_.2, bf16[3,1,4,8192]{3,2,1,0:T(4,128)(2,1)} %refs_3_.1), custom_call_target="tpu_custom_call" | custom-call | flops 20000000 | bytes 1048576 | tf_op jit(solution)/shard_map/pallas_call | solution.py:421
  2.0 0.0 copy-start
  2.0 4.1 %collective-permute-start.1 = (bf16[576,128]{1,0:T(8,128)(2,1)S(1)}, bf16[576,128]{1,0:T(8,128)(2,1)S(1)}, u32[]{:S(2)}, u32[]{:S(2)}) collective-permute-start(bf16[576,128]{1,0:T(8,128)(2,1)S(1)} %get-tuple-element.18.refs_3_.to_x.refs_0_), channel_id=1, source_target_pairs={{4,0},{5,1},{6,2},{7,3},{0,4},{1,5},{2,6},{3,7},{12,8},{13,9},{14,... | collective-permute-start | bytes 442376 | tf_op jit(solution)/shard_map/ppermute | solution.py:442
  6.1 0.2 shard_map.105
  6.3 1.5 %collective-permute-start.3 = (bf16[48,128]{1,0:T(8,128)(2,1)S(1)}, bf16[48,128]{1,0:T(8,128)(2,1)S(1)}, u32[]{:S(2)}, u32[]{:S(2)}) collective-permute-start(bf16[48,128]{1,0:T(8,128)(2,1)S(1)} %shard_map.105), channel_id=1, source_target_pairs={{1,0},{0,1},{3,2},{2,3},{5,4},{4,5},{7,6},{6,7},{9,8},{8,9},{11,10... | collective-permute-start | bytes 36872 | tf_op jit(solution)/shard_map/ppermute | solution.py:442
  7.8 0.0 collective-permute-start.4
  7.8 2.0 %shard_map.104 = (bf16[48,8192]{1,0:T(8,128)(2,1)S(1)}, bf16[144,96]{1,0:T(8,128)(2,1)S(1)}, bf16[256,768]{1,0:T(8,128)(2,1)S(1)}, bf16[384,128]{1,0:T(8,128)(2,1)S(1)}) custom-call(s32[3,1,16,1024]{3,2,1,0:T(8,128)} %refs_0_.3, s32[3,1,16,8192]{3,2,1,0:T(8,128)} %refs_1_.3, bf16[27,16,32]{2,1,0:T(8,128)(2,1)} %refs_2_.3, ...), custom_call_target="tpu_custom_call" | custom-call | flops 20000000 | bytes 3145728 | tf_op jit(solution)/shard_map/pallas_call | solution.py:421
  9.8 1.9 %collective-permute-start = (bf16[384,128]{1,0:T(8,128)(2,1)S(1)}, bf16[384,128]{1,0:T(8,128)(2,1)S(1)}, u32[]{:S(2)}, u32[]{:S(2)}) collective-permute-start(bf16[384,128]{1,0:T(8,128)(2,1)S(1)} %get-tuple-element.20), channel_id=1, source_target_pairs={{2,0},{3,1},{0,2},{1,3},{6,4},{7,5},{4,6},{5,7},{10,8},{11,9},{8,1... | collective-permute-start | bytes 294920 | tf_op jit(solution)/shard_map/ppermute | solution.py:442
  11.7 1.8 %collective-permute-done.1.refs_1_.refs_0_ = bf16[576,128]{1,0:T(8,128)(2,1)S(1)} collective-permute-done((bf16[576,128]{1,0:T(8,128)(2,1)S(1)}, bf16[576,128]{1,0:T(8,128)(2,1)S(1)}, u32[]{:S(2)}, u32[]{:S(2)}) %collective-permute-start.1) | collective-permute-done | bytes 147488 | tf_op jit(solution)/shard_map/ppermute | solution.py:442
  13.6 0.7 %collective-permute-start.2 = (bf16[288,128]{1,0:T(8,128)(2,1)S(1)}, bf16[288,128]{1,0:T(8,128)(2,1)S(1)}, u32[]{:S(2)}, u32[]{:S(2)}) collective-permute-start(bf16[288,128]{1,0:T(8,128)(2,1)S(1)} %pad_maximum_fusion), channel_id=1, source_target_pairs={{2,0},{3,1},{0,2},{1,3},{6,4},{7,5},{4,6},{5,7},{10,8},{11,9},{8,1... | collective-permute-start | bytes 221192 | tf_op jit(solution)/shard_map/ppermute | solution.py:442
  14.3 0.0 collective-permute-done.3.refs_2_.refs_1_
  14.3 0.4 collective-permute-done.4.refs_3_.refs_2_
  14.7 1.1 %collective-permute-start.5 = (bf16[96,128]{1,0:T(8,128)(2,1)S(1)}, bf16[96,128]{1,0:T(8,128)(2,1)S(1)}, u32[]{:S(2)}, u32[]{:S(2)}) collective-permute-start(bf16[96,128]{1,0:T(8,128)(2,1)S(1)} %pad_maximum_fusion.1), channel_id=1, source_target_pairs={{2,0},{3,1},{0,2},{1,3},{6,4},{7,5},{4,6},{5,7},{10,8},{11,9},{8,1... | collective-permute-start | bytes 73736 | tf_op jit(solution)/shard_map/ppermute | solution.py:442
  15.7 0.0 copy-done
  15.7 2.1 %shard_map.106 = (f32[48,1024]{1,0:T(8,128)S(1)}, f32[144,96]{1,0:T(8,128)S(1)}, bf16[3,144,1024]{2,1,0:T(8,128)(2,1)S(1)}) custom-call(bf16[576,128]{1,0:T(8,128)(2,1)S(1)} %get-tuple-element.18.refs_3_.to_x.refs_0_, bf16[576,128]{1,0:T(8,128)(2,1)S(1)} %collective-permute-done.1.refs_1_.refs_0_, ...), custom_call_target="tpu_custom_call" | custom-call | flops 500000000 | bytes 1048576 | tf_op jit(solution)/shard_map/pallas_call | solution.py:421
  17.8 0.5 %shard_map.109.refs_4_ = bf16[48,12288]{1,0:T(8,128)(2,1)S(1)} custom-call(bf16[576,128]{1,0:T(8,128)(2,1)S(1)} %collective-permute-done.1.refs_1_.refs_0_, bf16[48,128]{1,0:T(8,128)(2,1)S(1)} %collective-permute-done.3.refs_2_.refs_1_, bf16[48,128]{1,0:T(8,128)(2,1)S(1)} %collective-permute-done.4.refs_3_.refs_2_, ...), custom_call_target="tpu_custom_call" | custom-call | flops 100000000 | bytes 1048576 | tf_op jit(solution)/shard_map/pallas_call | solution.py:421
  18.3 0.2 collective-permute-done.5.refs_2_
  18.5 0.0 collective-permute-done.refs_0_
  18.5 0.0 collective-permute-done.2.refs_1_
  18.5 1.0 %shard_map.107 = (bf16[48,1024]{1,0:T(8,128)(2,1)S(1)}, f32[16,896]{1,0:T(8,128)S(1)}) custom-call(bf16[384,128]{1,0:T(8,128)(2,1)S(1)} %collective-permute-done.refs_0_, bf16[288,128]{1,0:T(8,128)(2,1)S(1)} %collective-permute-done.2.refs_1_, bf16[96,128]{1,0:T(8,128)(2,1)S(1)} %collective-permute-done.5.refs_2_, ...), custom_call_target="tpu_custom_call" | custom-call | flops 500000000 | bytes 1048576 | tf_op jit(solution)/shard_map/pallas_call | solution.py:421
  19.5 1.7 %shard_map.110 = (f32[8,1024]{1,0:T(8,128)S(1)}, f32[8,1024]{1,0:T(8,128)S(1)}) custom-call(bf16[384,128]{1,0:T(8,128)(2,1)S(1)} %collective-permute-done.refs_0_, bf16[288,128]{1,0:T(8,128)(2,1)S(1)} %collective-permute-done.2.refs_1_, bf16[96,128]{1,0:T(8,128)(2,1)S(1)} %collective-permute-done.5.refs_2_, ...), custom_call_target="tpu_custom_call" | custom-call | flops 500000000 | bytes 1048576 | tf_op jit(solution)/shard_map/pallas_call | solution.py:421
  21.2 0.0 collective-permute-start.6
  21.2 1.2 %collective-permute-done.6 = f32[8,1024]{1,0:T(8,128)S(1)} collective-permute-done((f32[8,1024]{1,0:T(8,128)S(1)}, f32[8,1024]{1,0:T(8,128)S(1)}, u32[]{:S(2)}, u32[]{:S(2)}) %collective-permute-start.6) | collective-permute-done | bytes 32800 | tf_op jit(solution)/shard_map/ppermute | solution.py:454
  22.4 1.5 %collective-permute-start.7 = (f32[8,1024]{1,0:T(8,128)S(1)}, f32[8,1024]{1,0:T(8,128)S(1)}, u32[]{:S(2)}, u32[]{:S(2)}) collective-permute-start(f32[8,1024]{1,0:T(8,128)S(1)} %add.20), channel_id=1, source_target_pairs={{0,16},{8,24},{16,0},{24,8},{1,17},{9,25},{17,1},{25,9},{2,18},{10... | collective-permute-start | bytes 98312 | tf_op jit(solution)/shard_map/ppermute | solution.py:454
  23.9 2.4 %collective-permute-done.7 = f32[8,1024]{1,0:T(8,128)S(1)} collective-permute-done((f32[8,1024]{1,0:T(8,128)S(1)}, f32[8,1024]{1,0:T(8,128)S(1)}, u32[]{:S(2)}, u32[]{:S(2)}) %collective-permute-start.7) | collective-permute-done | bytes 32800 | tf_op jit(solution)/shard_map/ppermute | solution.py:454
  26.3 1.4 %collective-permute-start.8 = (f32[8,1024]{1,0:T(8,128)S(1)}, f32[8,1024]{1,0:T(8,128)S(1)}, u32[]{:S(2)}, u32[]{:S(2)}) collective-permute-start(f32[8,1024]{1,0:T(8,128)S(1)} %add.21), channel_id=1, source_target_pairs={{0,1},{1,0},{2,3},{3,2},{4,5},{5,4},{6,7},{7,6},{8,9},{9,8},{10,11... | collective-permute-start | bytes 98312 | tf_op jit(solution)/shard_map/ppermute | solution.py:454
  27.7 2.5 %collective-permute-done.8 = f32[8,1024]{1,0:T(8,128)S(1)} collective-permute-done((f32[8,1024]{1,0:T(8,128)S(1)}, f32[8,1024]{1,0:T(8,128)S(1)}, u32[]{:S(2)}, u32[]{:S(2)}) %collective-permute-start.8) | collective-permute-done | bytes 32800 | tf_op jit(solution)/shard_map/ppermute | solution.py:454
  30.2 1.1 %collective-permute-start.9 = (f32[8,1024]{1,0:T(8,128)S(1)}, f32[8,1024]{1,0:T(8,128)S(1)}, u32[]{:S(2)}, u32[]{:S(2)}) collective-permute-start(f32[8,1024]{1,0:T(8,128)S(1)} %add.22), channel_id=1, source_target_pairs={{0,2},{1,3},{2,0},{3,1},{4,6},{5,7},{6,4},{7,5},{8,10},{9,11},{10,... | collective-permute-start | bytes 98312 | tf_op jit(solution)/shard_map/ppermute | solution.py:454
  31.3 2.9 %collective-permute-done.9 = f32[8,1024]{1,0:T(8,128)S(1)} collective-permute-done((f32[8,1024]{1,0:T(8,128)S(1)}, f32[8,1024]{1,0:T(8,128)S(1)}, u32[]{:S(2)}, u32[]{:S(2)}) %collective-permute-start.9) | collective-permute-done | bytes 32800 | tf_op jit(solution)/shard_map/ppermute | solution.py:454
  34.2 3.1 %collective-permute-start.10 = (f32[8,1024]{1,0:T(8,128)S(1)}, f32[8,1024]{1,0:T(8,128)S(1)}, u32[]{:S(2)}, u32[]{:S(2)}) collective-permute-start(f32[8,1024]{1,0:T(8,128)S(1)} %add.23), channel_id=1, source_target_pairs={{0,4},{1,5},{2,6},{3,7},{4,0},{5,1},{6,2},{7,3},{8,12},{9,13},{10,... | collective-permute-start | bytes 98312 | tf_op jit(solution)/shard_map/ppermute | solution.py:454
  37.3 1.9 %collective-permute-done.10 = f32[8,1024]{1,0:T(8,128)S(1)} collective-permute-done((f32[8,1024]{1,0:T(8,128)S(1)}, f32[8,1024]{1,0:T(8,128)S(1)}, u32[]{:S(2)}, u32[]{:S(2)}) %collective-permute-start.10) | collective-permute-done | bytes 32800 | tf_op jit(solution)/shard_map/ppermute | solution.py:454
  39.2 0.0 collective-permute-start.11
  39.2 0.6 %shard_map.108 = bf16[3,1,16,1024]{3,2,1,0:T(8,128)(2,1)} custom-call(bf16[48,1024]{1,0:T(8,128)(2,1)S(1)} %get-tuple-element.26.kept.refs_5_), custom_call_target="tpu_custom_call" | custom-call | flops 1000000 | bytes 262144 | tf_op jit(solution)/shard_map/pallas_call | solution.py:421
  39.9 0.5 %collective-permute-done.11.theirs = f32[8,1024]{1,0:T(8,128)S(1)} collective-permute-done((f32[8,1024]{1,0:T(8,128)S(1)}, f32[8,1024]{1,0:T(8,128)S(1)}, u32[]{:S(2)}, u32[]{:S(2)}) %collective-permute-start.11) | collective-permute-done | bytes 32800 | tf_op jit(solution)/shard_map/ppermute | solution.py:454
  40.4 0.8 %shard_map.111 = (f32[4,16,27]{2,1,0:T(8,128)}, f32[27,16,32]{2,1,0:T(8,128)}) custom-call(s32[1]{0:T(128)} %bitcast.refs_8_.half, f32[8,1024]{1,0:T(8,128)S(1)} %add.24.mine, f32[8,1024]{1,0:T(8,128)S(1)} %collective-permute-done.11.theirs), custom_call_target="tpu_custom_call" | custom-call | tf_op jit(solution)/shard_map/pallas_call | solution.py:421
  (9 shorter events, 0.0 us)
Async XLA Ops:
  2.0 13.8 %copy-start = (bf16[3,1,16,1024]{3,2,1,0:T(8,128)(2,1)S(1)}, bf16[3,1,16,1024]{3,2,1,0:T(8,128)(2,1)}, u32[]{:S(2)}) copy-start(bf16[3,1,16,1024]{3,2,1,0:T(8,128)(2,1)} %refs_4_.1) | copy-start | bytes 294916
  2.0 11.6 %collective-permute-start.1 = (bf16[576,128]{1,0:T(8,128)(2,1)S(1)}, bf16[576,128]{1,0:T(8,128)(2,1)S(1)}, u32[]{:S(2)}, u32[]{:S(2)}) collective-permute-start(bf16[576,128]{1,0:T(8,128)(2,1)S(1)} %get-tuple-element.18.refs_3_.to_x.refs_0_), channel_id=1, source_target_pairs={{4,0},{5,1},{6,2},{7,3},{0,4},{1,5},{2,6},{3,7},{12,8},{13,9},{14,... | collective-permute-start | bytes 442376 | tf_op jit(solution)/shard_map/ppermute | solution.py:442
  6.3 8.0 %collective-permute-start.3 = (bf16[48,128]{1,0:T(8,128)(2,1)S(1)}, bf16[48,128]{1,0:T(8,128)(2,1)S(1)}, u32[]{:S(2)}, u32[]{:S(2)}) collective-permute-start(bf16[48,128]{1,0:T(8,128)(2,1)S(1)} %shard_map.105), channel_id=1, source_target_pairs={{1,0},{0,1},{3,2},{2,3},{5,4},{4,5},{7,6},{6,7},{9,8},{8,9},{11,10... | collective-permute-start | bytes 36872 | tf_op jit(solution)/shard_map/ppermute | solution.py:442
  7.8 6.9 %collective-permute-start.4 = (bf16[48,128]{1,0:T(8,128)(2,1)S(1)}, bf16[48,128]{1,0:T(8,128)(2,1)S(1)}, u32[]{:S(2)}, u32[]{:S(2)}) collective-permute-start(bf16[48,128]{1,0:T(8,128)(2,1)S(1)} %shard_map.105), channel_id=1, source_target_pairs={{5,0},{4,1},{7,2},{6,3},{1,4},{0,5},{3,6},{2,7},{13,8},{12,9},{15,... | collective-permute-start | bytes 36872 | tf_op jit(solution)/shard_map/ppermute | solution.py:442
  9.8 8.7 %collective-permute-start = (bf16[384,128]{1,0:T(8,128)(2,1)S(1)}, bf16[384,128]{1,0:T(8,128)(2,1)S(1)}, u32[]{:S(2)}, u32[]{:S(2)}) collective-permute-start(bf16[384,128]{1,0:T(8,128)(2,1)S(1)} %get-tuple-element.20), channel_id=1, source_target_pairs={{2,0},{3,1},{0,2},{1,3},{6,4},{7,5},{4,6},{5,7},{10,8},{11,9},{8,1... | collective-permute-start | bytes 294920 | tf_op jit(solution)/shard_map/ppermute | solution.py:442
  13.6 4.9 %collective-permute-start.2 = (bf16[288,128]{1,0:T(8,128)(2,1)S(1)}, bf16[288,128]{1,0:T(8,128)(2,1)S(1)}, u32[]{:S(2)}, u32[]{:S(2)}) collective-permute-start(bf16[288,128]{1,0:T(8,128)(2,1)S(1)} %pad_maximum_fusion), channel_id=1, source_target_pairs={{2,0},{3,1},{0,2},{1,3},{6,4},{7,5},{4,6},{5,7},{10,8},{11,9},{8,1... | collective-permute-start | bytes 221192 | tf_op jit(solution)/shard_map/ppermute | solution.py:442
  14.7 3.8 %collective-permute-start.5 = (bf16[96,128]{1,0:T(8,128)(2,1)S(1)}, bf16[96,128]{1,0:T(8,128)(2,1)S(1)}, u32[]{:S(2)}, u32[]{:S(2)}) collective-permute-start(bf16[96,128]{1,0:T(8,128)(2,1)S(1)} %pad_maximum_fusion.1), channel_id=1, source_target_pairs={{2,0},{3,1},{0,2},{1,3},{6,4},{7,5},{4,6},{5,7},{10,8},{11,9},{8,1... | collective-permute-start | bytes 73736 | tf_op jit(solution)/shard_map/ppermute | solution.py:442
  21.2 1.2 %collective-permute-start.6 = (f32[8,1024]{1,0:T(8,128)S(1)}, f32[8,1024]{1,0:T(8,128)S(1)}, u32[]{:S(2)}, u32[]{:S(2)}) collective-permute-start(f32[8,1024]{1,0:T(8,128)S(1)} %get-tuple-element.30), channel_id=1, source_target_pairs={{0,8},{8,0},{16,24},{24,16},{1,9},{9,1},{17,25},{25,17},{2,10},{10... | collective-permute-start | bytes 98312 | tf_op jit(solution)/shard_map/ppermute | solution.py:454
  22.4 3.9 %collective-permute-start.7 = (f32[8,1024]{1,0:T(8,128)S(1)}, f32[8,1024]{1,0:T(8,128)S(1)}, u32[]{:S(2)}, u32[]{:S(2)}) collective-permute-start(f32[8,1024]{1,0:T(8,128)S(1)} %add.20), channel_id=1, source_target_pairs={{0,16},{8,24},{16,0},{24,8},{1,17},{9,25},{17,1},{25,9},{2,18},{10... | collective-permute-start | bytes 98312 | tf_op jit(solution)/shard_map/ppermute | solution.py:454
  26.3 3.9 %collective-permute-start.8 = (f32[8,1024]{1,0:T(8,128)S(1)}, f32[8,1024]{1,0:T(8,128)S(1)}, u32[]{:S(2)}, u32[]{:S(2)}) collective-permute-start(f32[8,1024]{1,0:T(8,128)S(1)} %add.21), channel_id=1, source_target_pairs={{0,1},{1,0},{2,3},{3,2},{4,5},{5,4},{6,7},{7,6},{8,9},{9,8},{10,11... | collective-permute-start | bytes 98312 | tf_op jit(solution)/shard_map/ppermute | solution.py:454
  30.2 3.9 %collective-permute-start.9 = (f32[8,1024]{1,0:T(8,128)S(1)}, f32[8,1024]{1,0:T(8,128)S(1)}, u32[]{:S(2)}, u32[]{:S(2)}) collective-permute-start(f32[8,1024]{1,0:T(8,128)S(1)} %add.22), channel_id=1, source_target_pairs={{0,2},{1,3},{2,0},{3,1},{4,6},{5,7},{6,4},{7,5},{8,10},{9,11},{10,... | collective-permute-start | bytes 98312 | tf_op jit(solution)/shard_map/ppermute | solution.py:454
  34.2 5.0 %collective-permute-start.10 = (f32[8,1024]{1,0:T(8,128)S(1)}, f32[8,1024]{1,0:T(8,128)S(1)}, u32[]{:S(2)}, u32[]{:S(2)}) collective-permute-start(f32[8,1024]{1,0:T(8,128)S(1)} %add.23), channel_id=1, source_target_pairs={{0,4},{1,5},{2,6},{3,7},{4,0},{5,1},{6,2},{7,3},{8,12},{9,13},{10,... | collective-permute-start | bytes 98312 | tf_op jit(solution)/shard_map/ppermute | solution.py:454
  39.2 1.2 %collective-permute-start.11 = (f32[8,1024]{1,0:T(8,128)S(1)}, f32[8,1024]{1,0:T(8,128)S(1)}, u32[]{:S(2)}, u32[]{:S(2)}) collective-permute-start(f32[8,1024]{1,0:T(8,128)S(1)} %add.24.mine), channel_id=1, source_target_pairs={{0,8},{8,0},{16,24},{24,16},{1,9},{9,1},{17,25},{25,17},{2,10},{10... | collective-permute-start | bytes 98312 | tf_op jit(solution)/shard_map/ppermute | solution.py:454

commit v4 on v3

--- a/solution.py
+++ b/solution.py
@@ -17,7 +17,7 @@
 QY, QZ = HY // 2, HZ // 2
 LANES = 128
 PACK = 16
-EDGE = C_TWO + PACK
+ENDS_AT = LANES - 2 * BX * BY
 OFFS = (-1, 0, 1)
 GRAD_W_TWO = 27 * C_TWO
 WIDTH = 1024
@@ -101,15 +101,15 @@
             pick = (spot + (8 * s + 4 * t) == column).astype(bf16)
             at = vp_row + t * rows + s * C_TWO
             packed = packed + jnp.dot(to_x[at : at + C_TWO], pick, preferred_element_type=f32)
-    edge[0:C_TWO] = packed.astype(bf16)
     lane = iota((PACK, LANES), 1)
-    packed = jnp.zeros((PACK, LANES), f32)
+    cells = packed[0:PACK]
     for row in range(BX * BY):
         left = own[:, row * BZ : row * BZ + LANES].astype(f32)
         right = own[:, (row + 1) * BZ - LANES : (row + 1) * BZ].astype(f32)
-        packed = jnp.where(lane == 2 * row, left[:, 0:1], packed)
-        packed = jnp.where(lane == 2 * row + 1, right[:, LANES - 1 :], packed)
-    edge[C_TWO:EDGE] = packed.astype(bf16)
+        cells = jnp.where(lane == ENDS_AT + 2 * row, left[:, 0:1], cells)
+        cells = jnp.where(lane == ENDS_AT + 2 * row + 1, right[:, LANES - 1 :], cells)
+    edge[0:PACK] = cells.astype(bf16)
+    edge[PACK:] = packed[PACK:].astype(bf16)
 
 
 def select_one(samples, vp_row, *refs):
@@ -312,8 +312,8 @@
         ends = []
         for nz in (-1, 1):
             ref, at = edge_at[nx, ny, nz]
-            ends.append(blocks[ref][at + C_TWO : at + EDGE].astype(f32))
-        at = 2 * (x * BY + y)
+            ends.append(blocks[ref][at : at + PACK].astype(f32))
+        at = ENDS_AT + 2 * (x * BY + y)
         to = line * BZ
         before = jnp.where(lane == 0, ends[0][:, at + 1 : at + 2], pltpu.roll(row, 1, 1))
         after = jnp.where(lane == BZ - 1, ends[1][:, at : at + 1], pltpu.roll(row, BZ - 1, 1))
@@ -386,10 +386,13 @@
         for s in range(samples):
             at = j * rows + s * C_ONE
             folded = folded + jnp.where(sample_of == s, product[at : at + C_ONE], 0.0)
-        fold = (to + 3 * j == iota((width, LANES), 1)).astype(f32)
-        total = total + jnp.dot(
-            folded, fold, preferred_element_type=f32, precision=lax.Precision.HIGHEST
-        )
+        fold = (to + 3 * j == iota((width, LANES), 1)).astype(bf16)
+        parts = []
+        for _ in range(3):
+            parts.append(folded.astype(bf16))
+            folded = folded - parts[-1].astype(f32)
+        got = jnp.dot(jnp.concatenate(parts, axis=0), fold, preferred_element_type=f32)
+        total = total + (got[2 * C_ONE :] + got[C_ONE : 2 * C_ONE] + got[0:C_ONE])
     sums = jnp.concatenate([before_sums[...], total * scale], axis=1)
     top, bottom = sums[0:HALF], sums[HALF:]
     first = half[0] == 0
@@ -502,7 +505,7 @@
     )
     edge = call(
         functools.partial(ends, samples, vp_row),
-        shape((EDGE, LANES), bf16),
+        shape((C_TWO, LANES), bf16),
         (to_x, own),
         flops=10**7,
         moved=2**19,

time: 41.4 us -> 40.8 us (0.986)
  waiting for transfers between devices: 13.8 us -> 13.1 us
  starting transfers between devices: 16.5 us -> 17 us
  Pallas kernels: 10.2 us -> 9.76 us
    ppermute x6, waiting for transfers between devices: 2.39 us -> 1.9 us  [from_block(): return lax.ppermute(array, 'space', pairs)]
    pallas_call x9, Pallas kernels: 10.2 us -> 9.76 us  [call(): pl.pallas_call(body, out_shape=shapes, in_specs=[pl.BlockSpec(memory_spac...]
    ppermute x6, starting transfers between devices: 7.13 us -> 7.55 us  [swapped(): return lax.ppermute(array, axis, [(i, i ^ bit) for i in range(size)])]
  transfers between devices with their start and end apart: 12 -> 12, of which waited for: 9 -> 8; matrix products, arithmetic and copies ran while one was open for 0% -> 0% of each run, Pallas kernels for 13% -> 13%
where the time goes in v4:
time: 40.8 us; the launch traced here: 40.6 us
  starting transfers between devices  17 us (42%)
  waiting for transfers between devices  13.1 us (32%)
  Pallas kernels  9.76 us (24%)
  between operations  0.72 us (2%)
    ppermute x6, waiting for transfers between devices, swapped(): return lax.ppermute(array, axis, [(i, i ^ bit) for i in range(size)])  11.2 us
    pallas_call x9, Pallas kernels, call(): pl.pallas_call(body, out_shape=shapes, in_specs=[pl.BlockSpec(memory_spac...  9.76 us
    ppermute x6, starting transfers between devices, from_block(): return lax.ppermute(array, 'space', pairs)  9.5 us
    ppermute x6, starting transfers between devices, swapped(): return lax.ppermute(array, axis, [(i, i ^ bit) for i in range(size)])  7.55 us
    ppermute x6, waiting for transfers between devices, from_block(): return lax.ppermute(array, 'space', pairs)  1.9 us
  transfers between devices with their start and end apart: 12, of which 8 were waited for; matrix products, arithmetic and copies ran while one was open for 0% of the time, Pallas kernels for 13%

profile of v4, /device:TPU:0, one launch (start us, length us, event | category | flops | bytes accessed | tf_op | source)
XLA Modules:
  0.0 40.6 jit_solution(468682107974797826)
XLA Ops:
  0.6 1.3 %shard_map.103 = (bf16[576,128]{1,0:T(8,128)(2,1)S(1)}, bf16[16,8192]{1,0:T(8,128)(2,1)S(1)}) custom-call(bf16[3,1,32,128]{3,2,1,0:T(8,128)(2,1)} %refs_0_.2, s32[3,1,32,128]{3,2,1,0:T(8,128)} %refs_1_.2, s32[3,1,32,1024]{3,2,1,0:T(8,128)} %refs_2_.2, bf16[3,1,4,8192]{3,2,1,0:T(4,128)(2,1)} %refs_3_.1), custom_call_target="tpu_custom_call" | custom-call | flops 20000000 | bytes 1048576 | tf_op jit(solution)/shard_map/pallas_call | solution.py:424
  2.0 0.0 copy-start
  2.0 4.1 %collective-permute-start.1 = (bf16[576,128]{1,0:T(8,128)(2,1)S(1)}, bf16[576,128]{1,0:T(8,128)(2,1)S(1)}, u32[]{:S(2)}, u32[]{:S(2)}) collective-permute-start(bf16[576,128]{1,0:T(8,128)(2,1)S(1)} %get-tuple-element.18.refs_3_.to_x.refs_0_), channel_id=1, source_target_pairs={{4,0},{5,1},{6,2},{7,3},{0,4},{1,5},{2,6},{3,7},{12,8},{13,9},{14,... | collective-permute-start | bytes 442376 | tf_op jit(solution)/shard_map/ppermute | solution.py:445
  6.1 0.2 shard_map.105
  6.3 1.6 %collective-permute-start.3 = (bf16[32,128]{1,0:T(8,128)(2,1)S(1)}, bf16[32,128]{1,0:T(8,128)(2,1)S(1)}, u32[]{:S(2)}, u32[]{:S(2)}) collective-permute-start(bf16[32,128]{1,0:T(8,128)(2,1)S(1)} %shard_map.105), channel_id=1, source_target_pairs={{1,0},{0,1},{3,2},{2,3},{5,4},{4,5},{7,6},{6,7},{9,8},{8,9},{11,10... | collective-permute-start | bytes 24584 | tf_op jit(solution)/shard_map/ppermute | solution.py:445
  7.9 0.0 collective-permute-start.4
  7.9 2.0 %shard_map.104 = (bf16[48,8192]{1,0:T(8,128)(2,1)S(1)}, bf16[144,96]{1,0:T(8,128)(2,1)S(1)}, bf16[256,768]{1,0:T(8,128)(2,1)S(1)}, bf16[384,128]{1,0:T(8,128)(2,1)S(1)}) custom-call(s32[3,1,16,1024]{3,2,1,0:T(8,128)} %refs_0_.3, s32[3,1,16,8192]{3,2,1,0:T(8,128)} %refs_1_.3, bf16[27,16,32]{2,1,0:T(8,128)(2,1)} %refs_2_.3, ...), custom_call_target="tpu_custom_call" | custom-call | flops 20000000 | bytes 3145728 | tf_op jit(solution)/shard_map/pallas_call | solution.py:424
  9.8 1.9 %collective-permute-start = (bf16[384,128]{1,0:T(8,128)(2,1)S(1)}, bf16[384,128]{1,0:T(8,128)(2,1)S(1)}, u32[]{:S(2)}, u32[]{:S(2)}) collective-permute-start(bf16[384,128]{1,0:T(8,128)(2,1)S(1)} %get-tuple-element.20), channel_id=1, source_target_pairs={{2,0},{3,1},{0,2},{1,3},{6,4},{7,5},{4,6},{5,7},{10,8},{11,9},{8,1... | collective-permute-start | bytes 294920 | tf_op jit(solution)/shard_map/ppermute | solution.py:445
  11.8 1.6 %collective-permute-done.1.refs_1_.refs_0_ = bf16[576,128]{1,0:T(8,128)(2,1)S(1)} collective-permute-done((bf16[576,128]{1,0:T(8,128)(2,1)S(1)}, bf16[576,128]{1,0:T(8,128)(2,1)S(1)}, u32[]{:S(2)}, u32[]{:S(2)}) %collective-permute-start.1) | collective-permute-done | bytes 147488 | tf_op jit(solution)/shard_map/ppermute | solution.py:445
  13.4 0.8 %collective-permute-start.2 = (bf16[288,128]{1,0:T(8,128)(2,1)S(1)}, bf16[288,128]{1,0:T(8,128)(2,1)S(1)}, u32[]{:S(2)}, u32[]{:S(2)}) collective-permute-start(bf16[288,128]{1,0:T(8,128)(2,1)S(1)} %pad_maximum_fusion), channel_id=1, source_target_pairs={{2,0},{3,1},{0,2},{1,3},{6,4},{7,5},{4,6},{5,7},{10,8},{11,9},{8,1... | collective-permute-start | bytes 221192 | tf_op jit(solution)/shard_map/ppermute | solution.py:445
  14.2 0.0 collective-permute-done.3.refs_2_.refs_1_
  14.2 0.3 collective-permute-done.4.refs_3_.refs_2_
  14.4 1.1 %collective-permute-start.5 = (bf16[64,128]{1,0:T(8,128)(2,1)S(1)}, bf16[64,128]{1,0:T(8,128)(2,1)S(1)}, u32[]{:S(2)}, u32[]{:S(2)}) collective-permute-start(bf16[64,128]{1,0:T(8,128)(2,1)S(1)} %pad_maximum_fusion.1), channel_id=1, source_target_pairs={{2,0},{3,1},{0,2},{1,3},{6,4},{7,5},{4,6},{5,7},{10,8},{11,9},{8,1... | collective-permute-start | bytes 49160 | tf_op jit(solution)/shard_map/ppermute | solution.py:445
  15.6 0.0 copy-done
  15.6 2.1 %shard_map.106 = (f32[48,1024]{1,0:T(8,128)S(1)}, f32[144,96]{1,0:T(8,128)S(1)}, bf16[3,144,1024]{2,1,0:T(8,128)(2,1)S(1)}) custom-call(bf16[576,128]{1,0:T(8,128)(2,1)S(1)} %get-tuple-element.18.refs_3_.to_x.refs_0_, bf16[576,128]{1,0:T(8,128)(2,1)S(1)} %collective-permute-done.1.refs_1_.refs_0_, ...), custom_call_target="tpu_custom_call" | custom-call | flops 500000000 | bytes 1048576 | tf_op jit(solution)/shard_map/pallas_call | solution.py:424
  17.7 0.5 %shard_map.109.refs_4_ = bf16[48,12288]{1,0:T(8,128)(2,1)S(1)} custom-call(bf16[576,128]{1,0:T(8,128)(2,1)S(1)} %collective-permute-done.1.refs_1_.refs_0_, bf16[32,128]{1,0:T(8,128)(2,1)S(1)} %collective-permute-done.3.refs_2_.refs_1_, bf16[32,128]{1,0:T(8,128)(2,1)S(1)} %collective-permute-done.4.refs_3_.refs_2_, ...), custom_call_target="tpu_custom_call" | custom-call | flops 100000000 | bytes 1048576 | tf_op jit(solution)/shard_map/pallas_call | solution.py:424
  18.1 0.0 collective-permute-done.5.refs_2_
  18.2 0.0 collective-permute-done.refs_0_
  18.2 0.0 collective-permute-done.2.refs_1_
  18.2 1.0 %shard_map.107 = (bf16[48,1024]{1,0:T(8,128)(2,1)S(1)}, f32[16,896]{1,0:T(8,128)S(1)}) custom-call(bf16[384,128]{1,0:T(8,128)(2,1)S(1)} %collective-permute-done.refs_0_, bf16[288,128]{1,0:T(8,128)(2,1)S(1)} %collective-permute-done.2.refs_1_, bf16[64,128]{1,0:T(8,128)(2,1)S(1)} %collective-permute-done.5.refs_2_, ...), custom_call_target="tpu_custom_call" | custom-call | flops 500000000 | bytes 1048576 | tf_op jit(solution)/shard_map/pallas_call | solution.py:424
  19.2 1.2 %shard_map.110 = (f32[8,1024]{1,0:T(8,128)S(1)}, f32[8,1024]{1,0:T(8,128)S(1)}) custom-call(bf16[384,128]{1,0:T(8,128)(2,1)S(1)} %collective-permute-done.refs_0_, bf16[288,128]{1,0:T(8,128)(2,1)S(1)} %collective-permute-done.2.refs_1_, bf16[64,128]{1,0:T(8,128)(2,1)S(1)} %collective-permute-done.5.refs_2_, ...), custom_call_target="tpu_custom_call" | custom-call | flops 500000000 | bytes 1048576 | tf_op jit(solution)/shard_map/pallas_call | solution.py:424
  20.4 0.0 collective-permute-start.6
  20.4 1.2 %collective-permute-done.6 = f32[8,1024]{1,0:T(8,128)S(1)} collective-permute-done((f32[8,1024]{1,0:T(8,128)S(1)}, f32[8,1024]{1,0:T(8,128)S(1)}, u32[]{:S(2)}, u32[]{:S(2)}) %collective-permute-start.6) | collective-permute-done | bytes 32800 | tf_op jit(solution)/shard_map/ppermute | solution.py:457
  21.7 1.6 %collective-permute-start.7 = (f32[8,1024]{1,0:T(8,128)S(1)}, f32[8,1024]{1,0:T(8,128)S(1)}, u32[]{:S(2)}, u32[]{:S(2)}) collective-permute-start(f32[8,1024]{1,0:T(8,128)S(1)} %add.20), channel_id=1, source_target_pairs={{0,16},{8,24},{16,0},{24,8},{1,17},{9,25},{17,1},{25,9},{2,18},{10... | collective-permute-start | bytes 98312 | tf_op jit(solution)/shard_map/ppermute | solution.py:457
  23.2 2.3 %collective-permute-done.7 = f32[8,1024]{1,0:T(8,128)S(1)} collective-permute-done((f32[8,1024]{1,0:T(8,128)S(1)}, f32[8,1024]{1,0:T(8,128)S(1)}, u32[]{:S(2)}, u32[]{:S(2)}) %collective-permute-start.7) | collective-permute-done | bytes 32800 | tf_op jit(solution)/shard_map/ppermute | solution.py:457
  25.6 1.5 %collective-permute-start.8 = (f32[8,1024]{1,0:T(8,128)S(1)}, f32[8,1024]{1,0:T(8,128)S(1)}, u32[]{:S(2)}, u32[]{:S(2)}) collective-permute-start(f32[8,1024]{1,0:T(8,128)S(1)} %add.21), channel_id=1, source_target_pairs={{0,1},{1,0},{2,3},{3,2},{4,5},{5,4},{6,7},{7,6},{8,9},{9,8},{10,11... | collective-permute-start | bytes 98312 | tf_op jit(solution)/shard_map/ppermute | solution.py:457
  27.1 2.4 %collective-permute-done.8 = f32[8,1024]{1,0:T(8,128)S(1)} collective-permute-done((f32[8,1024]{1,0:T(8,128)S(1)}, f32[8,1024]{1,0:T(8,128)S(1)}, u32[]{:S(2)}, u32[]{:S(2)}) %collective-permute-start.8) | collective-permute-done | bytes 32800 | tf_op jit(solution)/shard_map/ppermute | solution.py:457
  29.5 1.1 %collective-permute-start.9 = (f32[8,1024]{1,0:T(8,128)S(1)}, f32[8,1024]{1,0:T(8,128)S(1)}, u32[]{:S(2)}, u32[]{:S(2)}) collective-permute-start(f32[8,1024]{1,0:T(8,128)S(1)} %add.22), channel_id=1, source_target_pairs={{0,2},{1,3},{2,0},{3,1},{4,6},{5,7},{6,4},{7,5},{8,10},{9,11},{10,... | collective-permute-start | bytes 98312 | tf_op jit(solution)/shard_map/ppermute | solution.py:457
  30.6 2.8 %collective-permute-done.9 = f32[8,1024]{1,0:T(8,128)S(1)} collective-permute-done((f32[8,1024]{1,0:T(8,128)S(1)}, f32[8,1024]{1,0:T(8,128)S(1)}, u32[]{:S(2)}, u32[]{:S(2)}) %collective-permute-start.9) | collective-permute-done | bytes 32800 | tf_op jit(solution)/shard_map/ppermute | solution.py:457
  33.4 3.3 %collective-permute-start.10 = (f32[8,1024]{1,0:T(8,128)S(1)}, f32[8,1024]{1,0:T(8,128)S(1)}, u32[]{:S(2)}, u32[]{:S(2)}) collective-permute-start(f32[8,1024]{1,0:T(8,128)S(1)} %add.23), channel_id=1, source_target_pairs={{0,4},{1,5},{2,6},{3,7},{4,0},{5,1},{6,2},{7,3},{8,12},{9,13},{10,... | collective-permute-start | bytes 98312 | tf_op jit(solution)/shard_map/ppermute | solution.py:457
  36.7 1.9 %collective-permute-done.10 = f32[8,1024]{1,0:T(8,128)S(1)} collective-permute-done((f32[8,1024]{1,0:T(8,128)S(1)}, f32[8,1024]{1,0:T(8,128)S(1)}, u32[]{:S(2)}, u32[]{:S(2)}) %collective-permute-start.10) | collective-permute-done | bytes 32800 | tf_op jit(solution)/shard_map/ppermute | solution.py:457
  38.6 0.0 collective-permute-start.11
  38.6 0.6 %shard_map.108 = bf16[3,1,16,1024]{3,2,1,0:T(8,128)(2,1)} custom-call(bf16[48,1024]{1,0:T(8,128)(2,1)S(1)} %get-tuple-element.26.kept.refs_5_), custom_call_target="tpu_custom_call" | custom-call | flops 1000000 | bytes 262144 | tf_op jit(solution)/shard_map/pallas_call | solution.py:424
  39.3 0.5 %collective-permute-done.11.theirs = f32[8,1024]{1,0:T(8,128)S(1)} collective-permute-done((f32[8,1024]{1,0:T(8,128)S(1)}, f32[8,1024]{1,0:T(8,128)S(1)}, u32[]{:S(2)}, u32[]{:S(2)}) %collective-permute-start.11) | collective-permute-done | bytes 32800 | tf_op jit(solution)/shard_map/ppermute | solution.py:457
  39.8 0.8 %shard_map.111 = (f32[4,16,27]{2,1,0:T(8,128)}, f32[27,16,32]{2,1,0:T(8,128)}) custom-call(s32[1]{0:T(128)} %bitcast.refs_8_.half, f32[8,1024]{1,0:T(8,128)S(1)} %add.24.mine, f32[8,1024]{1,0:T(8,128)S(1)} %collective-permute-done.11.theirs), custom_call_target="tpu_custom_call" | custom-call | tf_op jit(solution)/shard_map/pallas_call | solution.py:424
  (9 shorter events, 0.0 us)
Async XLA Ops:
  2.0 13.6 %copy-start = (bf16[3,1,16,1024]{3,2,1,0:T(8,128)(2,1)S(1)}, bf16[3,1,16,1024]{3,2,1,0:T(8,128)(2,1)}, u32[]{:S(2)}) copy-start(bf16[3,1,16,1024]{3,2,1,0:T(8,128)(2,1)} %refs_4_.1) | copy-start | bytes 294916
  2.0 11.4 %collective-permute-start.1 = (bf16[576,128]{1,0:T(8,128)(2,1)S(1)}, bf16[576,128]{1,0:T(8,128)(2,1)S(1)}, u32[]{:S(2)}, u32[]{:S(2)}) collective-permute-start(bf16[576,128]{1,0:T(8,128)(2,1)S(1)} %get-tuple-element.18.refs_3_.to_x.refs_0_), channel_id=1, source_target_pairs={{4,0},{5,1},{6,2},{7,3},{0,4},{1,5},{2,6},{3,7},{12,8},{13,9},{14,... | collective-permute-start | bytes 442376 | tf_op jit(solution)/shard_map/ppermute | solution.py:445
  6.3 7.9 %collective-permute-start.3 = (bf16[32,128]{1,0:T(8,128)(2,1)S(1)}, bf16[32,128]{1,0:T(8,128)(2,1)S(1)}, u32[]{:S(2)}, u32[]{:S(2)}) collective-permute-start(bf16[32,128]{1,0:T(8,128)(2,1)S(1)} %shard_map.105), channel_id=1, source_target_pairs={{1,0},{0,1},{3,2},{2,3},{5,4},{4,5},{7,6},{6,7},{9,8},{8,9},{11,10... | collective-permute-start | bytes 24584 | tf_op jit(solution)/shard_map/ppermute | solution.py:445
  7.9 6.6 %collective-permute-start.4 = (bf16[32,128]{1,0:T(8,128)(2,1)S(1)}, bf16[32,128]{1,0:T(8,128)(2,1)S(1)}, u32[]{:S(2)}, u32[]{:S(2)}) collective-permute-start(bf16[32,128]{1,0:T(8,128)(2,1)S(1)} %shard_map.105), channel_id=1, source_target_pairs={{5,0},{4,1},{7,2},{6,3},{1,4},{0,5},{3,6},{2,7},{13,8},{12,9},{15,... | collective-permute-start | bytes 24584 | tf_op jit(solution)/shard_map/ppermute | solution.py:445
  9.8 8.3 %collective-permute-start = (bf16[384,128]{1,0:T(8,128)(2,1)S(1)}, bf16[384,128]{1,0:T(8,128)(2,1)S(1)}, u32[]{:S(2)}, u32[]{:S(2)}) collective-permute-start(bf16[384,128]{1,0:T(8,128)(2,1)S(1)} %get-tuple-element.20), channel_id=1, source_target_pairs={{2,0},{3,1},{0,2},{1,3},{6,4},{7,5},{4,6},{5,7},{10,8},{11,9},{8,1... | collective-permute-start | bytes 294920 | tf_op jit(solution)/shard_map/ppermute | solution.py:445
  13.4 4.8 %collective-permute-start.2 = (bf16[288,128]{1,0:T(8,128)(2,1)S(1)}, bf16[288,128]{1,0:T(8,128)(2,1)S(1)}, u32[]{:S(2)}, u32[]{:S(2)}) collective-permute-start(bf16[288,128]{1,0:T(8,128)(2,1)S(1)} %pad_maximum_fusion), channel_id=1, source_target_pairs={{2,0},{3,1},{0,2},{1,3},{6,4},{7,5},{4,6},{5,7},{10,8},{11,9},{8,1... | collective-permute-start | bytes 221192 | tf_op jit(solution)/shard_map/ppermute | solution.py:445
  14.4 3.7 %collective-permute-start.5 = (bf16[64,128]{1,0:T(8,128)(2,1)S(1)}, bf16[64,128]{1,0:T(8,128)(2,1)S(1)}, u32[]{:S(2)}, u32[]{:S(2)}) collective-permute-start(bf16[64,128]{1,0:T(8,128)(2,1)S(1)} %pad_maximum_fusion.1), channel_id=1, source_target_pairs={{2,0},{3,1},{0,2},{1,3},{6,4},{7,5},{4,6},{5,7},{10,8},{11,9},{8,1... | collective-permute-start | bytes 49160 | tf_op jit(solution)/shard_map/ppermute | solution.py:445
  20.4 1.2 %collective-permute-start.6 = (f32[8,1024]{1,0:T(8,128)S(1)}, f32[8,1024]{1,0:T(8,128)S(1)}, u32[]{:S(2)}, u32[]{:S(2)}) collective-permute-start(f32[8,1024]{1,0:T(8,128)S(1)} %get-tuple-element.30), channel_id=1, source_target_pairs={{0,8},{8,0},{16,24},{24,16},{1,9},{9,1},{17,25},{25,17},{2,10},{10... | collective-permute-start | bytes 98312 | tf_op jit(solution)/shard_map/ppermute | solution.py:457
  21.7 3.9 %collective-permute-start.7 = (f32[8,1024]{1,0:T(8,128)S(1)}, f32[8,1024]{1,0:T(8,128)S(1)}, u32[]{:S(2)}, u32[]{:S(2)}) collective-permute-start(f32[8,1024]{1,0:T(8,128)S(1)} %add.20), channel_id=1, source_target_pairs={{0,16},{8,24},{16,0},{24,8},{1,17},{9,25},{17,1},{25,9},{2,18},{10... | collective-permute-start | bytes 98312 | tf_op jit(solution)/shard_map/ppermute | solution.py:457
  25.6 3.9 %collective-permute-start.8 = (f32[8,1024]{1,0:T(8,128)S(1)}, f32[8,1024]{1,0:T(8,128)S(1)}, u32[]{:S(2)}, u32[]{:S(2)}) collective-permute-start(f32[8,1024]{1,0:T(8,128)S(1)} %add.21), channel_id=1, source_target_pairs={{0,1},{1,0},{2,3},{3,2},{4,5},{5,4},{6,7},{7,6},{8,9},{9,8},{10,11... | collective-permute-start | bytes 98312 | tf_op jit(solution)/shard_map/ppermute | solution.py:457
  29.5 3.9 %collective-permute-start.9 = (f32[8,1024]{1,0:T(8,128)S(1)}, f32[8,1024]{1,0:T(8,128)S(1)}, u32[]{:S(2)}, u32[]{:S(2)}) collective-permute-start(f32[8,1024]{1,0:T(8,128)S(1)} %add.22), channel_id=1, source_target_pairs={{0,2},{1,3},{2,0},{3,1},{4,6},{5,7},{6,4},{7,5},{8,10},{9,11},{10,... | collective-permute-start | bytes 98312 | tf_op jit(solution)/shard_map/ppermute | solution.py:457
  33.4 5.2 %collective-permute-start.10 = (f32[8,1024]{1,0:T(8,128)S(1)}, f32[8,1024]{1,0:T(8,128)S(1)}, u32[]{:S(2)}, u32[]{:S(2)}) collective-permute-start(f32[8,1024]{1,0:T(8,128)S(1)} %add.23), channel_id=1, source_target_pairs={{0,4},{1,5},{2,6},{3,7},{4,0},{5,1},{6,2},{7,3},{8,12},{9,13},{10,... | collective-permute-start | bytes 98312 | tf_op jit(solution)/shard_map/ppermute | solution.py:457
  38.6 1.2 %collective-permute-start.11 = (f32[8,1024]{1,0:T(8,128)S(1)}, f32[8,1024]{1,0:T(8,128)S(1)}, u32[]{:S(2)}, u32[]{:S(2)}) collective-permute-start(f32[8,1024]{1,0:T(8,128)S(1)} %add.24.mine), channel_id=1, source_target_pairs={{0,8},{8,0},{16,24},{24,16},{1,9},{9,1},{17,25},{25,17},{2,10},{10... | collective-permute-start | bytes 98312 | tf_op jit(solution)/shard_map/ppermute | solution.py:457

commit v5 on v4

--- a/solution.py
+++ b/solution.py
@@ -89,7 +89,7 @@
         to_x[4 * used * t : 4 * used * (t + 1)] = jnp.concatenate(group, axis=0).astype(bf16)
 
 
-def ends(samples, vp_row, to_x, own, edge):
+def ends(samples, vp_row, to_x, own, edge, to_y):
     rows = samples * C_TWO
     lane = iota((LANES, LANES), 0)
     spot = (lane // QZ) * 2 + (lane % QZ == QZ - 1).astype(i32)
@@ -110,14 +110,6 @@
         cells = jnp.where(lane == ENDS_AT + 2 * row + 1, right[:, LANES - 1 :], cells)
     edge[0:PACK] = cells.astype(bf16)
     edge[PACK:] = packed[PACK:].astype(bf16)
-
-
-def select_one(samples, vp_row, *refs):
-    far, (to_x, own), (chosen, folded_weights, expand, to_y), near, sems = (
-        refs[:3], refs[3:5], refs[5:9], refs[9:12], refs[12],
-    )
-    place, mask, weights = near
-    copies = fetch(tuple(zip(far, near)), sems)
     used = samples * C_IN
     to_y[4 * 4 * used :] = to_x[vp_row:]
     for t in range(4):
@@ -126,6 +118,12 @@
             at = (x * BY + (BY - 1) * (t // 2)) * BZ + (t % 2) * LANES
             group.append(own[:, at : at + LANES].astype(f32)[0:used])
         to_y[4 * used * t : 4 * used * (t + 1)] = jnp.concatenate(group, axis=0).astype(bf16)
+
+
+def select_one(samples, *refs):
+    far, (chosen, folded_weights, expand), near, sems = refs[:3], refs[3:6], refs[6:9], refs[9]
+    place, mask, weights = near
+    copies = fetch(tuple(zip(far, near)), sems)
     k = iota((2 * LANES, TABLE), 0)
     j = iota((1, TABLE), 1)
     shift = j // (QY * LANES) - 1
@@ -155,15 +153,14 @@
                     chosen[:, to : to + BZ] = jnp.where(hit, 1.0, 0.0).astype(bf16)
 
 
-def expand_windows(samples, vp_at, edge_at, ys, tile_of, blocks, expand, fields):
+def expand_windows(samples, vp_at, edge_at, tile_of, blocks, expand, fields):
     rows = samples * C_TWO
     lane = iota((rows, LANES), 1)
     odd = iota((C_TWO, LANES), 1) % 2 == 1
     groups = {}
-    for nx in OFFS:
-        for ny in ys:
-            key = (vp_at[nx, ny], edge_at[nx, ny, -1], edge_at[nx, ny, 1])
-            groups.setdefault(key, []).append((nx, ny))
+    for nx, ny in vp_at:
+        key = (vp_at[nx, ny], edge_at[nx, ny, -1], edge_at[nx, ny, 1])
+        groups.setdefault(key, []).append((nx, ny))
     for ((ref, at), low, high), places in groups.items():
         edge = blocks[low[0]][low[1] : low[1] + C_TWO].astype(f32)
         if low != high:
@@ -203,8 +200,12 @@
                                 )
 
 
-def tiles_inside():
-    return {(px, py): px * HY + py - 1 for px in range(HX + 2) for py in range(1, HY + 1)}
+def tiles_own():
+    return {(px, py): (px - 1) * HY + py - 1 for px in range(1, HX + 1) for py in range(1, HY + 1)}
+
+
+def tiles_x():
+    return {(px, py): (px > 0) * HY + py - 1 for px in (0, HX + 1) for py in range(1, HY + 1)}
 
 
 def tiles_ends():
@@ -246,26 +247,8 @@
     return totals
 
 
-def layer_two_inside(samples, vp_at, edge_at, *refs):
-    blocks, (pooled, weights, expand, part, total, moved_ends, fields, moved) = refs[:-8], refs[-8:]
-    tile_of = tiles_inside()
-    expand_windows(samples, vp_at, edge_at, (0,), tile_of, blocks, expand, fields)
-    shift_pooled(samples, tile_of, pooled, moved)
-    shift_pooled(samples, tiles_ends(), pooled, moved_ends)
-    sums = [{} for _ in range(samples)]
-    totals = jnp.zeros((9 * C_ONE, 3 * C_TWO), f32)
-    total[...] = products_two(samples, tile_of, fields, moved, weights, sums, totals)
-    for s in range(samples):
-        for (x, y), value in sums[s].items():
-            at = (x * HY + y) * LANES
-            part[s * C_ONE : (s + 1) * C_ONE, at : at + LANES] = value
-
-
-def layer_two_ends(samples, scale, vp_at, edge_at, *refs):
-    blocks, (weights, expand, part, total, moved, kept, message, fields) = refs[:-8], refs[-8:]
-    tile_of = tiles_ends()
-    expand_windows(samples, vp_at, edge_at, (-1, 1), tile_of, blocks, expand, fields)
-    sums = [
+def parts_of(samples, part):
+    return [
         {
             (x, y): part[s * C_ONE : (s + 1) * C_ONE, (x * HY + y) * LANES : (x * HY + y + 1) * LANES]
             for x in range(HX)
@@ -273,11 +256,44 @@
         }
         for s in range(samples)
     ]
+
+
+def store_parts(sums, part):
+    for s, tiles in enumerate(sums):
+        for (x, y), value in tiles.items():
+            at = (x * HY + y) * LANES
+            part[s * C_ONE : (s + 1) * C_ONE, at : at + LANES] = value.astype(part.dtype)
+
+
+def layer_two_own(samples, vp_at, edge_at, *refs):
+    blocks, (pooled, weights, expand, part, total, moved_x, moved_ends, fields, moved) = refs[:-9], refs[-9:]
+    tile_of = tiles_own()
+    expand_windows(samples, vp_at, edge_at, tile_of, blocks, expand, fields)
+    shift_pooled(samples, tile_of, pooled, moved)
+    shift_pooled(samples, tiles_x(), pooled, moved_x)
+    shift_pooled(samples, tiles_ends(), pooled, moved_ends)
+    sums = [{} for _ in range(samples)]
+    totals = jnp.zeros((9 * C_ONE, 3 * C_TWO), f32)
+    total[...] = products_two(samples, tile_of, fields, moved, weights, sums, totals)
+    store_parts(sums, part)
+
+
+def layer_two_x(samples, vp_at, edge_at, *refs):
+    blocks, (weights, expand, old, old_total, moved, part, total, fields) = refs[:-8], refs[-8:]
+    tile_of = tiles_x()
+    expand_windows(samples, vp_at, edge_at, tile_of, blocks, expand, fields)
+    sums = parts_of(samples, old)
+    total[...] = products_two(samples, tile_of, fields, moved, weights, sums, old_total[...])
+    store_parts(sums, part)
+
+
+def layer_two_ends(samples, scale, vp_at, edge_at, *refs):
+    blocks, (weights, expand, part, total, moved, kept, message, fields) = refs[:-8], refs[-8:]
+    tile_of = tiles_ends()
+    expand_windows(samples, vp_at, edge_at, tile_of, blocks, expand, fields)
+    sums = parts_of(samples, part)
     totals = products_two(samples, tile_of, fields, moved, weights, sums, total[...]) * scale
-    for s in range(samples):
-        for (x, y), value in sums[s].items():
-            at = (x * HY + y) * LANES
-            kept[s * C_ONE : (s + 1) * C_ONE, at : at + LANES] = value.astype(bf16)
+    store_parts(sums, kept)
     width = 3 * C_TWO
     for k in range(9):
         message[:, k * width : (k + 1) * width] = totals[k * C_ONE : (k + 1) * C_ONE]
@@ -452,9 +468,9 @@
     return {-1: below, 1: from_block(array, side, *(1 if a == axis else 0 for a in range(3)))}
 
 
-def swapped(array, axis, bit):
-    size = lax.axis_size(axis)
-    return lax.ppermute(array, axis, [(i, i ^ bit) for i in range(size)])
+def swapped(array, bits):
+    devices = lax.axis_size("dp") * lax.axis_size("space")
+    return lax.ppermute(array, ("dp", "space"), [(i, i ^ bits) for i in range(devices)])
 
 
 def stacked(parts):
@@ -503,22 +519,21 @@
         flops=2 * 10**7,
         moved=2**20,
     )
-    edge = call(
+    edge, to_y = call(
         functools.partial(ends, samples, vp_row),
-        shape((C_TWO, LANES), bf16),
+        (shape((C_TWO, LANES), bf16), shape((4 * four + vp_rows, LANES), bf16)),
         (to_x, own),
         flops=10**7,
         moved=2**19,
     )
-    chosen, folded_weights, expand, to_y = call(
-        functools.partial(select_one, samples, vp_row),
+    chosen, folded_weights, expand = call(
+        functools.partial(select_one, samples),
         (
             shape((samples * C_ONE, cells), bf16),
             shape((9 * C_ONE, 3 * C_TWO), bf16),
             shape((2 * LANES, TABLE), bf16),
-            shape((4 * four + vp_rows, LANES), bf16),
         ),
-        (place_one, mask_one, w_two, to_x, own),
+        (place_one, mask_one, w_two),
         far=3,
         flops=2 * 10**7,
         moved=3 * 2**20,
@@ -532,10 +547,31 @@
     else:
         edge_x = {nz: {nx: from_block(edge, side, nx, 0, nz) for nx in (-1, 1)} for nz in (-1, 1)}
     first = both_sides(to_y, side, 1)
+    end_tiles, x_tiles = (HX + 2) * 2, 2 * HY
+    part_shape = shape((samples * C_ONE, half_cells), f32)
+    total_shape = shape((9 * C_ONE, 3 * C_TWO), f32)
+    arrays, tables = operands_of({(0, 0): vp_at[0, 0]}, {(0, 0, n): (edge_z[n], 0) for n in (-1, 1)})
+    part, total_two, moved_x, moved_ends = call(
+        functools.partial(layer_two_own, samples, *tables),
+        (
+            part_shape,
+            total_shape,
+            shape((samples, 9 * C_ONE, x_tiles * LANES), bf16),
+            shape((samples, 9 * C_ONE, end_tiles * LANES), bf16),
+        ),
+        (*arrays, pooled_one, folded_weights, expand),
+        scratch=(
+            pltpu.VMEM((samples, 3 * C_TWO, half_cells), bf16),
+            pltpu.VMEM((samples, 9 * C_ONE, half_cells), bf16),
+        ),
+        flops=5 * 10**8,
+        moved=2**20,
+    )
+    ready = {n: lax.optimization_barrier((from_x[n], total_two))[0] for n in ((-1,) if side == 2 else (-1, 1))}
     parts = []
     for n in (-1, 1):
         again = n == 1 and side == 2
-        parts += parts[:2] if again else [from_x[n][vp_row:], from_x[n][: 2 * four]]
+        parts += parts[:2] if again else [ready[n][vp_row:], ready[n][: 2 * four]]
     second, starts = stacked(parts)
     second = both_sides(second, side, 1)
     parts = [edge_z[-1], edge_z[1]] + [edge_x[nz][nx] for nz in (-1, 1) for nx in (-1, 1)]
@@ -560,20 +596,14 @@
     def near(table, y):
         return {key: value for key, value in table.items() if key[1] in y}
 
-    arrays, tables = operands_of(near(vp_at, (0,)), near(edge_at, (0,)))
-    tiles, end_tiles = (HX + 2) * HY, (HX + 2) * 2
-    part, total_two, moved_ends = call(
-        functools.partial(layer_two_inside, samples, *tables),
-        (
-            shape((samples * C_ONE, half_cells), f32),
-            shape((9 * C_ONE, 3 * C_TWO), f32),
-            shape((samples, 9 * C_ONE, end_tiles * LANES), bf16),
-        ),
-        (*arrays, pooled_one, folded_weights, expand),
-        scratch=(
-            pltpu.VMEM((samples, 3 * C_TWO, tiles * LANES), bf16),
-            pltpu.VMEM((samples, 9 * C_ONE, tiles * LANES), bf16),
-        ),
+    arrays, tables = operands_of(
+        {(n, 0): vp_at[n, 0] for n in (-1, 1)}, {key: edge_at[key] for key in edge_at if key[0] != 0 and key[1] == 0}
+    )
+    part, total_two = call(
+        functools.partial(layer_two_x, samples, *tables),
+        (part_shape, total_shape),
+        (*arrays, folded_weights, expand, part, total_two, moved_x),
+        scratch=(pltpu.VMEM((samples, 3 * C_TWO, x_tiles * LANES), bf16),),
         flops=5 * 10**8,
         moved=2**20,
     )
@@ -621,16 +651,19 @@
         flops=10**6,
         moved=2**18,
     )
-    mine = mine + swapped(other, "dp", 1)
-    for axis in ("dp", "space"):
-        bit = 2 if axis == "dp" else 1
-        while bit < lax.axis_size(axis):
-            mine = mine + swapped(mine, axis, bit)
-            bit *= 2
+    mine = mine + swapped(other, blocks)
+    devices = lax.axis_size("dp") * blocks
+    bits = [1 << k for k in range(devices.bit_length() - 1) if 1 << k > blocks]
+    bits += [1 << k for k in range(devices.bit_length() - 1) if 1 << k < blocks]
+    while len(bits) > 1:
+        (a, b), bits = bits[:2], bits[2:]
+        mine = (mine + swapped(mine, a ^ b)) + (swapped(mine, a) + swapped(mine, b))
+    for a in bits:
+        mine = mine + swapped(mine, a)
     grad_w_one, grad_w_two = call(
         finish,
         (shape((C_IN, C_ONE, 27), f32), shape((27, C_ONE, C_TWO), f32)),
-        (half, mine, swapped(mine, "dp", 1)),
+        (half, mine, swapped(mine, blocks)),
         scalars=(0,),
     )
     return grad_pooled, jnp.transpose(grad_w_one, (2, 0, 1)), grad_w_two

time: 40.8 us -> 39.5 us (0.968)
  waiting for transfers between devices: 13.1 us -> 11 us
    ppermute x6 -> x8, waiting for transfers between devices: 11.2 us -> 9.32 us  [swapped(): lax.ppermute(array, ('dp', 'space'), [(i, i ^ bits) for i in range(device...]
    ppermute x6 -> x8, starting transfers between devices: 7.55 us -> 8.02 us  [swapped(): lax.ppermute(array, ('dp', 'space'), [(i, i ^ bits) for i in range(device...]
    pallas_call x9 -> x10, Pallas kernels: 9.76 us -> 10.1 us  [call(): pl.pallas_call(body, out_shape=shapes, in_specs=[pl.BlockSpec(memory_spac...]
  transfers between devices with their start and end apart: 12 -> 14, of which waited for: 8 -> 11; matrix products, arithmetic and copies ran while one was open for 0% -> 0% of each run, Pallas kernels for 13% -> 14%
where the time goes in v5:
time: 39.5 us; the launch traced here: 39.3 us
  starting transfers between devices  17.4 us (44%)
  waiting for transfers between devices  11 us (28%)
  Pallas kernels  10.1 us (26%)
  between operations  0.75 us (2%)
    pallas_call x10, Pallas kernels, call(): pl.pallas_call(body, out_shape=shapes, in_specs=[pl.BlockSpec(memory_spac...  10.1 us
    ppermute x6, starting transfers between devices, from_block(): return lax.ppermute(array, 'space', pairs)  9.38 us
    ppermute x8, waiting for transfers between devices, swapped(): lax.ppermute(array, ('dp', 'space'), [(i, i ^ bits) for i in range(device...  9.32 us
    ppermute x8, starting transfers between devices, swapped(): lax.ppermute(array, ('dp', 'space'), [(i, i ^ bits) for i in range(device...  8.02 us
    ppermute x6, waiting for transfers between devices, from_block(): return lax.ppermute(array, 'space', pairs)  1.73 us
  transfers between devices with their start and end apart: 14, of which 11 were waited for; matrix products, arithmetic and copies ran while one was open for 0% of the time, Pallas kernels for 14%

profile of v5, /device:TPU:0, one launch (start us, length us, event | category | flops | bytes accessed | tf_op | source)
XLA Modules:
  0.0 39.3 jit_solution(1014955159637576849)
XLA Ops:
  0.6 0.0 copy-start
  0.6 1.4 %shard_map.103 = (bf16[576,128]{1,0:T(8,128)(2,1)S(1)}, bf16[16,8192]{1,0:T(8,128)(2,1)S(1)}) custom-call(bf16[3,1,32,128]{3,2,1,0:T(8,128)(2,1)} %refs_0_.2, s32[3,1,32,128]{3,2,1,0:T(8,128)} %refs_1_.2, s32[3,1,32,1024]{3,2,1,0:T(8,128)} %refs_2_.3, bf16[3,1,4,8192]{3,2,1,0:T(4,128)(2,1)} %refs_3_.1), custom_call_target="tpu_custom_call" | custom-call | flops 20000000 | bytes 1048576 | tf_op jit(solution)/shard_map/pallas_call | solution.py:440
  2.0 4.1 %collective-permute-start.1 = (bf16[576,128]{1,0:T(8,128)(2,1)S(1)}, bf16[576,128]{1,0:T(8,128)(2,1)S(1)}, u32[]{:S(2)}, u32[]{:S(2)}) collective-permute-start(bf16[576,128]{1,0:T(8,128)(2,1)S(1)} %get-tuple-element.23.to_x.refs_0_), channel_id=1, source_target_pairs={{4,0},{5,1},{6,2},{7,3},{0,4},{1,5},{2,6},{3,7},{12,8},{13,9},{14,... | collective-permute-start | bytes 442376 | tf_op jit(solution)/shard_map/ppermute | solution.py:461
  6.1 0.2 shard_map.104
  6.3 1.6 %collective-permute-start.2 = (bf16[32,128]{1,0:T(8,128)(2,1)S(1)}, bf16[32,128]{1,0:T(8,128)(2,1)S(1)}, u32[]{:S(2)}, u32[]{:S(2)}) collective-permute-start(bf16[32,128]{1,0:T(8,128)(2,1)S(1)} %get-tuple-element.26), channel_id=1, source_target_pairs={{1,0},{0,1},{3,2},{2,3},{5,4},{4,5},{7,6},{6,7},{9,8},{8,9},{11,10... | collective-permute-start | bytes 24584 | tf_op jit(solution)/shard_map/ppermute | solution.py:461
  7.9 0.0 collective-permute-start.4
  7.9 1.9 %collective-permute-start = (bf16[384,128]{1,0:T(8,128)(2,1)S(1)}, bf16[384,128]{1,0:T(8,128)(2,1)S(1)}, u32[]{:S(2)}, u32[]{:S(2)}) collective-permute-start(bf16[384,128]{1,0:T(8,128)(2,1)S(1)} %get-tuple-element.25), channel_id=1, source_target_pairs={{2,0},{3,1},{0,2},{1,3},{6,4},{7,5},{4,6},{5,7},{10,8},{11,9},{8,1... | collective-permute-start | bytes 294920 | tf_op jit(solution)/shard_map/ppermute | solution.py:461
  9.8 2.0 %shard_map.105 = (bf16[48,8192]{1,0:T(8,128)(2,1)S(1)}, bf16[144,96]{1,0:T(8,128)(2,1)S(1)}, bf16[256,768]{1,0:T(8,128)(2,1)S(1)}) custom-call(s32[3,1,16,1024]{3,2,1,0:T(8,128)} %refs_0_.3, s32[3,1,16,8192]{3,2,1,0:T(8,128)} %refs_1_.3, bf16[27,16,32]{2,1,0:T(8,128)(2,1)} %refs_2_.4), custom_call_target="tpu_custom_call" | custom-call | flops 20000000 | bytes 3145728 | tf_op jit(solution)/shard_map/pallas_call | solution.py:440
  11.8 0.0 collective-permute-done.2.refs_1_
  11.8 0.0 copy-done
  11.8 1.4 %shard_map.106 = (f32[48,1024]{1,0:T(8,128)S(1)}, f32[144,96]{1,0:T(8,128)S(1)}, bf16[3,144,1024]{2,1,0:T(8,128)(2,1)S(1)}, bf16[3,144,1024]{2,1,0:T(8,128)(2,1)S(1)}) custom-call(bf16[576,128]{1,0:T(8,128)(2,1)S(1)} %get-tuple-element.23.to_x.refs_0_, bf16[32,128]{1,0:T(8,128)(2,1)S(1)} %collective-permute-done.2.refs_1_, ...), custom_call_target="tpu_custom_call" | custom-call | flops 500000000 | bytes 1048576 | tf_op jit(solution)/shard_map/pallas_call | solution.py:440
  13.2 0.1 collective-permute-done.1.refs_0_
  13.4 0.9 %collective-permute-start.3 = (bf16[288,128]{1,0:T(8,128)(2,1)S(1)}, bf16[288,128]{1,0:T(8,128)(2,1)S(1)}, u32[]{:S(2)}, u32[]{:S(2)}) collective-permute-start(bf16[288,128]{1,0:T(8,128)(2,1)S(1)} %pad_maximum_fusion), channel_id=1, source_target_pairs={{2,0},{3,1},{0,2},{1,3},{6,4},{7,5},{4,6},{5,7},{10,8},{11,9},{8,1... | collective-permute-start | bytes 221192 | tf_op jit(solution)/shard_map/ppermute | solution.py:461
  14.2 0.3 collective-permute-done.4.refs_1_.refs_2_
  14.5 1.0 %collective-permute-start.5 = (bf16[64,128]{1,0:T(8,128)(2,1)S(1)}, bf16[64,128]{1,0:T(8,128)(2,1)S(1)}, u32[]{:S(2)}, u32[]{:S(2)}) collective-permute-start(bf16[64,128]{1,0:T(8,128)(2,1)S(1)} %pad_maximum_fusion.1), channel_id=1, source_target_pairs={{2,0},{3,1},{0,2},{1,3},{6,4},{7,5},{4,6},{5,7},{10,8},{11,9},{8,1... | collective-permute-start | bytes 49160 | tf_op jit(solution)/shard_map/ppermute | solution.py:461
  15.5 0.9 %shard_map.107 = (f32[48,1024]{1,0:T(8,128)S(1)}, f32[144,96]{1,0:T(8,128)S(1)}) custom-call(bf16[576,128]{1,0:T(8,128)(2,1)S(1)} %collective-permute-done.1.refs_0_, bf16[32,128]{1,0:T(8,128)(2,1)S(1)} %collective-permute-done.4.refs_1_.refs_2_, bf16[144,96]{1,0:T(8,128)(2,1)S(1)} %get-tuple-element.27.refs_3_.refs_2_, ...), custom_call_target="tpu_custom_call" | custom-call | flops 500000000 | bytes 1048576 | tf_op jit(solution)/shard_map/pallas_call | solution.py:440
  16.4 0.5 %shard_map.110.refs_4_ = bf16[48,12288]{1,0:T(8,128)(2,1)S(1)} custom-call(bf16[576,128]{1,0:T(8,128)(2,1)S(1)} %collective-permute-done.1.refs_0_, bf16[32,128]{1,0:T(8,128)(2,1)S(1)} %collective-permute-done.2.refs_1_, bf16[32,128]{1,0:T(8,128)(2,1)S(1)} %collective-permute-done.4.refs_1_.refs_2_, bf16[16,8192]{1,0:T(8,128)(2,1)S(1)} %get-tuple-element.24.own.refs_3_), custom_call_target="tpu_custom_call" | custom-call | flops 100000000 | bytes 1048576 | tf_op jit(solution)/shard_map/pallas_call | solution.py:440
  16.9 1.3 %collective-permute-done.5.refs_2_ = bf16[64,128]{1,0:T(8,128)(2,1)S(1)} collective-permute-done((bf16[64,128]{1,0:T(8,128)(2,1)S(1)}, bf16[64,128]{1,0:T(8,128)(2,1)S(1)}, u32[]{:S(2)}, u32[]{:S(2)}) %collective-permute-start.5) | collective-permute-done | bytes 16416 | tf_op jit(solution)/shard_map/ppermute | solution.py:461
  18.2 0.0 collective-permute-done.refs_0_
  18.2 0.0 collective-permute-done.3.refs_1_
  18.3 1.0 %shard_map.108 = (bf16[48,1024]{1,0:T(8,128)(2,1)S(1)}, f32[16,896]{1,0:T(8,128)S(1)}) custom-call(bf16[384,128]{1,0:T(8,128)(2,1)S(1)} %collective-permute-done.refs_0_, bf16[288,128]{1,0:T(8,128)(2,1)S(1)} %collective-permute-done.3.refs_1_, bf16[64,128]{1,0:T(8,128)(2,1)S(1)} %collective-permute-done.5.refs_2_, ...), custom_call_target="tpu_custom_call" | custom-call | flops 500000000 | bytes 1048576 | tf_op jit(solution)/shard_map/pallas_call | solution.py:440
  19.3 1.2 %shard_map.111 = (f32[8,1024]{1,0:T(8,128)S(1)}, f32[8,1024]{1,0:T(8,128)S(1)}) custom-call(bf16[384,128]{1,0:T(8,128)(2,1)S(1)} %collective-permute-done.refs_0_, bf16[288,128]{1,0:T(8,128)(2,1)S(1)} %collective-permute-done.3.refs_1_, bf16[64,128]{1,0:T(8,128)(2,1)S(1)} %collective-permute-done.5.refs_2_, ...), custom_call_target="tpu_custom_call" | custom-call | flops 500000000 | bytes 1048576 | tf_op jit(solution)/shard_map/pallas_call | solution.py:440
  20.5 0.0 collective-permute-start.6
  20.5 1.2 %collective-permute-done.6 = f32[8,1024]{1,0:T(8,128)S(1)} collective-permute-done((f32[8,1024]{1,0:T(8,128)S(1)}, f32[8,1024]{1,0:T(8,128)S(1)}, u32[]{:S(2)}, u32[]{:S(2)}) %collective-permute-start.6) | collective-permute-done | bytes 32800 | tf_op jit(solution)/shard_map/ppermute | solution.py:473
  21.7 2.3 %collective-permute-start.7 = (f32[8,1024]{1,0:T(8,128)S(1)}, f32[8,1024]{1,0:T(8,128)S(1)}, u32[]{:S(2)}, u32[]{:S(2)}) collective-permute-start(f32[8,1024]{1,0:T(8,128)S(1)} %add.26), channel_id=1, source_target_pairs={{0,17},{1,16},{2,19},{3,18},{4,21},{5,20},{6,23},{7,22},{8,25},{9,... | collective-permute-start | bytes 98312 | tf_op jit(solution)/shard_map/ppermute | solution.py:473
  24.0 0.5 %collective-permute-start.8 = (f32[8,1024]{1,0:T(8,128)S(1)}, f32[8,1024]{1,0:T(8,128)S(1)}, u32[]{:S(2)}, u32[]{:S(2)}) collective-permute-start(f32[8,1024]{1,0:T(8,128)S(1)} %add.26), channel_id=1, source_target_pairs={{0,16},{1,17},{2,18},{3,19},{4,20},{5,21},{6,22},{7,23},{8,24},{9,... | collective-permute-start | bytes 98312 | tf_op jit(solution)/shard_map/ppermute | solution.py:473
  24.5 0.7 %collective-permute-start.9 = (f32[8,1024]{1,0:T(8,128)S(1)}, f32[8,1024]{1,0:T(8,128)S(1)}, u32[]{:S(2)}, u32[]{:S(2)}) collective-permute-start(f32[8,1024]{1,0:T(8,128)S(1)} %add.26), channel_id=1, source_target_pairs={{0,1},{1,0},{2,3},{3,2},{4,5},{5,4},{6,7},{7,6},{8,9},{9,8},{10,11... | collective-permute-start | bytes 98312 | tf_op jit(solution)/shard_map/ppermute | solution.py:473
  25.2 1.3 %collective-permute-done.7 = f32[8,1024]{1,0:T(8,128)S(1)} collective-permute-done((f32[8,1024]{1,0:T(8,128)S(1)}, f32[8,1024]{1,0:T(8,128)S(1)}, u32[]{:S(2)}, u32[]{:S(2)}) %collective-permute-start.7) | collective-permute-done | bytes 32800 | tf_op jit(solution)/shard_map/ppermute | solution.py:473
  26.5 1.4 %collective-permute-done.8 = f32[8,1024]{1,0:T(8,128)S(1)} collective-permute-done((f32[8,1024]{1,0:T(8,128)S(1)}, f32[8,1024]{1,0:T(8,128)S(1)}, u32[]{:S(2)}, u32[]{:S(2)}) %collective-permute-start.8) | collective-permute-done | bytes 32800 | tf_op jit(solution)/shard_map/ppermute | solution.py:473
  27.9 0.5 %collective-permute-done.9 = f32[8,1024]{1,0:T(8,128)S(1)} collective-permute-done((f32[8,1024]{1,0:T(8,128)S(1)}, f32[8,1024]{1,0:T(8,128)S(1)}, u32[]{:S(2)}, u32[]{:S(2)}) %collective-permute-start.9) | collective-permute-done | bytes 32800 | tf_op jit(solution)/shard_map/ppermute | solution.py:473
  28.5 3.6 %collective-permute-start.10 = (f32[8,1024]{1,0:T(8,128)S(1)}, f32[8,1024]{1,0:T(8,128)S(1)}, u32[]{:S(2)}, u32[]{:S(2)}) collective-permute-start(f32[8,1024]{1,0:T(8,128)S(1)} %add_add_fusion.1), channel_id=1, source_target_pairs={{0,6},{1,7},{2,4},{3,5},{4,2},{5,3},{6,0},{7,1},{8,14},{9,15},{10,... | collective-permute-start | bytes 98312 | tf_op jit(solution)/shard_map/ppermute | solution.py:473
  32.1 0.4 collective-permute-start.11
  32.4 0.5 %collective-permute-start.12 = (f32[8,1024]{1,0:T(8,128)S(1)}, f32[8,1024]{1,0:T(8,128)S(1)}, u32[]{:S(2)}, u32[]{:S(2)}) collective-permute-start(f32[8,1024]{1,0:T(8,128)S(1)} %add_add_fusion.1), channel_id=1, source_target_pairs={{0,4},{1,5},{2,6},{3,7},{4,0},{5,1},{6,2},{7,3},{8,12},{9,13},{10,... | collective-permute-start | bytes 98312 | tf_op jit(solution)/shard_map/ppermute | solution.py:473
  32.9 1.4 %collective-permute-done.10 = f32[8,1024]{1,0:T(8,128)S(1)} collective-permute-done((f32[8,1024]{1,0:T(8,128)S(1)}, f32[8,1024]{1,0:T(8,128)S(1)}, u32[]{:S(2)}, u32[]{:S(2)}) %collective-permute-start.10) | collective-permute-done | bytes 32800 | tf_op jit(solution)/shard_map/ppermute | solution.py:473
  34.3 1.7 %collective-permute-done.11 = f32[8,1024]{1,0:T(8,128)S(1)} collective-permute-done((f32[8,1024]{1,0:T(8,128)S(1)}, f32[8,1024]{1,0:T(8,128)S(1)}, u32[]{:S(2)}, u32[]{:S(2)}) %collective-permute-start.11) | collective-permute-done | bytes 32800 | tf_op jit(solution)/shard_map/ppermute | solution.py:473
  36.0 1.3 %collective-permute-done.12 = f32[8,1024]{1,0:T(8,128)S(1)} collective-permute-done((f32[8,1024]{1,0:T(8,128)S(1)}, f32[8,1024]{1,0:T(8,128)S(1)}, u32[]{:S(2)}, u32[]{:S(2)}) %collective-permute-start.12) | collective-permute-done | bytes 32800 | tf_op jit(solution)/shard_map/ppermute | solution.py:473
  37.3 0.1 collective-permute-start.13
  37.3 0.6 %shard_map.109 = bf16[3,1,16,1024]{3,2,1,0:T(8,128)(2,1)} custom-call(bf16[48,1024]{1,0:T(8,128)(2,1)S(1)} %get-tuple-element.36.kept.refs_5_), custom_call_target="tpu_custom_call" | custom-call | flops 1000000 | bytes 262144 | tf_op jit(solution)/shard_map/pallas_call | solution.py:440
  38.0 0.5 %collective-permute-done.13.theirs = f32[8,1024]{1,0:T(8,128)S(1)} collective-permute-done((f32[8,1024]{1,0:T(8,128)S(1)}, f32[8,1024]{1,0:T(8,128)S(1)}, u32[]{:S(2)}, u32[]{:S(2)}) %collective-permute-start.13) | collective-permute-done | bytes 32800 | tf_op jit(solution)/shard_map/ppermute | solution.py:473
  38.5 0.8 %shard_map.112 = (f32[4,16,27]{2,1,0:T(8,128)}, f32[27,16,32]{2,1,0:T(8,128)}) custom-call(s32[1]{0:T(128)} %bitcast.refs_8_.half, f32[8,1024]{1,0:T(8,128)S(1)} %add_add_fusion.mine, f32[8,1024]{1,0:T(8,128)S(1)} %collective-permute-done.13.theirs), custom_call_target="tpu_custom_call" | custom-call | tf_op jit(solution)/shard_map/pallas_call | solution.py:440
  (7 shorter events, 0.0 us)
Async XLA Ops:
  0.6 11.1 %copy-start = (bf16[3,1,16,1024]{3,2,1,0:T(8,128)(2,1)S(1)}, bf16[3,1,16,1024]{3,2,1,0:T(8,128)(2,1)}, u32[]{:S(2)}) copy-start(bf16[3,1,16,1024]{3,2,1,0:T(8,128)(2,1)} %refs_2_.5) | copy-start | bytes 294916
  2.0 11.3 %collective-permute-start.1 = (bf16[576,128]{1,0:T(8,128)(2,1)S(1)}, bf16[576,128]{1,0:T(8,128)(2,1)S(1)}, u32[]{:S(2)}, u32[]{:S(2)}) collective-permute-start(bf16[576,128]{1,0:T(8,128)(2,1)S(1)} %get-tuple-element.23.to_x.refs_0_), channel_id=1, source_target_pairs={{4,0},{5,1},{6,2},{7,3},{0,4},{1,5},{2,6},{3,7},{12,8},{13,9},{14,... | collective-permute-start | bytes 442376 | tf_op jit(solution)/shard_map/ppermute | solution.py:461
  6.3 5.4 %collective-permute-start.2 = (bf16[32,128]{1,0:T(8,128)(2,1)S(1)}, bf16[32,128]{1,0:T(8,128)(2,1)S(1)}, u32[]{:S(2)}, u32[]{:S(2)}) collective-permute-start(bf16[32,128]{1,0:T(8,128)(2,1)S(1)} %get-tuple-element.26), channel_id=1, source_target_pairs={{1,0},{0,1},{3,2},{2,3},{5,4},{4,5},{7,6},{6,7},{9,8},{8,9},{11,10... | collective-permute-start | bytes 24584 | tf_op jit(solution)/shard_map/ppermute | solution.py:461
  7.9 6.6 %collective-permute-start.4 = (bf16[32,128]{1,0:T(8,128)(2,1)S(1)}, bf16[32,128]{1,0:T(8,128)(2,1)S(1)}, u32[]{:S(2)}, u32[]{:S(2)}) collective-permute-start(bf16[32,128]{1,0:T(8,128)(2,1)S(1)} %get-tuple-element.26), channel_id=1, source_target_pairs={{5,0},{4,1},{7,2},{6,3},{1,4},{0,5},{3,6},{2,7},{13,8},{12,9},{15,... | collective-permute-start | bytes 24584 | tf_op jit(solution)/shard_map/ppermute | solution.py:461
  7.9 10.3 %collective-permute-start = (bf16[384,128]{1,0:T(8,128)(2,1)S(1)}, bf16[384,128]{1,0:T(8,128)(2,1)S(1)}, u32[]{:S(2)}, u32[]{:S(2)}) collective-permute-start(bf16[384,128]{1,0:T(8,128)(2,1)S(1)} %get-tuple-element.25), channel_id=1, source_target_pairs={{2,0},{3,1},{0,2},{1,3},{6,4},{7,5},{4,6},{5,7},{10,8},{11,9},{8,1... | collective-permute-start | bytes 294920 | tf_op jit(solution)/shard_map/ppermute | solution.py:461
  13.4 4.9 %collective-permute-start.3 = (bf16[288,128]{1,0:T(8,128)(2,1)S(1)}, bf16[288,128]{1,0:T(8,128)(2,1)S(1)}, u32[]{:S(2)}, u32[]{:S(2)}) collective-permute-start(bf16[288,128]{1,0:T(8,128)(2,1)S(1)} %pad_maximum_fusion), channel_id=1, source_target_pairs={{2,0},{3,1},{0,2},{1,3},{6,4},{7,5},{4,6},{5,7},{10,8},{11,9},{8,1... | collective-permute-start | bytes 221192 | tf_op jit(solution)/shard_map/ppermute | solution.py:461
  14.5 3.7 %collective-permute-start.5 = (bf16[64,128]{1,0:T(8,128)(2,1)S(1)}, bf16[64,128]{1,0:T(8,128)(2,1)S(1)}, u32[]{:S(2)}, u32[]{:S(2)}) collective-permute-start(bf16[64,128]{1,0:T(8,128)(2,1)S(1)} %pad_maximum_fusion.1), channel_id=1, source_target_pairs={{2,0},{3,1},{0,2},{1,3},{6,4},{7,5},{4,6},{5,7},{10,8},{11,9},{8,1... | collective-permute-start | bytes 49160 | tf_op jit(solution)/shard_map/ppermute | solution.py:461
  20.5 1.2 %collective-permute-start.6 = (f32[8,1024]{1,0:T(8,128)S(1)}, f32[8,1024]{1,0:T(8,128)S(1)}, u32[]{:S(2)}, u32[]{:S(2)}) collective-permute-start(f32[8,1024]{1,0:T(8,128)S(1)} %get-tuple-element.40), channel_id=1, source_target_pairs={{0,8},{1,9},{2,10},{3,11},{4,12},{5,13},{6,14},{7,15},{8,0},{9,1},... | collective-permute-start | bytes 98312 | tf_op jit(solution)/shard_map/ppermute | solution.py:473
  21.7 4.8 %collective-permute-start.7 = (f32[8,1024]{1,0:T(8,128)S(1)}, f32[8,1024]{1,0:T(8,128)S(1)}, u32[]{:S(2)}, u32[]{:S(2)}) collective-permute-start(f32[8,1024]{1,0:T(8,128)S(1)} %add.26), channel_id=1, source_target_pairs={{0,17},{1,16},{2,19},{3,18},{4,21},{5,20},{6,23},{7,22},{8,25},{9,... | collective-permute-start | bytes 98312 | tf_op jit(solution)/shard_map/ppermute | solution.py:473
  24.0 3.9 %collective-permute-start.8 = (f32[8,1024]{1,0:T(8,128)S(1)}, f32[8,1024]{1,0:T(8,128)S(1)}, u32[]{:S(2)}, u32[]{:S(2)}) collective-permute-start(f32[8,1024]{1,0:T(8,128)S(1)} %add.26), channel_id=1, source_target_pairs={{0,16},{1,17},{2,18},{3,19},{4,20},{5,21},{6,22},{7,23},{8,24},{9,... | collective-permute-start | bytes 98312 | tf_op jit(solution)/shard_map/ppermute | solution.py:473
  24.5 3.9 %collective-permute-start.9 = (f32[8,1024]{1,0:T(8,128)S(1)}, f32[8,1024]{1,0:T(8,128)S(1)}, u32[]{:S(2)}, u32[]{:S(2)}) collective-permute-start(f32[8,1024]{1,0:T(8,128)S(1)} %add.26), channel_id=1, source_target_pairs={{0,1},{1,0},{2,3},{3,2},{4,5},{5,4},{6,7},{7,6},{8,9},{9,8},{10,11... | collective-permute-start | bytes 98312 | tf_op jit(solution)/shard_map/ppermute | solution.py:473
  28.5 5.9 %collective-permute-start.10 = (f32[8,1024]{1,0:T(8,128)S(1)}, f32[8,1024]{1,0:T(8,128)S(1)}, u32[]{:S(2)}, u32[]{:S(2)}) collective-permute-start(f32[8,1024]{1,0:T(8,128)S(1)} %add_add_fusion.1), channel_id=1, source_target_pairs={{0,6},{1,7},{2,4},{3,5},{4,2},{5,3},{6,0},{7,1},{8,14},{9,15},{10,... | collective-permute-start | bytes 98312 | tf_op jit(solution)/shard_map/ppermute | solution.py:473
  32.1 3.9 %collective-permute-start.11 = (f32[8,1024]{1,0:T(8,128)S(1)}, f32[8,1024]{1,0:T(8,128)S(1)}, u32[]{:S(2)}, u32[]{:S(2)}) collective-permute-start(f32[8,1024]{1,0:T(8,128)S(1)} %add_add_fusion.1), channel_id=1, source_target_pairs={{0,2},{1,3},{2,0},{3,1},{4,6},{5,7},{6,4},{7,5},{8,10},{9,11},{10,... | collective-permute-start | bytes 98312 | tf_op jit(solution)/shard_map/ppermute | solution.py:473
  32.4 4.8 %collective-permute-start.12 = (f32[8,1024]{1,0:T(8,128)S(1)}, f32[8,1024]{1,0:T(8,128)S(1)}, u32[]{:S(2)}, u32[]{:S(2)}) collective-permute-start(f32[8,1024]{1,0:T(8,128)S(1)} %add_add_fusion.1), channel_id=1, source_target_pairs={{0,4},{1,5},{2,6},{3,7},{4,0},{5,1},{6,2},{7,3},{8,12},{9,13},{10,... | collective-permute-start | bytes 98312 | tf_op jit(solution)/shard_map/ppermute | solution.py:473
  37.3 1.3 %collective-permute-start.13 = (f32[8,1024]{1,0:T(8,128)S(1)}, f32[8,1024]{1,0:T(8,128)S(1)}, u32[]{:S(2)}, u32[]{:S(2)}) collective-permute-start(f32[8,1024]{1,0:T(8,128)S(1)} %add_add_fusion.mine), channel_id=1, source_target_pairs={{0,8},{1,9},{2,10},{3,11},{4,12},{5,13},{6,14},{7,15},{8,0},{9,1},... | collective-permute-start | bytes 98312 | tf_op jit(solution)/shard_map/ppermute | solution.py:473

commit v6 on v5

--- a/solution.py
+++ b/solution.py
@@ -204,12 +204,14 @@
     return {(px, py): (px - 1) * HY + py - 1 for px in range(1, HX + 1) for py in range(1, HY + 1)}
 
 
-def tiles_x():
-    return {(px, py): (px > 0) * HY + py - 1 for px in (0, HX + 1) for py in range(1, HY + 1)}
-
-
-def tiles_ends():
-    return {(px, py): 2 * px + (py > 0) for px in range(HX + 2) for py in (0, HY + 1)}
+def tiles_sides():
+    tiles = [(px, py) for px in (0, HX + 1) for py in range(1, HY + 1)]
+    tiles += [(px, py) for px in range(1, HX + 1) for py in (0, HY + 1)]
+    return {key: i for i, key in enumerate(tiles)}
+
+
+def tiles_corners():
+    return {(px, py): 2 * (px > 0) + (py > 0) for px in (0, HX + 1) for py in (0, HY + 1)}
 
 
 def shift_pooled(samples, tile_of, pooled, moved):
@@ -266,31 +268,31 @@
 
 
 def layer_two_own(samples, vp_at, edge_at, *refs):
-    blocks, (pooled, weights, expand, part, total, moved_x, moved_ends, fields, moved) = refs[:-9], refs[-9:]
+    blocks, (pooled, weights, expand, part, total, fields, moved) = refs[:-7], refs[-7:]
     tile_of = tiles_own()
     expand_windows(samples, vp_at, edge_at, tile_of, blocks, expand, fields)
     shift_pooled(samples, tile_of, pooled, moved)
-    shift_pooled(samples, tiles_x(), pooled, moved_x)
-    shift_pooled(samples, tiles_ends(), pooled, moved_ends)
     sums = [{} for _ in range(samples)]
     totals = jnp.zeros((9 * C_ONE, 3 * C_TWO), f32)
     total[...] = products_two(samples, tile_of, fields, moved, weights, sums, totals)
     store_parts(sums, part)
 
 
-def layer_two_x(samples, vp_at, edge_at, *refs):
-    blocks, (weights, expand, old, old_total, moved, part, total, fields) = refs[:-8], refs[-8:]
-    tile_of = tiles_x()
+def layer_two_sides(samples, vp_at, edge_at, *refs):
+    blocks, (pooled, weights, expand, old, old_total, part, total, fields, moved) = refs[:-9], refs[-9:]
+    tile_of = tiles_sides()
     expand_windows(samples, vp_at, edge_at, tile_of, blocks, expand, fields)
+    shift_pooled(samples, tile_of, pooled, moved)
     sums = parts_of(samples, old)
     total[...] = products_two(samples, tile_of, fields, moved, weights, sums, old_total[...])
     store_parts(sums, part)
 
 
-def layer_two_ends(samples, scale, vp_at, edge_at, *refs):
-    blocks, (weights, expand, part, total, moved, kept, message, fields) = refs[:-8], refs[-8:]
-    tile_of = tiles_ends()
+def layer_two_corners(samples, scale, vp_at, edge_at, *refs):
+    blocks, (pooled, weights, expand, part, total, kept, message, fields, moved) = refs[:-9], refs[-9:]
+    tile_of = tiles_corners()
     expand_windows(samples, vp_at, edge_at, tile_of, blocks, expand, fields)
+    shift_pooled(samples, tile_of, pooled, moved)
     sums = parts_of(samples, part)
     totals = products_two(samples, tile_of, fields, moved, weights, sums, total[...]) * scale
     store_parts(sums, kept)
@@ -546,26 +548,25 @@
         edge_x = {nz: {nx: diagonal for nx in (-1, 1)} for nz in (-1, 1)}
     else:
         edge_x = {nz: {nx: from_block(edge, side, nx, 0, nz) for nx in (-1, 1)} for nz in (-1, 1)}
-    first = both_sides(to_y, side, 1)
-    end_tiles, x_tiles = (HX + 2) * 2, 2 * HY
+    first, first_starts = stacked([to_y, edge_z[-1], edge_z[1]])
+    first = both_sides(first, side, 1)
+    side_tiles, corner_tiles = len(tiles_sides()), len(tiles_corners())
     part_shape = shape((samples * C_ONE, half_cells), f32)
     total_shape = shape((9 * C_ONE, 3 * C_TWO), f32)
     arrays, tables = operands_of({(0, 0): vp_at[0, 0]}, {(0, 0, n): (edge_z[n], 0) for n in (-1, 1)})
-    part, total_two, moved_x, moved_ends = call(
+    part, total_two = call(
         functools.partial(layer_two_own, samples, *tables),
         (
             part_shape,
             total_shape,
-            shape((samples, 9 * C_ONE, x_tiles * LANES), bf16),
-            shape((samples, 9 * C_ONE, end_tiles * LANES), bf16),
         ),
         (*arrays, pooled_one, folded_weights, expand),
         scratch=(
             pltpu.VMEM((samples, 3 * C_TWO, half_cells), bf16),
             pltpu.VMEM((samples, 9 * C_ONE, half_cells), bf16),
         ),
-        flops=5 * 10**8,
-        moved=2**20,
+        flops=1000,
+        moved=1000,
     )
     ready = {n: lax.optimization_barrier((from_x[n], total_two))[0] for n in ((-1,) if side == 2 else (-1, 1))}
     parts = []
@@ -574,8 +575,7 @@
         parts += parts[:2] if again else [ready[n][vp_row:], ready[n][: 2 * four]]
     second, starts = stacked(parts)
     second = both_sides(second, side, 1)
-    parts = [edge_z[-1], edge_z[1]] + [edge_x[nz][nx] for nz in (-1, 1) for nx in (-1, 1)]
-    third, edge_starts = stacked(parts)
+    third, edge_starts = stacked([edge_z[-1], edge_z[1]] + [edge_x[nz][nx] for nz in (-1, 1) for nx in (-1, 1)])
     third = both_sides(third, side, 1)
     for n in (-1, 1):
         vp_at[n, 0] = (from_x[n], vp_row)
@@ -588,7 +588,7 @@
             vp_at[nx, n] = (second[n], starts[2 * i])
             line_at[nx, n] = (second[n], starts[2 * i + 1])
         for i, nz in enumerate((-1, 1)):
-            edge_at[0, n, nz] = (third[n], edge_starts[i])
+            edge_at[0, n, nz] = (first[n], first_starts[1 + i])
             for j, nx in enumerate((-1, 1)):
                 edge_at[nx, n, nz] = (third[n], edge_starts[2 + 2 * i + j])
     total = lax.axis_size("dp") * samples * blocks * cells
@@ -597,15 +597,19 @@
         return {key: value for key, value in table.items() if key[1] in y}
 
     arrays, tables = operands_of(
-        {(n, 0): vp_at[n, 0] for n in (-1, 1)}, {key: edge_at[key] for key in edge_at if key[0] != 0 and key[1] == 0}
+        {key: value for key, value in vp_at.items() if (key[0] == 0) != (key[1] == 0)},
+        {key: value for key, value in edge_at.items() if (key[0] == 0) != (key[1] == 0)},
     )
     part, total_two = call(
-        functools.partial(layer_two_x, samples, *tables),
+        functools.partial(layer_two_sides, samples, *tables),
         (part_shape, total_shape),
-        (*arrays, folded_weights, expand, part, total_two, moved_x),
-        scratch=(pltpu.VMEM((samples, 3 * C_TWO, x_tiles * LANES), bf16),),
-        flops=5 * 10**8,
-        moved=2**20,
+        (*arrays, pooled_one, folded_weights, expand, part, total_two),
+        scratch=(
+            pltpu.VMEM((samples, 3 * C_TWO, side_tiles * LANES), bf16),
+            pltpu.VMEM((samples, 9 * C_ONE, side_tiles * LANES), bf16),
+        ),
+        flops=1000,
+        moved=1000,
     )
     arrays, tables = operands_of(face_at, near(edge_at, (0,)))
     ahead = call(
@@ -615,15 +619,21 @@
         flops=10**8,
         moved=2**20,
     )
-    arrays, tables = operands_of(near(vp_at, (-1, 1)), near(edge_at, (-1, 1)))
+    arrays, tables = operands_of(
+        {key: value for key, value in vp_at.items() if key[0] != 0 and key[1] != 0},
+        {key: value for key, value in edge_at.items() if key[0] != 0 and key[1] != 0},
+    )
     kept, sums = call(
-        functools.partial(layer_two_ends, samples, float(total // 8) ** -0.5, *tables),
+        functools.partial(layer_two_corners, samples, float(total // 8) ** -0.5, *tables),
         (
             shape((samples * C_ONE, half_cells), bf16),
             shape((C_ONE, ONE_AT), f32),
         ),
-        (*arrays, folded_weights, expand, part, total_two, moved_ends),
-        scratch=(pltpu.VMEM((samples, 3 * C_TWO, end_tiles * LANES), bf16),),
+        (*arrays, pooled_one, folded_weights, expand, part, total_two),
+        scratch=(
+            pltpu.VMEM((samples, 3 * C_TWO, corner_tiles * LANES), bf16),
+            pltpu.VMEM((samples, 9 * C_ONE, corner_tiles * LANES), bf16),
+        ),
         flops=5 * 10**8,
         moved=2**20,
     )

time: 39.5 us -> 39.2 us (level)
  transfers between devices with their start and end apart: 14 -> 14, of which waited for: 11 -> 13; matrix products, arithmetic and copies ran while one was open for 0% -> 0% of each run, Pallas kernels for 14% -> 15%
where the time goes in v6:
time: 39.2 us; the launch traced here: 39 us
  starting transfers between devices  17.3 us (44%)
  waiting for transfers between devices  11.1 us (28%)
  Pallas kernels  9.87 us (25%)
  between operations  0.74 us (2%)
    pallas_call x10, Pallas kernels, call(): pl.pallas_call(body, out_shape=shapes, in_specs=[pl.BlockSpec(memory_spac...  9.87 us
    ppermute x8, waiting for transfers between devices, swapped(): lax.ppermute(array, ('dp', 'space'), [(i, i ^ bits) for i in range(device...  9.34 us
    ppermute x6, starting transfers between devices, from_block(): return lax.ppermute(array, 'space', pairs)  9.27 us
    ppermute x8, starting transfers between devices, swapped(): lax.ppermute(array, ('dp', 'space'), [(i, i ^ bits) for i in range(device...  8.02 us
    ppermute x6, waiting for transfers between devices, from_block(): return lax.ppermute(array, 'space', pairs)  1.73 us
  transfers between devices with their start and end apart: 14, of which 13 were waited for; matrix products, arithmetic and copies ran while one was open for 0% of the time, Pallas kernels for 15%

profile of v6, /device:TPU:0, one launch (start us, length us, event | category | flops | bytes accessed | tf_op | source)
XLA Modules:
  0.0 39.0 jit_solution(6667480679953258334)
XLA Ops:
  0.6 0.0 copy-start
  0.6 1.4 %shard_map.103 = (bf16[576,128]{1,0:T(8,128)(2,1)S(1)}, bf16[16,8192]{1,0:T(8,128)(2,1)S(1)}) custom-call(bf16[3,1,32,128]{3,2,1,0:T(8,128)(2,1)} %refs_0_.2, s32[3,1,32,128]{3,2,1,0:T(8,128)} %refs_1_.2, s32[3,1,32,1024]{3,2,1,0:T(8,128)} %refs_2_.4, bf16[3,1,4,8192]{3,2,1,0:T(4,128)(2,1)} %refs_3_.2), custom_call_target="tpu_custom_call" | custom-call | flops 20000000 | bytes 1048576 | tf_op jit(solution)/shard_map/pallas_call | solution.py:442
  2.0 4.1 %collective-permute-start = (bf16[576,128]{1,0:T(8,128)(2,1)S(1)}, bf16[576,128]{1,0:T(8,128)(2,1)S(1)}, u32[]{:S(2)}, u32[]{:S(2)}) collective-permute-start(bf16[576,128]{1,0:T(8,128)(2,1)S(1)} %get-tuple-element.21.to_x.refs_0_), channel_id=1, source_target_pairs={{4,0},{5,1},{6,2},{7,3},{0,4},{1,5},{2,6},{3,7},{12,8},{13,9},{14,... | collective-permute-start | bytes 442376 | tf_op jit(solution)/shard_map/ppermute | solution.py:463
  6.1 0.2 shard_map.104
  6.3 1.6 %collective-permute-start.1 = (bf16[32,128]{1,0:T(8,128)(2,1)S(1)}, bf16[32,128]{1,0:T(8,128)(2,1)S(1)}, u32[]{:S(2)}, u32[]{:S(2)}) collective-permute-start(bf16[32,128]{1,0:T(8,128)(2,1)S(1)} %get-tuple-element.23), channel_id=1, source_target_pairs={{1,0},{0,1},{3,2},{2,3},{5,4},{4,5},{7,6},{6,7},{9,8},{8,9},{11,10... | collective-permute-start | bytes 24584 | tf_op jit(solution)/shard_map/ppermute | solution.py:463
  7.9 0.0 collective-permute-start.3
  7.9 2.0 %shard_map.105 = (bf16[48,8192]{1,0:T(8,128)(2,1)S(1)}, bf16[144,96]{1,0:T(8,128)(2,1)S(1)}, bf16[256,768]{1,0:T(8,128)(2,1)S(1)}) custom-call(s32[3,1,16,1024]{3,2,1,0:T(8,128)} %refs_0_.3, s32[3,1,16,8192]{3,2,1,0:T(8,128)} %refs_1_.3, bf16[27,16,32]{2,1,0:T(8,128)(2,1)} %refs_2_.5), custom_call_target="tpu_custom_call" | custom-call | flops 20000000 | bytes 3145728 | tf_op jit(solution)/shard_map/pallas_call | solution.py:442
  9.9 0.2 collective-permute-done.1.refs_1_
  10.1 1.8 %collective-permute-start.5 = (bf16[416,128]{1,0:T(8,128)(2,1)S(1)}, bf16[416,128]{1,0:T(8,128)(2,1)S(1)}, u32[]{:S(2)}, u32[]{:S(2)}) collective-permute-start(bf16[416,128]{1,0:T(8,128)(2,1)S(1)} %pad_maximum_fusion), channel_id=1, source_target_pairs={{2,0},{3,1},{0,2},{1,3},{6,4},{7,5},{4,6},{5,7},{10,8},{11,9},{8,1... | collective-permute-start | bytes 319496 | tf_op jit(solution)/shard_map/ppermute | solution.py:463
  11.9 0.0 copy-done
  11.9 1.1 %shard_map.106 = (f32[48,1024]{1,0:T(8,128)S(1)}, f32[144,96]{1,0:T(8,128)S(1)}) custom-call(bf16[576,128]{1,0:T(8,128)(2,1)S(1)} %get-tuple-element.21.to_x.refs_0_, bf16[32,128]{1,0:T(8,128)(2,1)S(1)} %collective-permute-done.1.refs_1_, bf16[3,1,16,1024]{3,2,1,0:T(8,128)(2,1)S(1)} %copy-done, bf16[144,96]{1,0:T(8,128)(2,1)S(1)} %get-tuple-element.24.refs_3_.refs_4_, ...), custom_call_target="tpu_custom_call" | custom-call | flops 1000 | bytes 1000 | tf_op jit(solution)/shard_map/pallas_call | solution.py:442
  12.9 0.5 %collective-permute-done.refs_0_ = bf16[576,128]{1,0:T(8,128)(2,1)S(1)} collective-permute-done((bf16[576,128]{1,0:T(8,128)(2,1)S(1)}, bf16[576,128]{1,0:T(8,128)(2,1)S(1)}, u32[]{:S(2)}, u32[]{:S(2)}) %collective-permute-start) | collective-permute-done | bytes 147488 | tf_op jit(solution)/shard_map/ppermute | solution.py:463
  13.4 0.8 %collective-permute-start.2 = (bf16[288,128]{1,0:T(8,128)(2,1)S(1)}, bf16[288,128]{1,0:T(8,128)(2,1)S(1)}, u32[]{:S(2)}, u32[]{:S(2)}) collective-permute-start(bf16[288,128]{1,0:T(8,128)(2,1)S(1)} %pad_maximum_fusion.1), channel_id=1, source_target_pairs={{2,0},{3,1},{0,2},{1,3},{6,4},{7,5},{4,6},{5,7},{10,8},{11,9},{8,1... | collective-permute-start | bytes 221192 | tf_op jit(solution)/shard_map/ppermute | solution.py:463
  14.2 0.3 collective-permute-done.3.refs_2_
  14.5 1.1 %collective-permute-start.4 = (bf16[64,128]{1,0:T(8,128)(2,1)S(1)}, bf16[64,128]{1,0:T(8,128)(2,1)S(1)}, u32[]{:S(2)}, u32[]{:S(2)}) collective-permute-start(bf16[64,128]{1,0:T(8,128)(2,1)S(1)} %pad_maximum_fusion.2), channel_id=1, source_target_pairs={{2,0},{3,1},{0,2},{1,3},{6,4},{7,5},{4,6},{5,7},{10,8},{11,9},{8,1... | collective-permute-start | bytes 49160 | tf_op jit(solution)/shard_map/ppermute | solution.py:463
  15.5 0.4 %collective-permute-done.5.refs_1_.refs_0_ = bf16[416,128]{1,0:T(8,128)(2,1)S(1)} collective-permute-done((bf16[416,128]{1,0:T(8,128)(2,1)S(1)}, bf16[416,128]{1,0:T(8,128)(2,1)S(1)}, u32[]{:S(2)}, u32[]{:S(2)}) %collective-permute-start.5) | collective-permute-done | bytes 106528 | tf_op jit(solution)/shard_map/ppermute | solution.py:463
  16.0 1.4 %shard_map.107 = (f32[48,1024]{1,0:T(8,128)S(1)}, f32[144,96]{1,0:T(8,128)S(1)}) custom-call(bf16[576,128]{1,0:T(8,128)(2,1)S(1)} %collective-permute-done.refs_0_, bf16[416,128]{1,0:T(8,128)(2,1)S(1)} %collective-permute-done.5.refs_1_.refs_0_, bf16[32,128]{1,0:T(8,128)(2,1)S(1)} %collective-permute-done.3.refs_2_, bf16[3,1,16,1024]{3,2,1,0:T(8,128)(2,1)S(1)} %copy-done, ...), custom_call_target="tpu_custom_call" | custom-call | flops 1000 | bytes 1000 | tf_op jit(solution)/shard_map/pallas_call | solution.py:442
  17.4 0.5 %shard_map.110.refs_4_ = bf16[48,12288]{1,0:T(8,128)(2,1)S(1)} custom-call(bf16[576,128]{1,0:T(8,128)(2,1)S(1)} %collective-permute-done.refs_0_, bf16[32,128]{1,0:T(8,128)(2,1)S(1)} %collective-permute-done.1.refs_1_, bf16[32,128]{1,0:T(8,128)(2,1)S(1)} %collective-permute-done.3.refs_2_, bf16[16,8192]{1,0:T(8,128)(2,1)S(1)} %get-tuple-element.22.own.refs_3_), custom_call_target="tpu_custom_call" | custom-call | flops 100000000 | bytes 1048576 | tf_op jit(solution)/shard_map/pallas_call | solution.py:442
  17.8 0.4 collective-permute-done.4.refs_1_.refs_2_
  18.2 0.0 collective-permute-done.2.refs_0_.refs_1_
  18.2 0.7 %shard_map.108 = (bf16[48,1024]{1,0:T(8,128)(2,1)S(1)}, f32[16,896]{1,0:T(8,128)S(1)}) custom-call(bf16[288,128]{1,0:T(8,128)(2,1)S(1)} %collective-permute-done.2.refs_0_.refs_1_, bf16[64,128]{1,0:T(8,128)(2,1)S(1)} %collective-permute-done.4.refs_1_.refs_2_, bf16[3,1,16,1024]{3,2,1,0:T(8,128)(2,1)S(1)} %copy-done, ...), custom_call_target="tpu_custom_call" | custom-call | flops 500000000 | bytes 1048576 | tf_op jit(solution)/shard_map/pallas_call | solution.py:442
  18.9 1.2 %shard_map.111 = (f32[8,1024]{1,0:T(8,128)S(1)}, f32[8,1024]{1,0:T(8,128)S(1)}) custom-call(bf16[416,128]{1,0:T(8,128)(2,1)S(1)} %collective-permute-done.5.refs_1_.refs_0_, bf16[288,128]{1,0:T(8,128)(2,1)S(1)} %collective-permute-done.2.refs_0_.refs_1_, bf16[64,128]{1,0:T(8,128)(2,1)S(1)} %collective-permute-done.4.refs_1_.refs_2_, ...), custom_call_target="tpu_custom_call" | custom-call | flops 500000000 | bytes 1048576 | tf_op jit(solution)/shard_map/pallas_call | solution.py:442
  20.1 0.0 collective-permute-start.6
  20.2 1.2 %collective-permute-done.6 = f32[8,1024]{1,0:T(8,128)S(1)} collective-permute-done((f32[8,1024]{1,0:T(8,128)S(1)}, f32[8,1024]{1,0:T(8,128)S(1)}, u32[]{:S(2)}, u32[]{:S(2)}) %collective-permute-start.6) | collective-permute-done | bytes 32800 | tf_op jit(solution)/shard_map/ppermute | solution.py:475
  21.4 2.3 %collective-permute-start.7 = (f32[8,1024]{1,0:T(8,128)S(1)}, f32[8,1024]{1,0:T(8,128)S(1)}, u32[]{:S(2)}, u32[]{:S(2)}) collective-permute-start(f32[8,1024]{1,0:T(8,128)S(1)} %add.26), channel_id=1, source_target_pairs={{0,17},{1,16},{2,19},{3,18},{4,21},{5,20},{6,23},{7,22},{8,25},{9,... | collective-permute-start | bytes 98312 | tf_op jit(solution)/shard_map/ppermute | solution.py:475
  23.7 0.5 %collective-permute-start.8 = (f32[8,1024]{1,0:T(8,128)S(1)}, f32[8,1024]{1,0:T(8,128)S(1)}, u32[]{:S(2)}, u32[]{:S(2)}) collective-permute-start(f32[8,1024]{1,0:T(8,128)S(1)} %add.26), channel_id=1, source_target_pairs={{0,16},{1,17},{2,18},{3,19},{4,20},{5,21},{6,22},{7,23},{8,24},{9,... | collective-permute-start | bytes 98312 | tf_op jit(solution)/shard_map/ppermute | solution.py:475
  24.2 0.7 %collective-permute-start.9 = (f32[8,1024]{1,0:T(8,128)S(1)}, f32[8,1024]{1,0:T(8,128)S(1)}, u32[]{:S(2)}, u32[]{:S(2)}) collective-permute-start(f32[8,1024]{1,0:T(8,128)S(1)} %add.26), channel_id=1, source_target_pairs={{0,1},{1,0},{2,3},{3,2},{4,5},{5,4},{6,7},{7,6},{8,9},{9,8},{10,11... | collective-permute-start | bytes 98312 | tf_op jit(solution)/shard_map/ppermute | solution.py:475
  24.9 1.3 %collective-permute-done.7 = f32[8,1024]{1,0:T(8,128)S(1)} collective-permute-done((f32[8,1024]{1,0:T(8,128)S(1)}, f32[8,1024]{1,0:T(8,128)S(1)}, u32[]{:S(2)}, u32[]{:S(2)}) %collective-permute-start.7) | collective-permute-done | bytes 32800 | tf_op jit(solution)/shard_map/ppermute | solution.py:475
  26.2 1.4 %collective-permute-done.8 = f32[8,1024]{1,0:T(8,128)S(1)} collective-permute-done((f32[8,1024]{1,0:T(8,128)S(1)}, f32[8,1024]{1,0:T(8,128)S(1)}, u32[]{:S(2)}, u32[]{:S(2)}) %collective-permute-start.8) | collective-permute-done | bytes 32800 | tf_op jit(solution)/shard_map/ppermute | solution.py:475
  27.6 0.5 %collective-permute-done.9 = f32[8,1024]{1,0:T(8,128)S(1)} collective-permute-done((f32[8,1024]{1,0:T(8,128)S(1)}, f32[8,1024]{1,0:T(8,128)S(1)}, u32[]{:S(2)}, u32[]{:S(2)}) %collective-permute-start.9) | collective-permute-done | bytes 32800 | tf_op jit(solution)/shard_map/ppermute | solution.py:475
  28.1 3.6 %collective-permute-start.10 = (f32[8,1024]{1,0:T(8,128)S(1)}, f32[8,1024]{1,0:T(8,128)S(1)}, u32[]{:S(2)}, u32[]{:S(2)}) collective-permute-start(f32[8,1024]{1,0:T(8,128)S(1)} %add_add_fusion.1), channel_id=1, source_target_pairs={{0,6},{1,7},{2,4},{3,5},{4,2},{5,3},{6,0},{7,1},{8,14},{9,15},{10,... | collective-permute-start | bytes 98312 | tf_op jit(solution)/shard_map/ppermute | solution.py:475
  31.8 0.3 collective-permute-start.11
  32.1 0.5 %collective-permute-start.12 = (f32[8,1024]{1,0:T(8,128)S(1)}, f32[8,1024]{1,0:T(8,128)S(1)}, u32[]{:S(2)}, u32[]{:S(2)}) collective-permute-start(f32[8,1024]{1,0:T(8,128)S(1)} %add_add_fusion.1), channel_id=1, source_target_pairs={{0,4},{1,5},{2,6},{3,7},{4,0},{5,1},{6,2},{7,3},{8,12},{9,13},{10,... | collective-permute-start | bytes 98312 | tf_op jit(solution)/shard_map/ppermute | solution.py:475
  32.6 1.4 %collective-permute-done.10 = f32[8,1024]{1,0:T(8,128)S(1)} collective-permute-done((f32[8,1024]{1,0:T(8,128)S(1)}, f32[8,1024]{1,0:T(8,128)S(1)}, u32[]{:S(2)}, u32[]{:S(2)}) %collective-permute-start.10) | collective-permute-done | bytes 32800 | tf_op jit(solution)/shard_map/ppermute | solution.py:475
  34.0 1.7 %collective-permute-done.11 = f32[8,1024]{1,0:T(8,128)S(1)} collective-permute-done((f32[8,1024]{1,0:T(8,128)S(1)}, f32[8,1024]{1,0:T(8,128)S(1)}, u32[]{:S(2)}, u32[]{:S(2)}) %collective-permute-start.11) | collective-permute-done | bytes 32800 | tf_op jit(solution)/shard_map/ppermute | solution.py:475
  35.7 1.2 %collective-permute-done.12 = f32[8,1024]{1,0:T(8,128)S(1)} collective-permute-done((f32[8,1024]{1,0:T(8,128)S(1)}, f32[8,1024]{1,0:T(8,128)S(1)}, u32[]{:S(2)}, u32[]{:S(2)}) %collective-permute-start.12) | collective-permute-done | bytes 32800 | tf_op jit(solution)/shard_map/ppermute | solution.py:475
  36.9 0.1 collective-permute-start.13
  37.0 0.6 %shard_map.109 = bf16[3,1,16,1024]{3,2,1,0:T(8,128)(2,1)} custom-call(bf16[48,1024]{1,0:T(8,128)(2,1)S(1)} %get-tuple-element.32.kept.refs_5_), custom_call_target="tpu_custom_call" | custom-call | flops 1000000 | bytes 262144 | tf_op jit(solution)/shard_map/pallas_call | solution.py:442
  37.7 0.5 %collective-permute-done.13.theirs = f32[8,1024]{1,0:T(8,128)S(1)} collective-permute-done((f32[8,1024]{1,0:T(8,128)S(1)}, f32[8,1024]{1,0:T(8,128)S(1)}, u32[]{:S(2)}, u32[]{:S(2)}) %collective-permute-start.13) | collective-permute-done | bytes 32800 | tf_op jit(solution)/shard_map/ppermute | solution.py:475
  38.2 0.8 %shard_map.112 = (f32[4,16,27]{2,1,0:T(8,128)}, f32[27,16,32]{2,1,0:T(8,128)}) custom-call(s32[1]{0:T(128)} %bitcast.refs_8_.half, f32[8,1024]{1,0:T(8,128)S(1)} %add_add_fusion.mine, f32[8,1024]{1,0:T(8,128)S(1)} %collective-permute-done.13.theirs), custom_call_target="tpu_custom_call" | custom-call | tf_op jit(solution)/shard_map/pallas_call | solution.py:442
  (8 shorter events, 0.0 us)
Async XLA Ops:
  0.6 11.2 %copy-start = (bf16[3,1,16,1024]{3,2,1,0:T(8,128)(2,1)S(1)}, bf16[3,1,16,1024]{3,2,1,0:T(8,128)(2,1)}, u32[]{:S(2)}) copy-start(bf16[3,1,16,1024]{3,2,1,0:T(8,128)(2,1)} %refs_2_.7) | copy-start | bytes 294916
  2.0 11.4 %collective-permute-start = (bf16[576,128]{1,0:T(8,128)(2,1)S(1)}, bf16[576,128]{1,0:T(8,128)(2,1)S(1)}, u32[]{:S(2)}, u32[]{:S(2)}) collective-permute-start(bf16[576,128]{1,0:T(8,128)(2,1)S(1)} %get-tuple-element.21.to_x.refs_0_), channel_id=1, source_target_pairs={{4,0},{5,1},{6,2},{7,3},{0,4},{1,5},{2,6},{3,7},{12,8},{13,9},{14,... | collective-permute-start | bytes 442376 | tf_op jit(solution)/shard_map/ppermute | solution.py:463
  6.3 3.7 %collective-permute-start.1 = (bf16[32,128]{1,0:T(8,128)(2,1)S(1)}, bf16[32,128]{1,0:T(8,128)(2,1)S(1)}, u32[]{:S(2)}, u32[]{:S(2)}) collective-permute-start(bf16[32,128]{1,0:T(8,128)(2,1)S(1)} %get-tuple-element.23), channel_id=1, source_target_pairs={{1,0},{0,1},{3,2},{2,3},{5,4},{4,5},{7,6},{6,7},{9,8},{8,9},{11,10... | collective-permute-start | bytes 24584 | tf_op jit(solution)/shard_map/ppermute | solution.py:463
  7.9 6.6 %collective-permute-start.3 = (bf16[32,128]{1,0:T(8,128)(2,1)S(1)}, bf16[32,128]{1,0:T(8,128)(2,1)S(1)}, u32[]{:S(2)}, u32[]{:S(2)}) collective-permute-start(bf16[32,128]{1,0:T(8,128)(2,1)S(1)} %get-tuple-element.23), channel_id=1, source_target_pairs={{5,0},{4,1},{7,2},{6,3},{1,4},{0,5},{3,6},{2,7},{13,8},{12,9},{15,... | collective-permute-start | bytes 24584 | tf_op jit(solution)/shard_map/ppermute | solution.py:463
  10.1 5.9 %collective-permute-start.5 = (bf16[416,128]{1,0:T(8,128)(2,1)S(1)}, bf16[416,128]{1,0:T(8,128)(2,1)S(1)}, u32[]{:S(2)}, u32[]{:S(2)}) collective-permute-start(bf16[416,128]{1,0:T(8,128)(2,1)S(1)} %pad_maximum_fusion), channel_id=1, source_target_pairs={{2,0},{3,1},{0,2},{1,3},{6,4},{7,5},{4,6},{5,7},{10,8},{11,9},{8,1... | collective-permute-start | bytes 319496 | tf_op jit(solution)/shard_map/ppermute | solution.py:463
  13.4 4.8 %collective-permute-start.2 = (bf16[288,128]{1,0:T(8,128)(2,1)S(1)}, bf16[288,128]{1,0:T(8,128)(2,1)S(1)}, u32[]{:S(2)}, u32[]{:S(2)}) collective-permute-start(bf16[288,128]{1,0:T(8,128)(2,1)S(1)} %pad_maximum_fusion.1), channel_id=1, source_target_pairs={{2,0},{3,1},{0,2},{1,3},{6,4},{7,5},{4,6},{5,7},{10,8},{11,9},{8,1... | collective-permute-start | bytes 221192 | tf_op jit(solution)/shard_map/ppermute | solution.py:463
  14.5 3.7 %collective-permute-start.4 = (bf16[64,128]{1,0:T(8,128)(2,1)S(1)}, bf16[64,128]{1,0:T(8,128)(2,1)S(1)}, u32[]{:S(2)}, u32[]{:S(2)}) collective-permute-start(bf16[64,128]{1,0:T(8,128)(2,1)S(1)} %pad_maximum_fusion.2), channel_id=1, source_target_pairs={{2,0},{3,1},{0,2},{1,3},{6,4},{7,5},{4,6},{5,7},{10,8},{11,9},{8,1... | collective-permute-start | bytes 49160 | tf_op jit(solution)/shard_map/ppermute | solution.py:463
  20.1 1.2 %collective-permute-start.6 = (f32[8,1024]{1,0:T(8,128)S(1)}, f32[8,1024]{1,0:T(8,128)S(1)}, u32[]{:S(2)}, u32[]{:S(2)}) collective-permute-start(f32[8,1024]{1,0:T(8,128)S(1)} %get-tuple-element.36), channel_id=1, source_target_pairs={{0,8},{1,9},{2,10},{3,11},{4,12},{5,13},{6,14},{7,15},{8,0},{9,1},... | collective-permute-start | bytes 98312 | tf_op jit(solution)/shard_map/ppermute | solution.py:475
  21.4 4.8 %collective-permute-start.7 = (f32[8,1024]{1,0:T(8,128)S(1)}, f32[8,1024]{1,0:T(8,128)S(1)}, u32[]{:S(2)}, u32[]{:S(2)}) collective-permute-start(f32[8,1024]{1,0:T(8,128)S(1)} %add.26), channel_id=1, source_target_pairs={{0,17},{1,16},{2,19},{3,18},{4,21},{5,20},{6,23},{7,22},{8,25},{9,... | collective-permute-start | bytes 98312 | tf_op jit(solution)/shard_map/ppermute | solution.py:475
  23.7 3.9 %collective-permute-start.8 = (f32[8,1024]{1,0:T(8,128)S(1)}, f32[8,1024]{1,0:T(8,128)S(1)}, u32[]{:S(2)}, u32[]{:S(2)}) collective-permute-start(f32[8,1024]{1,0:T(8,128)S(1)} %add.26), channel_id=1, source_target_pairs={{0,16},{1,17},{2,18},{3,19},{4,20},{5,21},{6,22},{7,23},{8,24},{9,... | collective-permute-start | bytes 98312 | tf_op jit(solution)/shard_map/ppermute | solution.py:475
  24.2 3.9 %collective-permute-start.9 = (f32[8,1024]{1,0:T(8,128)S(1)}, f32[8,1024]{1,0:T(8,128)S(1)}, u32[]{:S(2)}, u32[]{:S(2)}) collective-permute-start(f32[8,1024]{1,0:T(8,128)S(1)} %add.26), channel_id=1, source_target_pairs={{0,1},{1,0},{2,3},{3,2},{4,5},{5,4},{6,7},{7,6},{8,9},{9,8},{10,11... | collective-permute-start | bytes 98312 | tf_op jit(solution)/shard_map/ppermute | solution.py:475
  28.1 5.9 %collective-permute-start.10 = (f32[8,1024]{1,0:T(8,128)S(1)}, f32[8,1024]{1,0:T(8,128)S(1)}, u32[]{:S(2)}, u32[]{:S(2)}) collective-permute-start(f32[8,1024]{1,0:T(8,128)S(1)} %add_add_fusion.1), channel_id=1, source_target_pairs={{0,6},{1,7},{2,4},{3,5},{4,2},{5,3},{6,0},{7,1},{8,14},{9,15},{10,... | collective-permute-start | bytes 98312 | tf_op jit(solution)/shard_map/ppermute | solution.py:475
  31.8 3.9 %collective-permute-start.11 = (f32[8,1024]{1,0:T(8,128)S(1)}, f32[8,1024]{1,0:T(8,128)S(1)}, u32[]{:S(2)}, u32[]{:S(2)}) collective-permute-start(f32[8,1024]{1,0:T(8,128)S(1)} %add_add_fusion.1), channel_id=1, source_target_pairs={{0,2},{1,3},{2,0},{3,1},{4,6},{5,7},{6,4},{7,5},{8,10},{9,11},{10,... | collective-permute-start | bytes 98312 | tf_op jit(solution)/shard_map/ppermute | solution.py:475
  32.1 4.8 %collective-permute-start.12 = (f32[8,1024]{1,0:T(8,128)S(1)}, f32[8,1024]{1,0:T(8,128)S(1)}, u32[]{:S(2)}, u32[]{:S(2)}) collective-permute-start(f32[8,1024]{1,0:T(8,128)S(1)} %add_add_fusion.1), channel_id=1, source_target_pairs={{0,4},{1,5},{2,6},{3,7},{4,0},{5,1},{6,2},{7,3},{8,12},{9,13},{10,... | collective-permute-start | bytes 98312 | tf_op jit(solution)/shard_map/ppermute | solution.py:475
  36.9 1.3 %collective-permute-start.13 = (f32[8,1024]{1,0:T(8,128)S(1)}, f32[8,1024]{1,0:T(8,128)S(1)}, u32[]{:S(2)}, u32[]{:S(2)}) collective-permute-start(f32[8,1024]{1,0:T(8,128)S(1)} %add_add_fusion.mine), channel_id=1, source_target_pairs={{0,8},{1,9},{2,10},{3,11},{4,12},{5,13},{6,14},{7,15},{8,0},{9,1},... | collective-permute-start | bytes 98312 | tf_op jit(solution)/shard_map/ppermute | solution.py:475

commit v7 on v6

--- a/solution.py
+++ b/solution.py
@@ -352,14 +352,48 @@
         out[s, 0] = kept[s * C_ONE : (s + 1) * C_ONE]
 
 
+def middle_lines():
+    return range(3, BY - 3)
+
+
 def layer_one_inside(samples, face_at, edge_at, *refs):
-    blocks, (own, ahead) = refs[:-2], refs[-2:]
+    blocks, (own, part, chosen, ahead, product, middle) = refs[:-6], refs[-6:]
     shift_input(samples, lines_inside(), face_at, {}, edge_at, blocks, own, ahead)
+    rows = samples * C_ONE
+    table = doubling()
+    lines = middle_lines()
+    for x in range(HX):
+        for y in range(1, HY - 1):
+            at = (x * HY + y) * LANES
+            cells = part[:, at : at + LANES].astype(bf16)
+            wide = jnp.dot(cells, table, preferred_element_type=f32).astype(bf16)
+            for dx in range(2):
+                for dy in range(2):
+                    cx, cy = 2 * x + dx, 2 * y + dy
+                    value = wide * chosen[:, (cx * BY + cy) * BZ : (cx * BY + cy + 1) * BZ]
+                    for j, oy in enumerate(OFFS):
+                        if cy + oy in lines:
+                            to = (cy + oy - lines.start) * BZ
+                            middle[cx, j * rows : (j + 1) * rows, to : to + BZ] = value
+    plane = BY * BZ
+    total = jnp.zeros((3 * rows, 9 * PACK), f32)
+    for x in range(BX):
+        pieces = []
+        for ox in OFFS:
+            at = (x + 1 + ox) * plane
+            pieces.append(ahead[:, at + lines.start * BZ : at + lines.stop * BZ])
+        total = total + lax.dot_general(
+            middle[x], jnp.concatenate(pieces, axis=0), NT, preferred_element_type=f32
+        )
+    product[...] = total
 
 
 def layer_one(samples, scale, line_at, edge_at, *refs):
-    blocks, (own, ahead, grad, chosen, before_sums, half, mine, other, ahead_ends, inside, ends) = refs[:-11], refs[-11:]
+    blocks, (own, ahead, begun, grad, chosen, before_sums, half, mine, other, ahead_ends, inside, ends) = (
+        refs[:-12], refs[-12:],
+    )
     shift_input(samples, lines_ends(), {}, line_at, edge_at, blocks, own, ahead_ends)
+    lines = middle_lines()
     rows = samples * C_ONE
     table = doubling()
     empty = jnp.zeros((rows, BZ), bf16)
@@ -385,15 +419,20 @@
                             ends[cx, here, 0:BZ] = value
                         elif to >= BY:
                             ends[cx, here, BZ:] = value
-                        else:
+                        elif to not in lines:
                             inside[cx, here, to * BZ : (to + 1) * BZ] = value
     width = 3 * 3 * PACK
-    product = jnp.zeros((3 * rows, width), f32)
+    product = begun[...]
+    plane = BY * BZ
     for x in range(BX):
-        for left, right, size in ((inside, ahead, BY * BZ), (ends, ahead_ends, 2 * BZ)):
-            pieces = [right[:, (x + 1 + ox) * size : (x + 2 + ox) * size] for ox in OFFS]
+        for left, right, size, first, last in (
+            (inside, ahead, plane, 0, lines.start * BZ),
+            (inside, ahead, plane, lines.stop * BZ, plane),
+            (ends, ahead_ends, 2 * BZ, 0, 2 * BZ),
+        ):
+            pieces = [right[:, (x + 1 + ox) * size + first : (x + 1 + ox) * size + last] for ox in OFFS]
             product = product + lax.dot_general(
-                left[x], jnp.concatenate(pieces, axis=0), NT, preferred_element_type=f32
+                left[x, :, first:last], jnp.concatenate(pieces, axis=0), NT, preferred_element_type=f32
             )
     sample_of = (iota((C_ONE, width), 1) % PACK) // C_IN
     k = iota((width, LANES), 0)
@@ -612,10 +651,14 @@
         moved=1000,
     )
     arrays, tables = operands_of(face_at, near(edge_at, (0,)))
-    ahead = call(
+    ahead, begun = call(
         functools.partial(layer_one_inside, samples, *tables),
-        shape((3 * PACK, (BX + 2) * BY * BZ), bf16),
-        (*arrays, own),
+        (
+            shape((3 * PACK, (BX + 2) * BY * BZ), bf16),
+            shape((3 * samples * C_ONE, 9 * PACK), f32),
+        ),
+        (*arrays, own, part, chosen),
+        scratch=(pltpu.VMEM((BX, 3 * samples * C_ONE, len(middle_lines()) * BZ), bf16),),
         flops=10**8,
         moved=2**20,
     )
@@ -639,7 +682,7 @@
     )
     arrays, tables = operands_of(line_at, near(edge_at, (-1, 1)))
     half = (lax.axis_index("dp") % 2).astype(i32).reshape(1)
-    operands = (*arrays, own, ahead, kept, chosen, sums, half)
+    operands = (*arrays, own, ahead, begun, kept, chosen, sums, half)
     half_sums = shape((HALF, WIDTH), f32)
     mine, other = call(
         functools.partial(layer_one, samples, float(total) ** -0.5, *tables),
@@ -667,7 +710,7 @@
     bits += [1 << k for k in range(devices.bit_length() - 1) if 1 << k < blocks]
     while len(bits) > 1:
         (a, b), bits = bits[:2], bits[2:]
-        mine = (mine + swapped(mine, a ^ b)) + (swapped(mine, a) + swapped(mine, b))
+        mine = (mine + swapped(mine, a)) + (swapped(mine, b) + swapped(mine, a ^ b))
     for a in bits:
         mine = mine + swapped(mine, a)
     grad_w_one, grad_w_two = call(

time: 39.2 us -> 38.9 us (level)
  waiting for transfers between devices: 11.1 us -> 10.7 us
  transfers between devices with their start and end apart: 14 -> 14, of which waited for: 13 -> 12; matrix products, arithmetic and copies ran while one was open for 0% -> 0% of each run, Pallas kernels for 15% -> 15%
where the time goes in v7:
time: 38.9 us; the launch traced here: 38.7 us
  starting transfers between devices  17.3 us (44%)
  waiting for transfers between devices  10.7 us (28%)
  Pallas kernels  9.88 us (25%)
  between operations  0.74 us (2%)
    pallas_call x10, Pallas kernels, call(): pl.pallas_call(body, out_shape=shapes, in_specs=[pl.BlockSpec(memory_spac...  9.88 us
    ppermute x6, starting transfers between devices, from_block(): return lax.ppermute(array, 'space', pairs)  9.27 us
    ppermute x8, waiting for transfers between devices, swapped(): lax.ppermute(array, ('dp', 'space'), [(i, i ^ bits) for i in range(device...  9.17 us
    ppermute x8, starting transfers between devices, swapped(): lax.ppermute(array, ('dp', 'space'), [(i, i ^ bits) for i in range(device...  8.02 us
    ppermute x6, waiting for transfers between devices, from_block(): return lax.ppermute(array, 'space', pairs)  1.57 us
  transfers between devices with their start and end apart: 14, of which 12 were waited for; matrix products, arithmetic and copies ran while one was open for 0% of the time, Pallas kernels for 15%

profile of v7, /device:TPU:0, one launch (start us, length us, event | category | flops | bytes accessed | tf_op | source)
XLA Modules:
  0.0 38.7 jit_solution(18164737607331201328)
XLA Ops:
  0.6 0.0 copy-start
  0.6 1.4 %shard_map.103 = (bf16[576,128]{1,0:T(8,128)(2,1)S(1)}, bf16[16,8192]{1,0:T(8,128)(2,1)S(1)}) custom-call(bf16[3,1,32,128]{3,2,1,0:T(8,128)(2,1)} %refs_0_.2, s32[3,1,32,128]{3,2,1,0:T(8,128)} %refs_1_.2, s32[3,1,32,1024]{3,2,1,0:T(8,128)} %refs_2_.4, bf16[3,1,4,8192]{3,2,1,0:T(4,128)(2,1)} %refs_3_.2), custom_call_target="tpu_custom_call" | custom-call | flops 20000000 | bytes 1048576 | tf_op jit(solution)/shard_map/pallas_call | solution.py:481
  2.0 4.1 %collective-permute-start = (bf16[576,128]{1,0:T(8,128)(2,1)S(1)}, bf16[576,128]{1,0:T(8,128)(2,1)S(1)}, u32[]{:S(2)}, u32[]{:S(2)}) collective-permute-start(bf16[576,128]{1,0:T(8,128)(2,1)S(1)} %get-tuple-element.23.to_x.refs_0_), channel_id=1, source_target_pairs={{4,0},{5,1},{6,2},{7,3},{0,4},{1,5},{2,6},{3,7},{12,8},{13,9},{14,... | collective-permute-start | bytes 442376 | tf_op jit(solution)/shard_map/ppermute | solution.py:502
  6.1 0.2 shard_map.104
  6.3 1.6 %collective-permute-start.1 = (bf16[32,128]{1,0:T(8,128)(2,1)S(1)}, bf16[32,128]{1,0:T(8,128)(2,1)S(1)}, u32[]{:S(2)}, u32[]{:S(2)}) collective-permute-start(bf16[32,128]{1,0:T(8,128)(2,1)S(1)} %get-tuple-element.25), channel_id=1, source_target_pairs={{1,0},{0,1},{3,2},{2,3},{5,4},{4,5},{7,6},{6,7},{9,8},{8,9},{11,10... | collective-permute-start | bytes 24584 | tf_op jit(solution)/shard_map/ppermute | solution.py:502
  7.9 0.0 collective-permute-start.3
  7.9 2.0 %shard_map.105 = (bf16[48,8192]{1,0:T(8,128)(2,1)S(1)}, bf16[144,96]{1,0:T(8,128)(2,1)S(1)}, bf16[256,768]{1,0:T(8,128)(2,1)S(1)}) custom-call(s32[3,1,16,1024]{3,2,1,0:T(8,128)} %refs_0_.3, s32[3,1,16,8192]{3,2,1,0:T(8,128)} %refs_1_.3, bf16[27,16,32]{2,1,0:T(8,128)(2,1)} %refs_2_.5), custom_call_target="tpu_custom_call" | custom-call | flops 20000000 | bytes 3145728 | tf_op jit(solution)/shard_map/pallas_call | solution.py:481
  9.9 0.2 collective-permute-done.1.refs_1_
  10.1 1.8 %collective-permute-start.5 = (bf16[416,128]{1,0:T(8,128)(2,1)S(1)}, bf16[416,128]{1,0:T(8,128)(2,1)S(1)}, u32[]{:S(2)}, u32[]{:S(2)}) collective-permute-start(bf16[416,128]{1,0:T(8,128)(2,1)S(1)} %pad_maximum_fusion), channel_id=1, source_target_pairs={{2,0},{3,1},{0,2},{1,3},{6,4},{7,5},{4,6},{5,7},{10,8},{11,9},{8,1... | collective-permute-start | bytes 319496 | tf_op jit(solution)/shard_map/ppermute | solution.py:502
  11.9 0.0 copy-done
  11.9 1.1 %shard_map.106 = (f32[48,1024]{1,0:T(8,128)S(1)}, f32[144,96]{1,0:T(8,128)S(1)}) custom-call(bf16[576,128]{1,0:T(8,128)(2,1)S(1)} %get-tuple-element.23.to_x.refs_0_, bf16[32,128]{1,0:T(8,128)(2,1)S(1)} %collective-permute-done.1.refs_1_, bf16[3,1,16,1024]{3,2,1,0:T(8,128)(2,1)S(1)} %copy-done, bf16[144,96]{1,0:T(8,128)(2,1)S(1)} %get-tuple-element.26.refs_3_.refs_4_, ...), custom_call_target="tpu_custom_call" | custom-call | flops 1000 | bytes 1000 | tf_op jit(solution)/shard_map/pallas_call | solution.py:481
  12.9 0.5 %collective-permute-done.refs_0_ = bf16[576,128]{1,0:T(8,128)(2,1)S(1)} collective-permute-done((bf16[576,128]{1,0:T(8,128)(2,1)S(1)}, bf16[576,128]{1,0:T(8,128)(2,1)S(1)}, u32[]{:S(2)}, u32[]{:S(2)}) %collective-permute-start) | collective-permute-done | bytes 147488 | tf_op jit(solution)/shard_map/ppermute | solution.py:502
  13.4 0.8 %collective-permute-start.2 = (bf16[288,128]{1,0:T(8,128)(2,1)S(1)}, bf16[288,128]{1,0:T(8,128)(2,1)S(1)}, u32[]{:S(2)}, u32[]{:S(2)}) collective-permute-start(bf16[288,128]{1,0:T(8,128)(2,1)S(1)} %pad_maximum_fusion.1), channel_id=1, source_target_pairs={{2,0},{3,1},{0,2},{1,3},{6,4},{7,5},{4,6},{5,7},{10,8},{11,9},{8,1... | collective-permute-start | bytes 221192 | tf_op jit(solution)/shard_map/ppermute | solution.py:502
  14.2 0.3 collective-permute-done.3.refs_2_
  14.5 1.1 %collective-permute-start.4 = (bf16[64,128]{1,0:T(8,128)(2,1)S(1)}, bf16[64,128]{1,0:T(8,128)(2,1)S(1)}, u32[]{:S(2)}, u32[]{:S(2)}) collective-permute-start(bf16[64,128]{1,0:T(8,128)(2,1)S(1)} %pad_maximum_fusion.2), channel_id=1, source_target_pairs={{2,0},{3,1},{0,2},{1,3},{6,4},{7,5},{4,6},{5,7},{10,8},{11,9},{8,1... | collective-permute-start | bytes 49160 | tf_op jit(solution)/shard_map/ppermute | solution.py:502
  15.5 0.4 %collective-permute-done.5.refs_1_.refs_0_ = bf16[416,128]{1,0:T(8,128)(2,1)S(1)} collective-permute-done((bf16[416,128]{1,0:T(8,128)(2,1)S(1)}, bf16[416,128]{1,0:T(8,128)(2,1)S(1)}, u32[]{:S(2)}, u32[]{:S(2)}) %collective-permute-start.5) | collective-permute-done | bytes 106528 | tf_op jit(solution)/shard_map/ppermute | solution.py:502
  16.0 1.4 %shard_map.107 = (f32[48,1024]{1,0:T(8,128)S(1)}, f32[144,96]{1,0:T(8,128)S(1)}) custom-call(bf16[576,128]{1,0:T(8,128)(2,1)S(1)} %collective-permute-done.refs_0_, bf16[416,128]{1,0:T(8,128)(2,1)S(1)} %collective-permute-done.5.refs_1_.refs_0_, bf16[32,128]{1,0:T(8,128)(2,1)S(1)} %collective-permute-done.3.refs_2_, bf16[3,1,16,1024]{3,2,1,0:T(8,128)(2,1)S(1)} %copy-done, ...), custom_call_target="tpu_custom_call" | custom-call | flops 1000 | bytes 1000 | tf_op jit(solution)/shard_map/pallas_call | solution.py:481
  17.4 0.6 %shard_map.110 = (bf16[48,12288]{1,0:T(8,128)(2,1)S(1)}, f32[144,144]{1,0:T(8,128)S(1)}) custom-call(bf16[576,128]{1,0:T(8,128)(2,1)S(1)} %collective-permute-done.refs_0_, bf16[32,128]{1,0:T(8,128)(2,1)S(1)} %collective-permute-done.1.refs_1_, bf16[32,128]{1,0:T(8,128)(2,1)S(1)} %collective-permute-done.3.refs_2_, ...), custom_call_target="tpu_custom_call" | custom-call | flops 100000000 | bytes 1048576 | tf_op jit(solution)/shard_map/pallas_call | solution.py:481
  18.0 0.2 collective-permute-done.4.refs_1_.refs_2_
  18.2 0.0 collective-permute-done.2.refs_0_.refs_1_
  18.2 0.7 %shard_map.108 = (bf16[48,1024]{1,0:T(8,128)(2,1)S(1)}, f32[16,896]{1,0:T(8,128)S(1)}) custom-call(bf16[288,128]{1,0:T(8,128)(2,1)S(1)} %collective-permute-done.2.refs_0_.refs_1_, bf16[64,128]{1,0:T(8,128)(2,1)S(1)} %collective-permute-done.4.refs_1_.refs_2_, bf16[3,1,16,1024]{3,2,1,0:T(8,128)(2,1)S(1)} %copy-done, ...), custom_call_target="tpu_custom_call" | custom-call | flops 500000000 | bytes 1048576 | tf_op jit(solution)/shard_map/pallas_call | solution.py:481
  18.9 1.1 %shard_map.111 = (f32[8,1024]{1,0:T(8,128)S(1)}, f32[8,1024]{1,0:T(8,128)S(1)}) custom-call(bf16[416,128]{1,0:T(8,128)(2,1)S(1)} %collective-permute-done.5.refs_1_.refs_0_, bf16[288,128]{1,0:T(8,128)(2,1)S(1)} %collective-permute-done.2.refs_0_.refs_1_, bf16[64,128]{1,0:T(8,128)(2,1)S(1)} %collective-permute-done.4.refs_1_.refs_2_, ...), custom_call_target="tpu_custom_call" | custom-call | flops 500000000 | bytes 1048576 | tf_op jit(solution)/shard_map/pallas_call | solution.py:481
  20.0 0.0 collective-permute-start.6
  20.0 1.2 %collective-permute-done.6 = f32[8,1024]{1,0:T(8,128)S(1)} collective-permute-done((f32[8,1024]{1,0:T(8,128)S(1)}, f32[8,1024]{1,0:T(8,128)S(1)}, u32[]{:S(2)}, u32[]{:S(2)}) %collective-permute-start.6) | collective-permute-done | bytes 32800 | tf_op jit(solution)/shard_map/ppermute | solution.py:514
  21.2 2.5 %collective-permute-start.9 = (f32[8,1024]{1,0:T(8,128)S(1)}, f32[8,1024]{1,0:T(8,128)S(1)}, u32[]{:S(2)}, u32[]{:S(2)}) collective-permute-start(f32[8,1024]{1,0:T(8,128)S(1)} %add.26), channel_id=1, source_target_pairs={{0,17},{1,16},{2,19},{3,18},{4,21},{5,20},{6,23},{7,22},{8,25},{9,... | collective-permute-start | bytes 98312 | tf_op jit(solution)/shard_map/ppermute | solution.py:514
  23.7 0.5 %collective-permute-start.8 = (f32[8,1024]{1,0:T(8,128)S(1)}, f32[8,1024]{1,0:T(8,128)S(1)}, u32[]{:S(2)}, u32[]{:S(2)}) collective-permute-start(f32[8,1024]{1,0:T(8,128)S(1)} %add.26), channel_id=1, source_target_pairs={{0,1},{1,0},{2,3},{3,2},{4,5},{5,4},{6,7},{7,6},{8,9},{9,8},{10,11... | collective-permute-start | bytes 98312 | tf_op jit(solution)/shard_map/ppermute | solution.py:514
  24.2 0.5 %collective-permute-start.7 = (f32[8,1024]{1,0:T(8,128)S(1)}, f32[8,1024]{1,0:T(8,128)S(1)}, u32[]{:S(2)}, u32[]{:S(2)}) collective-permute-start(f32[8,1024]{1,0:T(8,128)S(1)} %add.26), channel_id=1, source_target_pairs={{0,16},{1,17},{2,18},{3,19},{4,20},{5,21},{6,22},{7,23},{8,24},{9,... | collective-permute-start | bytes 98312 | tf_op jit(solution)/shard_map/ppermute | solution.py:514
  24.7 1.3 %collective-permute-done.9 = f32[8,1024]{1,0:T(8,128)S(1)} collective-permute-done((f32[8,1024]{1,0:T(8,128)S(1)}, f32[8,1024]{1,0:T(8,128)S(1)}, u32[]{:S(2)}, u32[]{:S(2)}) %collective-permute-start.9) | collective-permute-done | bytes 32800 | tf_op jit(solution)/shard_map/ppermute | solution.py:514
  26.1 1.6 %collective-permute-done.8 = f32[8,1024]{1,0:T(8,128)S(1)} collective-permute-done((f32[8,1024]{1,0:T(8,128)S(1)}, f32[8,1024]{1,0:T(8,128)S(1)}, u32[]{:S(2)}, u32[]{:S(2)}) %collective-permute-start.8) | collective-permute-done | bytes 32800 | tf_op jit(solution)/shard_map/ppermute | solution.py:514
  27.6 0.5 %collective-permute-done.7 = f32[8,1024]{1,0:T(8,128)S(1)} collective-permute-done((f32[8,1024]{1,0:T(8,128)S(1)}, f32[8,1024]{1,0:T(8,128)S(1)}, u32[]{:S(2)}, u32[]{:S(2)}) %collective-permute-start.7) | collective-permute-done | bytes 32800 | tf_op jit(solution)/shard_map/ppermute | solution.py:514
  28.2 3.6 %collective-permute-start.12 = (f32[8,1024]{1,0:T(8,128)S(1)}, f32[8,1024]{1,0:T(8,128)S(1)}, u32[]{:S(2)}, u32[]{:S(2)}) collective-permute-start(f32[8,1024]{1,0:T(8,128)S(1)} %add_add_fusion.1), channel_id=1, source_target_pairs={{0,6},{1,7},{2,4},{3,5},{4,2},{5,3},{6,0},{7,1},{8,14},{9,15},{10,... | collective-permute-start | bytes 98312 | tf_op jit(solution)/shard_map/ppermute | solution.py:514
  31.8 0.0 collective-permute-start.11
  31.8 0.8 %collective-permute-start.10 = (f32[8,1024]{1,0:T(8,128)S(1)}, f32[8,1024]{1,0:T(8,128)S(1)}, u32[]{:S(2)}, u32[]{:S(2)}) collective-permute-start(f32[8,1024]{1,0:T(8,128)S(1)} %add_add_fusion.1), channel_id=1, source_target_pairs={{0,2},{1,3},{2,0},{3,1},{4,6},{5,7},{6,4},{7,5},{8,10},{9,11},{10,... | collective-permute-start | bytes 98312 | tf_op jit(solution)/shard_map/ppermute | solution.py:514
  32.6 1.3 %collective-permute-done.12 = f32[8,1024]{1,0:T(8,128)S(1)} collective-permute-done((f32[8,1024]{1,0:T(8,128)S(1)}, f32[8,1024]{1,0:T(8,128)S(1)}, u32[]{:S(2)}, u32[]{:S(2)}) %collective-permute-start.12) | collective-permute-done | bytes 32800 | tf_op jit(solution)/shard_map/ppermute | solution.py:514
  34.0 2.7 %collective-permute-done.11 = f32[8,1024]{1,0:T(8,128)S(1)} collective-permute-done((f32[8,1024]{1,0:T(8,128)S(1)}, f32[8,1024]{1,0:T(8,128)S(1)}, u32[]{:S(2)}, u32[]{:S(2)}) %collective-permute-start.11) | collective-permute-done | bytes 32800 | tf_op jit(solution)/shard_map/ppermute | solution.py:514
  36.6 0.0 collective-permute-done.10
  36.6 0.1 collective-permute-start.13
  36.7 0.6 %shard_map.109 = bf16[3,1,16,1024]{3,2,1,0:T(8,128)(2,1)} custom-call(bf16[48,1024]{1,0:T(8,128)(2,1)S(1)} %get-tuple-element.34.kept.refs_6_), custom_call_target="tpu_custom_call" | custom-call | flops 1000000 | bytes 262144 | tf_op jit(solution)/shard_map/pallas_call | solution.py:481
  37.4 0.5 %collective-permute-done.13.theirs = f32[8,1024]{1,0:T(8,128)S(1)} collective-permute-done((f32[8,1024]{1,0:T(8,128)S(1)}, f32[8,1024]{1,0:T(8,128)S(1)}, u32[]{:S(2)}, u32[]{:S(2)}) %collective-permute-start.13) | collective-permute-done | bytes 32800 | tf_op jit(solution)/shard_map/ppermute | solution.py:514
  37.9 0.8 %shard_map.112 = (f32[4,16,27]{2,1,0:T(8,128)}, f32[27,16,32]{2,1,0:T(8,128)}) custom-call(s32[1]{0:T(128)} %bitcast.refs_9_.half, f32[8,1024]{1,0:T(8,128)S(1)} %add_add_fusion.mine, f32[8,1024]{1,0:T(8,128)S(1)} %collective-permute-done.13.theirs), custom_call_target="tpu_custom_call" | custom-call | tf_op jit(solution)/shard_map/pallas_call | solution.py:481
  (8 shorter events, 0.0 us)
Async XLA Ops:
  0.6 11.2 %copy-start = (bf16[3,1,16,1024]{3,2,1,0:T(8,128)(2,1)S(1)}, bf16[3,1,16,1024]{3,2,1,0:T(8,128)(2,1)}, u32[]{:S(2)}) copy-start(bf16[3,1,16,1024]{3,2,1,0:T(8,128)(2,1)} %refs_2_.7) | copy-start | bytes 294916
  2.0 11.4 %collective-permute-start = (bf16[576,128]{1,0:T(8,128)(2,1)S(1)}, bf16[576,128]{1,0:T(8,128)(2,1)S(1)}, u32[]{:S(2)}, u32[]{:S(2)}) collective-permute-start(bf16[576,128]{1,0:T(8,128)(2,1)S(1)} %get-tuple-element.23.to_x.refs_0_), channel_id=1, source_target_pairs={{4,0},{5,1},{6,2},{7,3},{0,4},{1,5},{2,6},{3,7},{12,8},{13,9},{14,... | collective-permute-start | bytes 442376 | tf_op jit(solution)/shard_map/ppermute | solution.py:502
  6.3 3.7 %collective-permute-start.1 = (bf16[32,128]{1,0:T(8,128)(2,1)S(1)}, bf16[32,128]{1,0:T(8,128)(2,1)S(1)}, u32[]{:S(2)}, u32[]{:S(2)}) collective-permute-start(bf16[32,128]{1,0:T(8,128)(2,1)S(1)} %get-tuple-element.25), channel_id=1, source_target_pairs={{1,0},{0,1},{3,2},{2,3},{5,4},{4,5},{7,6},{6,7},{9,8},{8,9},{11,10... | collective-permute-start | bytes 24584 | tf_op jit(solution)/shard_map/ppermute | solution.py:502
  7.9 6.6 %collective-permute-start.3 = (bf16[32,128]{1,0:T(8,128)(2,1)S(1)}, bf16[32,128]{1,0:T(8,128)(2,1)S(1)}, u32[]{:S(2)}, u32[]{:S(2)}) collective-permute-start(bf16[32,128]{1,0:T(8,128)(2,1)S(1)} %get-tuple-element.25), channel_id=1, source_target_pairs={{5,0},{4,1},{7,2},{6,3},{1,4},{0,5},{3,6},{2,7},{13,8},{12,9},{15,... | collective-permute-start | bytes 24584 | tf_op jit(solution)/shard_map/ppermute | solution.py:502
  10.1 5.9 %collective-permute-start.5 = (bf16[416,128]{1,0:T(8,128)(2,1)S(1)}, bf16[416,128]{1,0:T(8,128)(2,1)S(1)}, u32[]{:S(2)}, u32[]{:S(2)}) collective-permute-start(bf16[416,128]{1,0:T(8,128)(2,1)S(1)} %pad_maximum_fusion), channel_id=1, source_target_pairs={{2,0},{3,1},{0,2},{1,3},{6,4},{7,5},{4,6},{5,7},{10,8},{11,9},{8,1... | collective-permute-start | bytes 319496 | tf_op jit(solution)/shard_map/ppermute | solution.py:502
  13.4 4.8 %collective-permute-start.2 = (bf16[288,128]{1,0:T(8,128)(2,1)S(1)}, bf16[288,128]{1,0:T(8,128)(2,1)S(1)}, u32[]{:S(2)}, u32[]{:S(2)}) collective-permute-start(bf16[288,128]{1,0:T(8,128)(2,1)S(1)} %pad_maximum_fusion.1), channel_id=1, source_target_pairs={{2,0},{3,1},{0,2},{1,3},{6,4},{7,5},{4,6},{5,7},{10,8},{11,9},{8,1... | collective-permute-start | bytes 221192 | tf_op jit(solution)/shard_map/ppermute | solution.py:502
  14.5 3.7 %collective-permute-start.4 = (bf16[64,128]{1,0:T(8,128)(2,1)S(1)}, bf16[64,128]{1,0:T(8,128)(2,1)S(1)}, u32[]{:S(2)}, u32[]{:S(2)}) collective-permute-start(bf16[64,128]{1,0:T(8,128)(2,1)S(1)} %pad_maximum_fusion.2), channel_id=1, source_target_pairs={{2,0},{3,1},{0,2},{1,3},{6,4},{7,5},{4,6},{5,7},{10,8},{11,9},{8,1... | collective-permute-start | bytes 49160 | tf_op jit(solution)/shard_map/ppermute | solution.py:502
  20.0 1.2 %collective-permute-start.6 = (f32[8,1024]{1,0:T(8,128)S(1)}, f32[8,1024]{1,0:T(8,128)S(1)}, u32[]{:S(2)}, u32[]{:S(2)}) collective-permute-start(f32[8,1024]{1,0:T(8,128)S(1)} %get-tuple-element.40), channel_id=1, source_target_pairs={{0,8},{1,9},{2,10},{3,11},{4,12},{5,13},{6,14},{7,15},{8,0},{9,1},... | collective-permute-start | bytes 98312 | tf_op jit(solution)/shard_map/ppermute | solution.py:514
  21.2 4.8 %collective-permute-start.9 = (f32[8,1024]{1,0:T(8,128)S(1)}, f32[8,1024]{1,0:T(8,128)S(1)}, u32[]{:S(2)}, u32[]{:S(2)}) collective-permute-start(f32[8,1024]{1,0:T(8,128)S(1)} %add.26), channel_id=1, source_target_pairs={{0,17},{1,16},{2,19},{3,18},{4,21},{5,20},{6,23},{7,22},{8,25},{9,... | collective-permute-start | bytes 98312 | tf_op jit(solution)/shard_map/ppermute | solution.py:514
  23.7 3.9 %collective-permute-start.8 = (f32[8,1024]{1,0:T(8,128)S(1)}, f32[8,1024]{1,0:T(8,128)S(1)}, u32[]{:S(2)}, u32[]{:S(2)}) collective-permute-start(f32[8,1024]{1,0:T(8,128)S(1)} %add.26), channel_id=1, source_target_pairs={{0,1},{1,0},{2,3},{3,2},{4,5},{5,4},{6,7},{7,6},{8,9},{9,8},{10,11... | collective-permute-start | bytes 98312 | tf_op jit(solution)/shard_map/ppermute | solution.py:514
  24.2 3.9 %collective-permute-start.7 = (f32[8,1024]{1,0:T(8,128)S(1)}, f32[8,1024]{1,0:T(8,128)S(1)}, u32[]{:S(2)}, u32[]{:S(2)}) collective-permute-start(f32[8,1024]{1,0:T(8,128)S(1)} %add.26), channel_id=1, source_target_pairs={{0,16},{1,17},{2,18},{3,19},{4,20},{5,21},{6,22},{7,23},{8,24},{9,... | collective-permute-start | bytes 98312 | tf_op jit(solution)/shard_map/ppermute | solution.py:514
  28.2 5.8 %collective-permute-start.12 = (f32[8,1024]{1,0:T(8,128)S(1)}, f32[8,1024]{1,0:T(8,128)S(1)}, u32[]{:S(2)}, u32[]{:S(2)}) collective-permute-start(f32[8,1024]{1,0:T(8,128)S(1)} %add_add_fusion.1), channel_id=1, source_target_pairs={{0,6},{1,7},{2,4},{3,5},{4,2},{5,3},{6,0},{7,1},{8,14},{9,15},{10,... | collective-permute-start | bytes 98312 | tf_op jit(solution)/shard_map/ppermute | solution.py:514
  31.8 4.8 %collective-permute-start.11 = (f32[8,1024]{1,0:T(8,128)S(1)}, f32[8,1024]{1,0:T(8,128)S(1)}, u32[]{:S(2)}, u32[]{:S(2)}) collective-permute-start(f32[8,1024]{1,0:T(8,128)S(1)} %add_add_fusion.1), channel_id=1, source_target_pairs={{0,4},{1,5},{2,6},{3,7},{4,0},{5,1},{6,2},{7,3},{8,12},{9,13},{10,... | collective-permute-start | bytes 98312 | tf_op jit(solution)/shard_map/ppermute | solution.py:514
  31.8 4.8 %collective-permute-start.10 = (f32[8,1024]{1,0:T(8,128)S(1)}, f32[8,1024]{1,0:T(8,128)S(1)}, u32[]{:S(2)}, u32[]{:S(2)}) collective-permute-start(f32[8,1024]{1,0:T(8,128)S(1)} %add_add_fusion.1), channel_id=1, source_target_pairs={{0,2},{1,3},{2,0},{3,1},{4,6},{5,7},{6,4},{7,5},{8,10},{9,11},{10,... | collective-permute-start | bytes 98312 | tf_op jit(solution)/shard_map/ppermute | solution.py:514
  36.6 1.3 %collective-permute-start.13 = (f32[8,1024]{1,0:T(8,128)S(1)}, f32[8,1024]{1,0:T(8,128)S(1)}, u32[]{:S(2)}, u32[]{:S(2)}) collective-permute-start(f32[8,1024]{1,0:T(8,128)S(1)} %add_add_fusion.mine), channel_id=1, source_target_pairs={{0,8},{1,9},{2,10},{3,11},{4,12},{5,13},{6,14},{7,15},{8,0},{9,1},... | collective-permute-start | bytes 98312 | tf_op jit(solution)/shard_map/ppermute | solution.py:514

commit v8 on v7

--- a/solution.py
+++ b/solution.py
@@ -289,16 +289,28 @@
 
 
 def layer_two_corners(samples, scale, vp_at, edge_at, *refs):
-    blocks, (pooled, weights, expand, part, total, kept, message, fields, moved) = refs[:-9], refs[-9:]
+    blocks, (pooled, weights, expand, part, total, kept, message, fields) = refs[:-8], refs[-8:]
     tile_of = tiles_corners()
     expand_windows(samples, vp_at, edge_at, tile_of, blocks, expand, fields)
-    shift_pooled(samples, tile_of, pooled, moved)
     sums = parts_of(samples, part)
-    totals = products_two(samples, tile_of, fields, moved, weights, sums, total[...]) * scale
+    totals = [total[k * C_ONE : (k + 1) * C_ONE] for k in range(9)]
+    for (px, py), tile in tile_of.items():
+        x, ox = (0, 1) if px == 0 else (HX - 1, -1)
+        y, oy = (0, 1) if py == 0 else (HY - 1, -1)
+        k = 3 * (ox + 1) + oy + 1
+        at = (x * HY + y) * LANES
+        for s in range(samples):
+            cells = fields[s, :, tile * LANES : (tile + 1) * LANES]
+            sums[s][x, y] = sums[s][x, y] + jnp.dot(
+                weights[k * C_ONE : (k + 1) * C_ONE], cells, preferred_element_type=f32
+            )
+            totals[k] = totals[k] + lax.dot_general(
+                pooled[s, 0, :, at : at + LANES], cells, NT, preferred_element_type=f32
+            )
     store_parts(sums, kept)
     width = 3 * C_TWO
     for k in range(9):
-        message[:, k * width : (k + 1) * width] = totals[k * C_ONE : (k + 1) * C_ONE]
+        message[:, k * width : (k + 1) * width] = totals[k] * scale
     message[:, GRAD_W_TWO:ONE_AT] = jnp.zeros((C_ONE, ONE_AT - GRAD_W_TWO), f32)
 
 
@@ -673,10 +685,7 @@
             shape((C_ONE, ONE_AT), f32),
         ),
         (*arrays, pooled_one, folded_weights, expand, part, total_two),
-        scratch=(
-            pltpu.VMEM((samples, 3 * C_TWO, corner_tiles * LANES), bf16),
-            pltpu.VMEM((samples, 9 * C_ONE, corner_tiles * LANES), bf16),
-        ),
+        scratch=(pltpu.VMEM((samples, 3 * C_TWO, corner_tiles * LANES), bf16),),
         flops=5 * 10**8,
         moved=2**20,
     )

time: 38.9 us -> 38.8 us (level)
  no operation moved by 1% of the time
where the time goes in v8:
time: 38.8 us; the launch traced here: 38.7 us
  starting transfers between devices  17.3 us (45%)
  waiting for transfers between devices  10.7 us (28%)
  Pallas kernels  9.86 us (25%)
  between operations  0.74 us (2%)
    pallas_call x10, Pallas kernels, call(): pl.pallas_call(body, out_shape=shapes, in_specs=[pl.BlockSpec(memory_spac...  9.86 us
    ppermute x6, starting transfers between devices, from_block(): return lax.ppermute(array, 'space', pairs)  9.27 us
    ppermute x8, waiting for transfers between devices, swapped(): lax.ppermute(array, ('dp', 'space'), [(i, i ^ bits) for i in range(device...  9.17 us
    ppermute x8, starting transfers between devices, swapped(): lax.ppermute(array, ('dp', 'space'), [(i, i ^ bits) for i in range(device...  8.02 us
    ppermute x6, waiting for transfers between devices, from_block(): return lax.ppermute(array, 'space', pairs)  1.57 us
  transfers between devices with their start and end apart: 14, of which 12 were waited for; matrix products, arithmetic and copies ran while one was open for 0% of the time, Pallas kernels for 15%

profile of v8, /device:TPU:0, one launch (start us, length us, event | category | flops | bytes accessed | tf_op | source)
XLA Modules:
  0.0 38.7 jit_solution(7458673691425103177)
XLA Ops:
  0.6 0.0 copy-start
  0.6 1.4 %shard_map.103 = (bf16[576,128]{1,0:T(8,128)(2,1)S(1)}, bf16[16,8192]{1,0:T(8,128)(2,1)S(1)}) custom-call(bf16[3,1,32,128]{3,2,1,0:T(8,128)(2,1)} %refs_0_.2, s32[3,1,32,128]{3,2,1,0:T(8,128)} %refs_1_.2, s32[3,1,32,1024]{3,2,1,0:T(8,128)} %refs_2_.4, bf16[3,1,4,8192]{3,2,1,0:T(4,128)(2,1)} %refs_3_.2), custom_call_target="tpu_custom_call" | custom-call | flops 20000000 | bytes 1048576 | tf_op jit(solution)/shard_map/pallas_call | solution.py:493
  2.0 4.1 %collective-permute-start = (bf16[576,128]{1,0:T(8,128)(2,1)S(1)}, bf16[576,128]{1,0:T(8,128)(2,1)S(1)}, u32[]{:S(2)}, u32[]{:S(2)}) collective-permute-start(bf16[576,128]{1,0:T(8,128)(2,1)S(1)} %get-tuple-element.23.to_x.refs_0_), channel_id=1, source_target_pairs={{4,0},{5,1},{6,2},{7,3},{0,4},{1,5},{2,6},{3,7},{12,8},{13,9},{14,... | collective-permute-start | bytes 442376 | tf_op jit(solution)/shard_map/ppermute | solution.py:514
  6.1 0.2 shard_map.104
  6.3 1.6 %collective-permute-start.1 = (bf16[32,128]{1,0:T(8,128)(2,1)S(1)}, bf16[32,128]{1,0:T(8,128)(2,1)S(1)}, u32[]{:S(2)}, u32[]{:S(2)}) collective-permute-start(bf16[32,128]{1,0:T(8,128)(2,1)S(1)} %get-tuple-element.25), channel_id=1, source_target_pairs={{1,0},{0,1},{3,2},{2,3},{5,4},{4,5},{7,6},{6,7},{9,8},{8,9},{11,10... | collective-permute-start | bytes 24584 | tf_op jit(solution)/shard_map/ppermute | solution.py:514
  7.9 0.0 collective-permute-start.3
  7.9 2.0 %shard_map.105 = (bf16[48,8192]{1,0:T(8,128)(2,1)S(1)}, bf16[144,96]{1,0:T(8,128)(2,1)S(1)}, bf16[256,768]{1,0:T(8,128)(2,1)S(1)}) custom-call(s32[3,1,16,1024]{3,2,1,0:T(8,128)} %refs_0_.3, s32[3,1,16,8192]{3,2,1,0:T(8,128)} %refs_1_.3, bf16[27,16,32]{2,1,0:T(8,128)(2,1)} %refs_2_.5), custom_call_target="tpu_custom_call" | custom-call | flops 20000000 | bytes 3145728 | tf_op jit(solution)/shard_map/pallas_call | solution.py:493
  9.9 0.2 collective-permute-done.1.refs_1_
  10.1 1.8 %collective-permute-start.5 = (bf16[416,128]{1,0:T(8,128)(2,1)S(1)}, bf16[416,128]{1,0:T(8,128)(2,1)S(1)}, u32[]{:S(2)}, u32[]{:S(2)}) collective-permute-start(bf16[416,128]{1,0:T(8,128)(2,1)S(1)} %pad_maximum_fusion), channel_id=1, source_target_pairs={{2,0},{3,1},{0,2},{1,3},{6,4},{7,5},{4,6},{5,7},{10,8},{11,9},{8,1... | collective-permute-start | bytes 319496 | tf_op jit(solution)/shard_map/ppermute | solution.py:514
  11.9 0.0 copy-done
  11.9 1.1 %shard_map.106 = (f32[48,1024]{1,0:T(8,128)S(1)}, f32[144,96]{1,0:T(8,128)S(1)}) custom-call(bf16[576,128]{1,0:T(8,128)(2,1)S(1)} %get-tuple-element.23.to_x.refs_0_, bf16[32,128]{1,0:T(8,128)(2,1)S(1)} %collective-permute-done.1.refs_1_, bf16[3,1,16,1024]{3,2,1,0:T(8,128)(2,1)S(1)} %copy-done, bf16[144,96]{1,0:T(8,128)(2,1)S(1)} %get-tuple-element.26.refs_3_.refs_4_, ...), custom_call_target="tpu_custom_call" | custom-call | flops 1000 | bytes 1000 | tf_op jit(solution)/shard_map/pallas_call | solution.py:493
  12.9 0.5 %collective-permute-done.refs_0_ = bf16[576,128]{1,0:T(8,128)(2,1)S(1)} collective-permute-done((bf16[576,128]{1,0:T(8,128)(2,1)S(1)}, bf16[576,128]{1,0:T(8,128)(2,1)S(1)}, u32[]{:S(2)}, u32[]{:S(2)}) %collective-permute-start) | collective-permute-done | bytes 147488 | tf_op jit(solution)/shard_map/ppermute | solution.py:514
  13.4 0.8 %collective-permute-start.2 = (bf16[288,128]{1,0:T(8,128)(2,1)S(1)}, bf16[288,128]{1,0:T(8,128)(2,1)S(1)}, u32[]{:S(2)}, u32[]{:S(2)}) collective-permute-start(bf16[288,128]{1,0:T(8,128)(2,1)S(1)} %pad_maximum_fusion.1), channel_id=1, source_target_pairs={{2,0},{3,1},{0,2},{1,3},{6,4},{7,5},{4,6},{5,7},{10,8},{11,9},{8,1... | collective-permute-start | bytes 221192 | tf_op jit(solution)/shard_map/ppermute | solution.py:514
  14.2 0.3 collective-permute-done.3.refs_2_
  14.5 1.1 %collective-permute-start.4 = (bf16[64,128]{1,0:T(8,128)(2,1)S(1)}, bf16[64,128]{1,0:T(8,128)(2,1)S(1)}, u32[]{:S(2)}, u32[]{:S(2)}) collective-permute-start(bf16[64,128]{1,0:T(8,128)(2,1)S(1)} %pad_maximum_fusion.2), channel_id=1, source_target_pairs={{2,0},{3,1},{0,2},{1,3},{6,4},{7,5},{4,6},{5,7},{10,8},{11,9},{8,1... | collective-permute-start | bytes 49160 | tf_op jit(solution)/shard_map/ppermute | solution.py:514
  15.5 0.4 %collective-permute-done.5.refs_1_.refs_0_ = bf16[416,128]{1,0:T(8,128)(2,1)S(1)} collective-permute-done((bf16[416,128]{1,0:T(8,128)(2,1)S(1)}, bf16[416,128]{1,0:T(8,128)(2,1)S(1)}, u32[]{:S(2)}, u32[]{:S(2)}) %collective-permute-start.5) | collective-permute-done | bytes 106528 | tf_op jit(solution)/shard_map/ppermute | solution.py:514
  16.0 1.4 %shard_map.107 = (f32[48,1024]{1,0:T(8,128)S(1)}, f32[144,96]{1,0:T(8,128)S(1)}) custom-call(bf16[576,128]{1,0:T(8,128)(2,1)S(1)} %collective-permute-done.refs_0_, bf16[416,128]{1,0:T(8,128)(2,1)S(1)} %collective-permute-done.5.refs_1_.refs_0_, bf16[32,128]{1,0:T(8,128)(2,1)S(1)} %collective-permute-done.3.refs_2_, bf16[3,1,16,1024]{3,2,1,0:T(8,128)(2,1)S(1)} %copy-done, ...), custom_call_target="tpu_custom_call" | custom-call | flops 1000 | bytes 1000 | tf_op jit(solution)/shard_map/pallas_call | solution.py:493
  17.4 0.6 %shard_map.110 = (bf16[48,12288]{1,0:T(8,128)(2,1)S(1)}, f32[144,144]{1,0:T(8,128)S(1)}) custom-call(bf16[576,128]{1,0:T(8,128)(2,1)S(1)} %collective-permute-done.refs_0_, bf16[32,128]{1,0:T(8,128)(2,1)S(1)} %collective-permute-done.1.refs_1_, bf16[32,128]{1,0:T(8,128)(2,1)S(1)} %collective-permute-done.3.refs_2_, ...), custom_call_target="tpu_custom_call" | custom-call | flops 100000000 | bytes 1048576 | tf_op jit(solution)/shard_map/pallas_call | solution.py:493
  18.0 0.2 collective-permute-done.4.refs_1_.refs_2_
  18.2 0.0 collective-permute-done.2.refs_0_.refs_1_
  18.2 0.7 %shard_map.108 = (bf16[48,1024]{1,0:T(8,128)(2,1)S(1)}, f32[16,896]{1,0:T(8,128)S(1)}) custom-call(bf16[288,128]{1,0:T(8,128)(2,1)S(1)} %collective-permute-done.2.refs_0_.refs_1_, bf16[64,128]{1,0:T(8,128)(2,1)S(1)} %collective-permute-done.4.refs_1_.refs_2_, bf16[3,1,16,1024]{3,2,1,0:T(8,128)(2,1)S(1)} %copy-done, ...), custom_call_target="tpu_custom_call" | custom-call | flops 500000000 | bytes 1048576 | tf_op jit(solution)/shard_map/pallas_call | solution.py:493
  18.9 1.1 %shard_map.111 = (f32[8,1024]{1,0:T(8,128)S(1)}, f32[8,1024]{1,0:T(8,128)S(1)}) custom-call(bf16[416,128]{1,0:T(8,128)(2,1)S(1)} %collective-permute-done.5.refs_1_.refs_0_, bf16[288,128]{1,0:T(8,128)(2,1)S(1)} %collective-permute-done.2.refs_0_.refs_1_, bf16[64,128]{1,0:T(8,128)(2,1)S(1)} %collective-permute-done.4.refs_1_.refs_2_, ...), custom_call_target="tpu_custom_call" | custom-call | flops 500000000 | bytes 1048576 | tf_op jit(solution)/shard_map/pallas_call | solution.py:493
  20.0 0.0 collective-permute-start.6
  20.0 1.2 %collective-permute-done.6 = f32[8,1024]{1,0:T(8,128)S(1)} collective-permute-done((f32[8,1024]{1,0:T(8,128)S(1)}, f32[8,1024]{1,0:T(8,128)S(1)}, u32[]{:S(2)}, u32[]{:S(2)}) %collective-permute-start.6) | collective-permute-done | bytes 32800 | tf_op jit(solution)/shard_map/ppermute | solution.py:526
  21.2 2.5 %collective-permute-start.9 = (f32[8,1024]{1,0:T(8,128)S(1)}, f32[8,1024]{1,0:T(8,128)S(1)}, u32[]{:S(2)}, u32[]{:S(2)}) collective-permute-start(f32[8,1024]{1,0:T(8,128)S(1)} %add.26), channel_id=1, source_target_pairs={{0,17},{1,16},{2,19},{3,18},{4,21},{5,20},{6,23},{7,22},{8,25},{9,... | collective-permute-start | bytes 98312 | tf_op jit(solution)/shard_map/ppermute | solution.py:526
  23.7 0.5 %collective-permute-start.8 = (f32[8,1024]{1,0:T(8,128)S(1)}, f32[8,1024]{1,0:T(8,128)S(1)}, u32[]{:S(2)}, u32[]{:S(2)}) collective-permute-start(f32[8,1024]{1,0:T(8,128)S(1)} %add.26), channel_id=1, source_target_pairs={{0,1},{1,0},{2,3},{3,2},{4,5},{5,4},{6,7},{7,6},{8,9},{9,8},{10,11... | collective-permute-start | bytes 98312 | tf_op jit(solution)/shard_map/ppermute | solution.py:526
  24.2 0.5 %collective-permute-start.7 = (f32[8,1024]{1,0:T(8,128)S(1)}, f32[8,1024]{1,0:T(8,128)S(1)}, u32[]{:S(2)}, u32[]{:S(2)}) collective-permute-start(f32[8,1024]{1,0:T(8,128)S(1)} %add.26), channel_id=1, source_target_pairs={{0,16},{1,17},{2,18},{3,19},{4,20},{5,21},{6,22},{7,23},{8,24},{9,... | collective-permute-start | bytes 98312 | tf_op jit(solution)/shard_map/ppermute | solution.py:526
  24.7 1.3 %collective-permute-done.9 = f32[8,1024]{1,0:T(8,128)S(1)} collective-permute-done((f32[8,1024]{1,0:T(8,128)S(1)}, f32[8,1024]{1,0:T(8,128)S(1)}, u32[]{:S(2)}, u32[]{:S(2)}) %collective-permute-start.9) | collective-permute-done | bytes 32800 | tf_op jit(solution)/shard_map/ppermute | solution.py:526
  26.0 1.6 %collective-permute-done.8 = f32[8,1024]{1,0:T(8,128)S(1)} collective-permute-done((f32[8,1024]{1,0:T(8,128)S(1)}, f32[8,1024]{1,0:T(8,128)S(1)}, u32[]{:S(2)}, u32[]{:S(2)}) %collective-permute-start.8) | collective-permute-done | bytes 32800 | tf_op jit(solution)/shard_map/ppermute | solution.py:526
  27.6 0.5 %collective-permute-done.7 = f32[8,1024]{1,0:T(8,128)S(1)} collective-permute-done((f32[8,1024]{1,0:T(8,128)S(1)}, f32[8,1024]{1,0:T(8,128)S(1)}, u32[]{:S(2)}, u32[]{:S(2)}) %collective-permute-start.7) | collective-permute-done | bytes 32800 | tf_op jit(solution)/shard_map/ppermute | solution.py:526
  28.1 3.6 %collective-permute-start.12 = (f32[8,1024]{1,0:T(8,128)S(1)}, f32[8,1024]{1,0:T(8,128)S(1)}, u32[]{:S(2)}, u32[]{:S(2)}) collective-permute-start(f32[8,1024]{1,0:T(8,128)S(1)} %add_add_fusion.1), channel_id=1, source_target_pairs={{0,6},{1,7},{2,4},{3,5},{4,2},{5,3},{6,0},{7,1},{8,14},{9,15},{10,... | collective-permute-start | bytes 98312 | tf_op jit(solution)/shard_map/ppermute | solution.py:526
  31.8 0.0 collective-permute-start.11
  31.8 0.8 %collective-permute-start.10 = (f32[8,1024]{1,0:T(8,128)S(1)}, f32[8,1024]{1,0:T(8,128)S(1)}, u32[]{:S(2)}, u32[]{:S(2)}) collective-permute-start(f32[8,1024]{1,0:T(8,128)S(1)} %add_add_fusion.1), channel_id=1, source_target_pairs={{0,2},{1,3},{2,0},{3,1},{4,6},{5,7},{6,4},{7,5},{8,10},{9,11},{10,... | collective-permute-start | bytes 98312 | tf_op jit(solution)/shard_map/ppermute | solution.py:526
  32.6 1.3 %collective-permute-done.12 = f32[8,1024]{1,0:T(8,128)S(1)} collective-permute-done((f32[8,1024]{1,0:T(8,128)S(1)}, f32[8,1024]{1,0:T(8,128)S(1)}, u32[]{:S(2)}, u32[]{:S(2)}) %collective-permute-start.12) | collective-permute-done | bytes 32800 | tf_op jit(solution)/shard_map/ppermute | solution.py:526
  33.9 2.7 %collective-permute-done.11 = f32[8,1024]{1,0:T(8,128)S(1)} collective-permute-done((f32[8,1024]{1,0:T(8,128)S(1)}, f32[8,1024]{1,0:T(8,128)S(1)}, u32[]{:S(2)}, u32[]{:S(2)}) %collective-permute-start.11) | collective-permute-done | bytes 32800 | tf_op jit(solution)/shard_map/ppermute | solution.py:526
  36.6 0.0 collective-permute-done.10
  36.6 0.1 collective-permute-start.13
  36.7 0.6 %shard_map.109 = bf16[3,1,16,1024]{3,2,1,0:T(8,128)(2,1)} custom-call(bf16[48,1024]{1,0:T(8,128)(2,1)S(1)} %get-tuple-element.34.kept.refs_6_), custom_call_target="tpu_custom_call" | custom-call | flops 1000000 | bytes 262144 | tf_op jit(solution)/shard_map/pallas_call | solution.py:493
  37.3 0.5 %collective-permute-done.13.theirs = f32[8,1024]{1,0:T(8,128)S(1)} collective-permute-done((f32[8,1024]{1,0:T(8,128)S(1)}, f32[8,1024]{1,0:T(8,128)S(1)}, u32[]{:S(2)}, u32[]{:S(2)}) %collective-permute-start.13) | collective-permute-done | bytes 32800 | tf_op jit(solution)/shard_map/ppermute | solution.py:526
  37.9 0.8 %shard_map.112 = (f32[4,16,27]{2,1,0:T(8,128)}, f32[27,16,32]{2,1,0:T(8,128)}) custom-call(s32[1]{0:T(128)} %bitcast.refs_9_.half, f32[8,1024]{1,0:T(8,128)S(1)} %add_add_fusion.mine, f32[8,1024]{1,0:T(8,128)S(1)} %collective-permute-done.13.theirs), custom_call_target="tpu_custom_call" | custom-call | tf_op jit(solution)/shard_map/pallas_call | solution.py:493
  (8 shorter events, 0.0 us)
Async XLA Ops:
  0.6 11.2 %copy-start = (bf16[3,1,16,1024]{3,2,1,0:T(8,128)(2,1)S(1)}, bf16[3,1,16,1024]{3,2,1,0:T(8,128)(2,1)}, u32[]{:S(2)}) copy-start(bf16[3,1,16,1024]{3,2,1,0:T(8,128)(2,1)} %refs_2_.7) | copy-start | bytes 294916
  2.0 11.4 %collective-permute-start = (bf16[576,128]{1,0:T(8,128)(2,1)S(1)}, bf16[576,128]{1,0:T(8,128)(2,1)S(1)}, u32[]{:S(2)}, u32[]{:S(2)}) collective-permute-start(bf16[576,128]{1,0:T(8,128)(2,1)S(1)} %get-tuple-element.23.to_x.refs_0_), channel_id=1, source_target_pairs={{4,0},{5,1},{6,2},{7,3},{0,4},{1,5},{2,6},{3,7},{12,8},{13,9},{14,... | collective-permute-start | bytes 442376 | tf_op jit(solution)/shard_map/ppermute | solution.py:514
  6.3 3.7 %collective-permute-start.1 = (bf16[32,128]{1,0:T(8,128)(2,1)S(1)}, bf16[32,128]{1,0:T(8,128)(2,1)S(1)}, u32[]{:S(2)}, u32[]{:S(2)}) collective-permute-start(bf16[32,128]{1,0:T(8,128)(2,1)S(1)} %get-tuple-element.25), channel_id=1, source_target_pairs={{1,0},{0,1},{3,2},{2,3},{5,4},{4,5},{7,6},{6,7},{9,8},{8,9},{11,10... | collective-permute-start | bytes 24584 | tf_op jit(solution)/shard_map/ppermute | solution.py:514
  7.9 6.6 %collective-permute-start.3 = (bf16[32,128]{1,0:T(8,128)(2,1)S(1)}, bf16[32,128]{1,0:T(8,128)(2,1)S(1)}, u32[]{:S(2)}, u32[]{:S(2)}) collective-permute-start(bf16[32,128]{1,0:T(8,128)(2,1)S(1)} %get-tuple-element.25), channel_id=1, source_target_pairs={{5,0},{4,1},{7,2},{6,3},{1,4},{0,5},{3,6},{2,7},{13,8},{12,9},{15,... | collective-permute-start | bytes 24584 | tf_op jit(solution)/shard_map/ppermute | solution.py:514
  10.1 5.9 %collective-permute-start.5 = (bf16[416,128]{1,0:T(8,128)(2,1)S(1)}, bf16[416,128]{1,0:T(8,128)(2,1)S(1)}, u32[]{:S(2)}, u32[]{:S(2)}) collective-permute-start(bf16[416,128]{1,0:T(8,128)(2,1)S(1)} %pad_maximum_fusion), channel_id=1, source_target_pairs={{2,0},{3,1},{0,2},{1,3},{6,4},{7,5},{4,6},{5,7},{10,8},{11,9},{8,1... | collective-permute-start | bytes 319496 | tf_op jit(solution)/shard_map/ppermute | solution.py:514
  13.4 4.8 %collective-permute-start.2 = (bf16[288,128]{1,0:T(8,128)(2,1)S(1)}, bf16[288,128]{1,0:T(8,128)(2,1)S(1)}, u32[]{:S(2)}, u32[]{:S(2)}) collective-permute-start(bf16[288,128]{1,0:T(8,128)(2,1)S(1)} %pad_maximum_fusion.1), channel_id=1, source_target_pairs={{2,0},{3,1},{0,2},{1,3},{6,4},{7,5},{4,6},{5,7},{10,8},{11,9},{8,1... | collective-permute-start | bytes 221192 | tf_op jit(solution)/shard_map/ppermute | solution.py:514
  14.5 3.7 %collective-permute-start.4 = (bf16[64,128]{1,0:T(8,128)(2,1)S(1)}, bf16[64,128]{1,0:T(8,128)(2,1)S(1)}, u32[]{:S(2)}, u32[]{:S(2)}) collective-permute-start(bf16[64,128]{1,0:T(8,128)(2,1)S(1)} %pad_maximum_fusion.2), channel_id=1, source_target_pairs={{2,0},{3,1},{0,2},{1,3},{6,4},{7,5},{4,6},{5,7},{10,8},{11,9},{8,1... | collective-permute-start | bytes 49160 | tf_op jit(solution)/shard_map/ppermute | solution.py:514
  20.0 1.2 %collective-permute-start.6 = (f32[8,1024]{1,0:T(8,128)S(1)}, f32[8,1024]{1,0:T(8,128)S(1)}, u32[]{:S(2)}, u32[]{:S(2)}) collective-permute-start(f32[8,1024]{1,0:T(8,128)S(1)} %get-tuple-element.40), channel_id=1, source_target_pairs={{0,8},{1,9},{2,10},{3,11},{4,12},{5,13},{6,14},{7,15},{8,0},{9,1},... | collective-permute-start | bytes 98312 | tf_op jit(solution)/shard_map/ppermute | solution.py:526
  21.2 4.8 %collective-permute-start.9 = (f32[8,1024]{1,0:T(8,128)S(1)}, f32[8,1024]{1,0:T(8,128)S(1)}, u32[]{:S(2)}, u32[]{:S(2)}) collective-permute-start(f32[8,1024]{1,0:T(8,128)S(1)} %add.26), channel_id=1, source_target_pairs={{0,17},{1,16},{2,19},{3,18},{4,21},{5,20},{6,23},{7,22},{8,25},{9,... | collective-permute-start | bytes 98312 | tf_op jit(solution)/shard_map/ppermute | solution.py:526
  23.7 3.9 %collective-permute-start.8 = (f32[8,1024]{1,0:T(8,128)S(1)}, f32[8,1024]{1,0:T(8,128)S(1)}, u32[]{:S(2)}, u32[]{:S(2)}) collective-permute-start(f32[8,1024]{1,0:T(8,128)S(1)} %add.26), channel_id=1, source_target_pairs={{0,1},{1,0},{2,3},{3,2},{4,5},{5,4},{6,7},{7,6},{8,9},{9,8},{10,11... | collective-permute-start | bytes 98312 | tf_op jit(solution)/shard_map/ppermute | solution.py:526
  24.2 3.9 %collective-permute-start.7 = (f32[8,1024]{1,0:T(8,128)S(1)}, f32[8,1024]{1,0:T(8,128)S(1)}, u32[]{:S(2)}, u32[]{:S(2)}) collective-permute-start(f32[8,1024]{1,0:T(8,128)S(1)} %add.26), channel_id=1, source_target_pairs={{0,16},{1,17},{2,18},{3,19},{4,20},{5,21},{6,22},{7,23},{8,24},{9,... | collective-permute-start | bytes 98312 | tf_op jit(solution)/shard_map/ppermute | solution.py:526
  28.1 5.8 %collective-permute-start.12 = (f32[8,1024]{1,0:T(8,128)S(1)}, f32[8,1024]{1,0:T(8,128)S(1)}, u32[]{:S(2)}, u32[]{:S(2)}) collective-permute-start(f32[8,1024]{1,0:T(8,128)S(1)} %add_add_fusion.1), channel_id=1, source_target_pairs={{0,6},{1,7},{2,4},{3,5},{4,2},{5,3},{6,0},{7,1},{8,14},{9,15},{10,... | collective-permute-start | bytes 98312 | tf_op jit(solution)/shard_map/ppermute | solution.py:526
  31.8 4.8 %collective-permute-start.11 = (f32[8,1024]{1,0:T(8,128)S(1)}, f32[8,1024]{1,0:T(8,128)S(1)}, u32[]{:S(2)}, u32[]{:S(2)}) collective-permute-start(f32[8,1024]{1,0:T(8,128)S(1)} %add_add_fusion.1), channel_id=1, source_target_pairs={{0,4},{1,5},{2,6},{3,7},{4,0},{5,1},{6,2},{7,3},{8,12},{9,13},{10,... | collective-permute-start | bytes 98312 | tf_op jit(solution)/shard_map/ppermute | solution.py:526
  31.8 4.8 %collective-permute-start.10 = (f32[8,1024]{1,0:T(8,128)S(1)}, f32[8,1024]{1,0:T(8,128)S(1)}, u32[]{:S(2)}, u32[]{:S(2)}) collective-permute-start(f32[8,1024]{1,0:T(8,128)S(1)} %add_add_fusion.1), channel_id=1, source_target_pairs={{0,2},{1,3},{2,0},{3,1},{4,6},{5,7},{6,4},{7,5},{8,10},{9,11},{10,... | collective-permute-start | bytes 98312 | tf_op jit(solution)/shard_map/ppermute | solution.py:526
  36.6 1.3 %collective-permute-start.13 = (f32[8,1024]{1,0:T(8,128)S(1)}, f32[8,1024]{1,0:T(8,128)S(1)}, u32[]{:S(2)}, u32[]{:S(2)}) collective-permute-start(f32[8,1024]{1,0:T(8,128)S(1)} %add_add_fusion.mine), channel_id=1, source_target_pairs={{0,8},{1,9},{2,10},{3,11},{4,12},{5,13},{6,14},{7,15},{8,0},{9,1},... | collective-permute-start | bytes 98312 | tf_op jit(solution)/shard_map/ppermute | solution.py:526
